TPU v7x, 512 devices: a whole 4x4x16 slice. The times are simulated.
512 devices in a mesh: ens: 16 (over z_lo, core), space: 32 (over y, x, z_hi).
Axes of the slice: x: 4, y: 4, z: 16 (z_hi: 2, z_lo: 8; z = z_hi * 8 + z_lo), core: 2. Of those that a mesh axis runs over, the one named last changes fastest.
Arguments:
- latents: bfloat16 [16, 16384, 1024], P('ens', 'space'), may hold values from -6 to 6
- w_mix: bfloat16 [1024, 1024], P('space'), may hold values from -0.1875 to 0.1875
- w_out: bfloat16 [1024, 16], replicated, may hold values from -0.1875 to 0.1875
- bias: float32 [16], replicated, may hold values from -3 to 3
- truth: float32 [16, 16384], P(None, 'space'), may hold values from -6 to 6
- area: float32 [16384], P('space'), may hold values from 0.25 to 4
Outputs:
- grad_latents: bfloat16 [16, 16384, 1024], P('ens', 'space')
- grad_mix: float32 [1024, 1024], P('space')
- grad_out: float32 [1024, 16], replicated
- grad_bias: float32 [16], replicated
- loss: float32 [], replicated
All inputs are finite; a program needn't handle non-finite values.
Results may differ from a plain program's by a relative error of at most 0.0057.
The roundings to bfloat16 on the way count: a program that leaves them out, or rounds other values in their place, can miss the bound.
Values may be sent and summed in bfloat16 or wider, within the bound.
No kernel may reach another device: no remote copies, remote signals or barrier semaphores. Data moves between devices by JAX's collectives and lax.ppermute only.
A program may use at most 64 MiB of HBM per device.

v0:
```python
import jax
import jax.numpy as jnp
from jax import lax
from jax.sharding import PartitionSpec as P

M = 16


smoothing = 0.1


def pairwise_terms(chosen, members, observed, weights_pt):
    count_all = float(M)
    differ = chosen[:, :, None, :] - members[:, None, :, :]
    smooth = jnp.sqrt(differ * differ + smoothing * smoothing)
    slopes = differ / smooth
    to_truth = chosen - observed[:, None, :]
    absolute = jnp.sqrt(to_truth * to_truth + smoothing * smoothing)
    pairs_norm = count_all * (count_all - 1.0)
    member_gradient = weights_pt * (
        to_truth / absolute / count_all - jnp.sum(slopes, axis=2) / pairs_norm
    )
    partial_loss = jnp.sum(
        weights_pt
        * (absolute / count_all - (jnp.sum(smooth, axis=2) - smoothing) / (2.0 * pairs_norm))
    )
    return (member_gradient, partial_loss)


def body(latents, w_mix, w_out, bias, truth, area):
    local_members = latents.shape[0]
    local_points = latents.shape[1]
    width = latents.shape[2]
    field_values = w_out.shape[1]
    row_count = local_members * local_points
    flat_rows = latents.reshape(row_count, width)
    columns = flat_rows
    pre_act = jnp.dot(
        columns,
        lax.all_gather(w_mix, "space", axis=0, tiled=True),
        preferred_element_type=jnp.float32,
    )
    hidden = jax.nn.gelu(pre_act).astype(jnp.bfloat16)
    predicted_fields = (
        lax.dot_general(w_out, hidden, (((0,), (1,)), ((), ())), preferred_element_type=jnp.float32)
        + bias[:, None]
    )
    predicted_fields = predicted_fields.reshape(field_values, local_members, local_points)
    collected_members = lax.all_gather(predicted_fields, "ens", axis=1, tiled=True)
    member_gradient, partial_loss = pairwise_terms(predicted_fields, collected_members, truth, area)
    grad_bf = member_gradient.astype(jnp.bfloat16)
    grad_flat = grad_bf.reshape(field_values, row_count)
    grad_out = lax.dot_general(
        hidden, grad_flat, (((0,), (1,)), ((), ())), preferred_element_type=jnp.float32
    )
    grad_bias = jnp.sum(grad_bf.astype(jnp.float32), axis=(1, 2))
    grad_hidden = lax.dot_general(
        grad_flat, w_out, (((0,), (1,)), ((), ())), preferred_element_type=jnp.float32
    )
    unused_value, pullback = jax.vjp(jax.nn.gelu, pre_act)
    grad_pre = pullback(grad_hidden)[0].astype(jnp.bfloat16)
    grad_rows = lax.dot_general(
        grad_pre,
        lax.all_gather(w_mix, "space", axis=0, tiled=True),
        (((1,), (1,)), ((), ())),
        preferred_element_type=jnp.float32,
    )
    grad_latents = grad_rows.astype(jnp.bfloat16).reshape(local_members, local_points, width)
    columns = flat_rows
    grad_mix = lax.psum_scatter(
        lax.dot_general(
            columns, grad_pre, (((0,), (0,)), ((), ())), preferred_element_type=jnp.float32
        ),
        "space",
        scatter_dimension=0,
        tiled=True,
    )
    grad_mix = lax.psum(grad_mix, "ens")
    grad_out, grad_bias, overall_loss = lax.psum(
        (grad_out, grad_bias, partial_loss), ("ens", "space")
    )
    loss = overall_loss / (local_points * lax.axis_size("space"))
    return (grad_latents, grad_mix, grad_out, grad_bias, loss)


def solution(mesh):
    in_specs = (P("ens", "space", None), P("space", None), P(), P(), P(None, "space"), P("space"))
    out_specs = (P("ens", "space", None), P("space", None), P(), P(), P())
    return jax.shard_map(body, mesh=mesh, in_specs=in_specs, out_specs=out_specs, check_vma=False)
```

profile of v0, /device:TPU:1, one launch (start us, length us, event | category | flops | bytes accessed | tf_op | source)
XLA Modules:
  0.0 1265.6 jit_solution(17231808029564454761)
XLA Ops:
  7.2 0.0 copy-start
  7.2 0.0 all-gather.3.cloned.1.call-start
  7.2 0.7 all-gather.3.cloned.1.call-update
  7.9 0.0 copy-start.1
  7.9 0.0 copy-start.4
  7.9 0.0 reduce-scatter.4.cloned.1.call-start
  8.0 140.1 %all-gather.3.cloned.1.call-done = bf16[1024,1024]{1,0:T(8,128)(2,1)} async-done(((bf16[32,1024]{1,0:T(8,128)(2,1)}), bf16[1024,1024]{1,0:T(8,128)(2,1)}) %all-gather.3.cloned.1.call-update) | async-done | bytes 2097168 | tf_op jit(solution)/shard_map/all_gather | solution.py:40
  148.1 0.0 copy-done
  148.1 3.2 multiply_convert_fusion
  151.3 0.0 copy-start.2
  151.3 0.0 copy-start.3
  151.3 0.0 copy-done.1
  151.3 0.0 copy-done.4
  151.3 0.4 fusion.8
  151.7 30.0 %all-gather = f32[16,8192]{1,0:T(8,128)S(1)} all-gather(f32[16,512]{1,0:T(8,128)S(1)} %fusion.8), channel_id=2, replica_groups=mesh['ens'=16,'space'=32] {'ens'}, dimensions={1}, use_global_device_ids=true | all-gather | bytes 557056 | tf_op jit(solution)/shard_map/all_gather | solution.py:49
  181.8 0.3 copy.15
  182.1 0.4 fusion.12
  182.5 0.0 copy-done.2
  182.5 0.0 copy-done.3
  182.5 0.6 convert_reduce_fusion
  183.2 1.5 fusion.6
  184.7 3.3 convolution_bitcast_fusion
  188.0 5.3 copy.13
  193.3 0.0 reduce-scatter.4.cloned.1.call-update
  193.4 0.0 all-reduce.4.cloned.1.call-start
  193.4 384.6 %reduce-scatter.4.cloned.1.call-done = f32[32,1024]{1,0:T(8,128)} async-done(((f32[1024,1024]{1,0:T(8,128)}), f32[32,1024]{1,0:T(8,128)}) %reduce-scatter.4.cloned.1.call-update) | async-done | bytes 131088
  578.0 1.9 copy.14
  579.9 0.0 all-reduce.4.cloned.1.call-update
  579.9 0.0 all-reduce.6.cloned.1.call-start
  580.0 0.9 fusion.15
  580.9 0.0 all-reduce.6.cloned.1.call-update
  580.9 3.9 fusion.7
  584.7 139.4 %all-reduce = (f32[16]{0:T(128)}, f32[]{:T(128)}) all-reduce(f32[16]{0:T(128)S(1)} %get-tuple-element.19, f32[]{:T(128)} %get-tuple-element.21), channel_id=1, replica_groups=mesh['ens'=16,'space'=32] {'ens','space'}, use_global_device_ids=true, to_apply=%region_5.0 | all-reduce | flops 17 | bytes 136 | tf_op jit(solution)/shard_map/psum | solution.py:79
  724.7 83.7 %all-reduce.4.cloned.1.call-done = f32[32,1024]{0,1:T(8,128)} async-done(((f32[32,1024]{0,1:T(8,128)}), f32[32,1024]{0,1:T(8,128)}) %all-reduce.4.cloned.1.call-update) | async-done | bytes 131088 | tf_op jit(solution)/shard_map/psum | solution.py:78
  808.5 1.9 copy.12
  810.4 446.2 %all-reduce.6.cloned.1.call-done = f32[1024,16]{0,1:T(8,128)} async-done(((f32[1024,16]{0,1:T(8,128)}), f32[1024,16]{0,1:T(8,128)}) %all-reduce.6.cloned.1.call-update) | async-done | bytes 65552 | tf_op jit(solution)/shard_map/psum | solution.py:79
  1256.5 1.5 copy.18
Async XLA Ops:
  7.2 140.9 %copy-start = (bf16[1,512,1024]{2,1,0:T(8,128)(2,1)S(1)}, bf16[1,512,1024]{2,1,0:T(8,128)(2,1)}, u32[]{:S(2)}) copy-start(bf16[1,512,1024]{2,1,0:T(8,128)(2,1)} %param.6) | copy-start | bytes 3145732
  7.2 140.9 %all-gather.3.cloned.1.call-start = ((), (), s32[]{:S(2)}) async-start(), calls=%async_computation.1 | async-start | bytes 2162688 | tf_op jit(solution)/shard_map/all_gather | solution.py:40
  7.9 143.4 %copy-start.1 = (bf16[1024,16]{0,1:T(8,128)(2,1)S(1)}, bf16[1024,16]{0,1:T(8,128)(2,1)}, u32[]{:S(2)}) copy-start(bf16[1024,16]{0,1:T(8,128)(2,1)} %param.8) | copy-start | bytes 98308
  7.9 143.4 %copy-start.4 = (f32[16]{0:T(128)S(1)}, f32[16]{0:T(128)}, u32[]{:S(2)}) copy-start(f32[16]{0:T(128)} %param.9) | copy-start | bytes 196
  7.9 570.1 %reduce-scatter.4.cloned.1.call-start = ((), (), s32[]{:S(2)}) async-start(), calls=%async_computation.4 | async-start | bytes 4325376
  151.3 31.2 %copy-start.2 = (f32[16,512]{1,0:T(8,128)S(1)}, f32[16,512]{1,0:T(8,128)}, u32[]{:S(2)}) copy-start(f32[16,512]{1,0:T(8,128)} %param.10) | copy-start | bytes 98308
  151.3 31.2 %copy-start.3 = (f32[512]{0:T(512)S(1)}, f32[512]{0:T(512)}, u32[]{:S(2)}) copy-start(f32[512]{0:T(512)} %param.11) | copy-start | bytes 6148
  193.4 615.1 %all-reduce.4.cloned.1.call-start = ((), (), s32[]{:S(2)}) async-start(), calls=%async_computation.2 | async-start | bytes 1048576 | tf_op jit(solution)/shard_map/psum | solution.py:78
  579.9 676.6 %all-reduce.6.cloned.1.call-start = ((), (), s32[]{:S(2)}) async-start(), calls=%async_computation.3 | async-start | bytes 131072 | tf_op jit(solution)/shard_map/psum | solution.py:79
Sparse Core Ops, SparseCore 0:
  12.3 135.6 all-gather.2
  193.5 384.4 reduce-scatter.3
  580.9 227.5 all-reduce.3
  815.2 441.2 all-reduce.5
where the time goes:
time: 1270 us
  waiting for transfers between devices  1060 us (83%)
  blocking collectives  169 us (13%)
  between operations  15.6 us (1%)
  matrix products  13.2 us (1%)
    psum x1, waiting for transfers between devices, body(): lax.psum((grad_out, grad_bias, partial_loss), ('ens', 'space'))  446 us
    unnamed x5, waiting for transfers between devices  385 us
    all_gather x1, waiting for transfers between devices, body(): lax.all_gather(w_mix, 'space', axis=0, tiled=True)  140 us
    psum x1, blocking collectives, body(): lax.psum((grad_out, grad_bias, partial_loss), ('ens', 'space'))  139 us
    psum x1, waiting for transfers between devices, body(): grad_mix = lax.psum(grad_mix, 'ens')  83.7 us
    all_gather x1, blocking collectives, body(): lax.all_gather(predicted_fields, 'ens', axis=1, tiled=True)  30 us
  transfers between devices with their start and end apart: 4, of which 4 were waited for; matrix products, arithmetic and copies ran while one was open for 1% of the time, Pallas kernels for 0%

commit v1 on v0

v1 whole, which is shorter than its diff:
```python
import jax
import jax.numpy as jnp
from jax import lax
from jax.sharding import Mesh
from jax.sharding import PartitionSpec as P

M = 16
smoothing = 0.1
Z, CORES, Y, X, H = 8, 2, 4, 4, 2
ENS, SPACE, PLANE = ("z", "c"), ("y", "x", "h"), ("y", "x")
f32, bf16 = jnp.float32, jnp.bfloat16
SWAP = ((0, 1), (1, 0))
MIRROR = tuple((z * H + h, (Z - 1 - z) * H + 1 - h) for z in range(Z) for h in range(H))


def split3(values):
    first = lax.reduce_precision(values, 8, 7)
    second = lax.reduce_precision(values - first, 8, 7)
    third = values - first - second
    return jnp.concatenate([first, second, third]).astype(bf16)


def scalar_rows(values, width):
    terms = split3(values)
    row = jnp.pad(terms, (0, width - terms.shape[0]))
    return jnp.pad(row[None, :], ((0, 7), (0, 0)))


def scalars_of(row, count):
    return row[:count] + row[count : 2 * count] + row[2 * count : 3 * count]


def pairwise(chosen, members, observed, weights):
    count_all = float(M)
    differ = chosen[:, None] - members[None]
    smooth = jnp.sqrt(differ * differ + smoothing * smoothing)
    slopes = differ / smooth
    to_truth = chosen - observed
    absolute = jnp.sqrt(to_truth * to_truth + smoothing * smoothing)
    pairs_norm = count_all * (count_all - 1.0)
    gradient = weights * (
        to_truth / absolute / count_all - jnp.sum(slopes, axis=1) / pairs_norm
    )
    partial = jnp.sum(
        weights
        * (absolute / count_all - (jnp.sum(smooth, axis=1) - smoothing) / (2.0 * pairs_norm))
    )
    return gradient, partial


def dot(a, b, ca, cb):
    return lax.dot_general(a, b, (((ca,), (cb,)), ((), ())), preferred_element_type=f32)


def body(latents, w_mix, w_out, bias, truth, area):
    core = lax.axis_index("c")
    first = core == 0
    half_ring = lax.axis_index("h")
    points, width = latents.shape[1], latents.shape[2]
    fields = w_out.shape[1]
    rows = w_mix.shape[0]
    half, ph = width // 2, points // 2
    lat = latents[0]

    def pick(a, b):
        return jnp.where(first, a, b)

    def ordered(own, other, axis):
        return pick(
            jnp.concatenate([own, other], axis), jnp.concatenate([other, own], axis)
        )

    mine = pick(w_mix[:, :half], w_mix[:, half:])
    far = lax.ppermute(mine, ("z", "h"), MIRROR)
    near = jnp.where(
        half_ring == 0, jnp.concatenate([mine, far], 0), jnp.concatenate([far, mine], 0)
    )
    sent = jnp.broadcast_to(near[None], (Y * X, H * rows, half))
    w_own = lax.all_to_all(sent, PLANE, 0, 0, tiled=True).reshape(width, half)
    w_oth = lax.ppermute(w_own, "c", SWAP)
    out_own = pick(w_out[:half], w_out[half:])
    out_oth = pick(w_out[half:], w_out[:half])

    pre_own = dot(lat, w_own, 1, 0)
    hid_own = jax.nn.gelu(pre_own).astype(bf16)
    pre_oth = dot(lat, w_oth, 1, 0)
    hid_oth = jax.nn.gelu(pre_oth).astype(bf16)
    forecast = dot(out_own, hid_own, 0, 1) + dot(out_oth, hid_oth, 0, 1) + bias[:, None]

    fc_own = pick(forecast[:, :ph], forecast[:, ph:])
    fc_oth = lax.ppermute(pick(forecast[:, ph:], forecast[:, :ph]), "c", SWAP)
    chosen = jnp.stack([fc_own, fc_oth])
    members = lax.all_to_all(
        jnp.broadcast_to(chosen.reshape(1, 2 * fields, ph), (Z, 2 * fields, ph)),
        "z", 0, 0, tiled=True,
    ).reshape(M, fields, ph)
    observed = pick(truth[:, :ph], truth[:, ph:])
    weights = pick(area[:ph], area[ph:])
    gradient, partial = pairwise(chosen, members, observed, weights)
    grad_bf = gradient.astype(bf16)
    g_back = lax.ppermute(grad_bf[1], "c", SWAP)
    g = ordered(grad_bf[0], g_back, 1)
    sums = jnp.concatenate(
        [jnp.sum(grad_bf.astype(f32), axis=(0, 2)), partial.reshape(1)]
    )

    def backward(pre, out):
        unused_value, pullback = jax.vjp(jax.nn.gelu, pre)
        return pullback(dot(g, out, 0, 1))[0].astype(bf16)

    gp_oth = backward(pre_oth, out_oth)
    mix_oth = dot(lat, gp_oth, 0, 0)
    mix_in = lax.ppermute(mix_oth.astype(bf16), "c", SWAP)
    head_oth = jnp.concatenate(
        [dot(g, hid_oth, 1, 0).astype(bf16), scalar_rows(sums, half)], 0
    )
    head_in = lax.ppermute(head_oth, "c", SWAP).astype(f32)
    gp_own = backward(pre_own, out_own)
    mix = dot(lat, gp_own, 0, 0) + mix_in.astype(f32)
    head = dot(g, hid_own, 1, 0) + head_in[:fields]
    sums = sums + scalars_of(head_in[fields], fields + 1)
    grad_rows = dot(gp_own, w_own, 1, 1) + dot(gp_oth, w_oth, 1, 1)
    grad_latents = grad_rows.astype(bf16)[None]

    extra = jnp.concatenate([head.astype(bf16), scalar_rows(sums, half)], 0)
    sent = jnp.concatenate(
        [
            mix.astype(bf16).reshape(Y * X, H * rows, half),
            jnp.broadcast_to(extra[None], (Y * X,) + extra.shape),
        ],
        1,
    )
    got = jnp.sum(lax.all_to_all(sent, PLANE, 0, 0, tiled=True).astype(f32), axis=0)
    mix, head = got[: H * rows], got[H * rows : H * rows + fields]
    sums = scalars_of(got[H * rows + fields], fields + 1)

    per, hper = rows // Z, fields // Z
    tail = jnp.broadcast_to(scalar_rows(sums, half)[:1][None], (H * Z, 1, half))
    head = jnp.broadcast_to(
        head.astype(bf16).reshape(1, Z, hper, half), (H, Z, hper, half)
    ).reshape(H * Z, hper, half)
    sent = jnp.concatenate(
        [mix.astype(bf16).reshape(H * Z, per, half), head, tail, jnp.zeros_like(tail)], 1
    )
    got = jnp.sum(lax.all_to_all(sent, ("h", "z"), 0, 0, tiled=True).astype(f32), axis=0)
    sums = scalars_of(got[per + hper], fields + 1)
    sent = jnp.broadcast_to(got[None].astype(bf16), (Z,) + got.shape)
    got = lax.all_to_all(sent, "z", 0, 0, tiled=True)
    own = jnp.concatenate(
        [got[:, :per].reshape(rows, half), got[:, per : per + hper].reshape(fields, half)], 0
    )
    other = lax.ppermute(own, "c", SWAP)
    whole = ordered(own, other, 1).astype(f32)
    grad_mix, grad_out = whole[:rows], whole[rows:].T
    loss = sums[fields] / (points * Y * X * H)
    return grad_latents, grad_mix, grad_out, sums[:fields], loss


def solution(mesh):
    fine = Mesh(mesh.devices.reshape(Z, CORES, Y, X, H), ("z", "c", "y", "x", "h"))
    in_specs = (P(ENS, SPACE, None), P(SPACE, None), P(), P(), P(None, SPACE), P(SPACE))
    out_specs = (P(ENS, SPACE, None), P(SPACE, None), P(), P(), P())
    return jax.shard_map(
        body, mesh=fine, in_specs=in_specs, out_specs=out_specs, check_vma=False
    )
```

time: 1270 us -> 169 us (0.13)
  waiting for transfers between devices: 1060 us -> 59.1 us
  blocking collectives: 169 us -> 20 us
  starting transfers between devices: 0.16 us -> 62.2 us
  between operations: 15.6 us -> 2.82 us
    psum x2 -> x0, waiting for transfers between devices: 530 us -> none  [the longest x1 446 us: body(): lax.psum((grad_out, grad_bias, partial_loss), ('ens', 'space'))]
    unnamed x5 -> x0, waiting for transfers between devices: 385 us -> none
    all_gather x1 -> x0, waiting for transfers between devices: 140 us -> none  [body(): lax.all_gather(w_mix, 'space', axis=0, tiled=True)]
    psum x1 -> x0, blocking collectives: 139 us -> none  [body(): lax.psum((grad_out, grad_bias, partial_loss), ('ens', 'space'))]
    all_to_all x0 -> x4, waiting for transfers between devices: none -> 54.9 us  [the longest x1 24.3 us: body(): lax.all_to_all(sent, PLANE, 0, 0, tiled=True).astype(f32)]
    ppermute x0 -> x7, starting transfers between devices: none -> 35.8 us  [the longest x1 11.9 us: body(): far = lax.ppermute(mine, ('z', 'h'), MIRROR)]
    all_gather x1 -> x0, blocking collectives: 30 us -> none  [body(): lax.all_gather(predicted_fields, 'ens', axis=1, tiled=True)]
    all_to_all x0 -> x4, starting transfers between devices: none -> 26.4 us  [the longest x1 10.2 us: body(): lax.all_to_all(sent, ('h', 'z'), 0, 0, tiled=True).astype(f32)]
  transfers between devices with their start and end apart: 4 -> 11, of which waited for: 4 -> 9; matrix products, arithmetic and copies ran while one was open for 1% -> 8% of each run, Pallas kernels for 0% -> 0%
where the time goes in v1:
time: 169 us; the launch traced here: 168 us
  starting transfers between devices  62.2 us (37%)
  waiting for transfers between devices  59.1 us (35%)
  blocking collectives  20 us (12%)
  matrix products  14.1 us (8%)
  other arithmetic  5.36 us (3%)
  local copies, waits for them, and re-layouts  4.74 us (3%)
  between operations  2.82 us (2%)
    all_to_all x1, waiting for transfers between devices, body(): lax.all_to_all(sent, PLANE, 0, 0, tiled=True).astype(f32)  24.3 us
    all_to_all x1, blocking collectives, body(): w_own = lax.all_to_all(sent, PLANE, 0, 0, tiled=True).reshape(width, half)  20 us
    all_to_all x1, waiting for transfers between devices, body(): lax.all_to_all(jnp.broadcast_to(chosen.reshape(1, 2 * fields, ph), (Z, 2...  14.2 us
    dot_general x12, matrix products, dot(): lax.dot_general(a, b, (((ca,), (cb,)), ((), ())), preferred_element_type=...  14.1 us
    ppermute x1, starting transfers between devices, body(): far = lax.ppermute(mine, ('z', 'h'), MIRROR)  11.9 us
    all_to_all x1, starting transfers between devices, body(): lax.all_to_all(sent, ('h', 'z'), 0, 0, tiled=True).astype(f32)  10.2 us
    all_to_all x1, waiting for transfers between devices, body(): lax.all_to_all(sent, ('h', 'z'), 0, 0, tiled=True).astype(f32)  9.83 us
    all_to_all x1, starting transfers between devices, body(): lax.all_to_all(jnp.broadcast_to(chosen.reshape(1, 2 * fields, ph), (Z, 2...  7.36 us
  transfers between devices with their start and end apart: 11, of which 9 were waited for; matrix products, arithmetic and copies ran while one was open for 8% of the time, Pallas kernels for 0%

profile of v1, /device:TPU:1, one launch (start us, length us, event | category | flops | bytes accessed | tf_op | source)
XLA Modules:
  0.0 168.3 jit_solution(1027883464973861092)
XLA Ops:
  0.7 0.9 slice_select_fusion
  1.5 11.9 %collective-permute-start = (bf16[32,512]{1,0:T(8,128)(2,1)S(1)}, bf16[32,512]{1,0:T(8,128)(2,1)S(1)}, u32[]{:S(2)}, u32[]{:S(2)}) collective-permute-start(bf16[32,512]{1,0:T(8,128)(2,1)S(1)} %slice_select_fusion), channel_id=1, source_target_pairs={{0,449},{1,448},{64,385},{65,384},{128,321},{129,320},{192,257},{1... | collective-permute-start | bytes 98312 | tf_op jit(solution)/shard_map/ppermute | solution.py:74
  13.5 1.3 collective-permute-done
  14.8 0.1 broadcast_in_dim.24
  14.9 20.0 %all_to_all.25 = bf16[16,64,512]{2,1,0:T(8,128)(2,1)S(1)} all-to-all(bf16[16,64,512]{2,1,0:T(8,128)(2,1)S(1)} %broadcast_in_dim.24), channel_id=1, replica_groups=mesh['z'=8,'c'=2,'y'=4,'x'=4,'h'=2] {'y','x'}, dimensions={0} | all-to-all | bytes 2097152 | tf_op jit(solution)/shard_map/all_to_all | solution.py:79
  34.9 6.7 %collective-permute-start.1 = (bf16[1024,512]{1,0:T(8,128)(2,1)S(1)}, bf16[1024,512]{1,0:T(8,128)(2,1)S(1)}, u32[]{:S(2)}, u32[]{:S(2)}) collective-permute-start(bf16[1024,512]{1,0:T(8,128)(2,1)S(1)} %bitcast.64), channel_id=1, source_target_pairs={{0,32},{32,0},{1,33},{33,1},{2,34},{34,2},{3,35},{35,3},{4,36},{36... | collective-permute-start | bytes 3145736 | tf_op jit(solution)/shard_map/ppermute | solution.py:80
  41.6 1.8 %multiply_convert_fusion.1 = (bf16[512,512]{0,1:T(8,128)(2,1)S(1)}, f32[512,512]{0,1:T(8,128)}) fusion(bf16[1024,512]{1,0:T(8,128)(2,1)S(1)} %bitcast.65, bf16[1,512,1024]{2,1,0:T(8,128)(2,1)S(1)} %copy-done), kind=kOutput, calls=%fused_computation.38 | convolution fusion | flops 539230208 | bytes 3670016 | tf_op jit(solution)/shard_map/dot_general | solution.py:52
  43.5 0.2 fusion.32
  43.7 0.2 collective-permute-done.1
  43.9 1.8 %multiply_convert_fusion = (bf16[512,512]{0,1:T(8,128)(2,1)S(1)}, f32[512,512]{0,1:T(8,128)}) fusion(bf16[1024,512]{1,0:T(8,128)(2,1)S(1)} %collective-permute-done.1, bf16[1,512,1024]{2,1,0:T(8,128)(2,1)S(1)} %copy-done), kind=kOutput, calls=%fused_computation.37 | convolution fusion | flops 539230208 | bytes 3670016 | tf_op jit(solution)/shard_map/dot_general | solution.py:52
  45.7 0.1 fusion.3
  45.9 2.3 %collective-permute-start.2 = (f32[16,256]{1,0:T(8,128)S(1)}, f32[16,256]{1,0:T(8,128)S(1)}, u32[]{:S(2)}, u32[]{:S(2)}) collective-permute-start(f32[16,256]{1,0:T(8,128)S(1)} %get-tuple-element.17), channel_id=1, source_target_pairs={{0,32},{32,0},{1,33},{33,1},{2,34},{34,2},{3,35},{35,3},{4,36},{36... | collective-permute-start | bytes 49160 | tf_op jit(solution)/shard_map/ppermute | solution.py:91
  48.2 0.8 collective-permute-done.2
  49.0 0.7 broadcast_in_dim.26
  49.8 7.4 %all-to-all-start.1 = ((f32[8,32,256]{2,1,0:T(8,128)}), f32[8,32,256]{2,1,0:T(8,128)S(1)}, u32[]{:S(2)}, u32[]{:S(2)}) async-start(f32[8,32,256]{2,1,0:T(8,128)} %broadcast_in_dim.26), calls=%async_computation.1 | async-start | bytes 524288 | tf_op jit(solution)/shard_map/all_to_all | solution.py:93
  57.2 14.2 %all-to-all-done.1 = f32[8,32,256]{2,1,0:T(8,128)S(1)} async-done(((f32[8,32,256]{2,1,0:T(8,128)}), f32[8,32,256]{2,1,0:T(8,128)S(1)}, u32[]{:S(2)}, u32[]{:S(2)}) %all-to-all-start.1) | async-done | bytes 262176 | tf_op jit(solution)/shard_map/all_to_all | solution.py:93
  71.4 0.2 fusion.25
  71.7 0.6 convert_reduce_fusion.2
  72.3 0.7 reduce-precision_convert_fusion.5
  73.0 5.2 %collective-permute-start.3 = (bf16[16,256]{1,0:T(8,128)(2,1)S(1)}, bf16[16,256]{1,0:T(8,128)(2,1)S(1)}, u32[]{:S(2)}, u32[]{:S(2)}) collective-permute-start(bf16[16,256]{1,0:T(8,128)(2,1)S(1)} %get-tuple-element.19), channel_id=1, source_target_pairs={{0,32},{32,0},{1,33},{33,1},{2,34},{34,2},{3,35},{35,3},{4,36},{36... | collective-permute-start | bytes 24584 | tf_op jit(solution)/shard_map/ppermute | solution.py:101
  78.4 0.7 collective-permute-done.3
  79.1 0.2 convolution_convert_fusion.1
  79.3 2.3 %collective-permute-start.5 = (bf16[24,512]{1,0:T(8,128)(2,1)S(1)}, bf16[24,512]{1,0:T(8,128)(2,1)S(1)}, u32[]{:S(2)}, u32[]{:S(2)}) collective-permute-start(bf16[24,512]{1,0:T(8,128)(2,1)S(1)} %fusion.30), channel_id=1, source_target_pairs={{0,32},{32,0},{1,33},{33,1},{2,34},{34,2},{3,35},{35,3},{4,36},{36... | collective-permute-start | bytes 73736 | tf_op jit(solution)/shard_map/ppermute | solution.py:117
  81.6 2.1 %fusion.18 = bf16[512,512]{0,1:T(8,128)(2,1)S(1)} fusion(f32[512,512]{0,1:T(8,128)} %get-tuple-element.29, pred[]{:T(512)S(6)} %eq.6, bf16[1024,16]{0,1:T(8,128)(2,1)S(1)} %copy-done.6, bf16[16,256]{1,0:T(8,128)(2,1)S(1)} %collective-permute-done.3, bf16[16,256]{1,0:T(8,128)(2,1)S(1)} %get-tuple-element.18), kind=kOutput, calls=%fused_computation.32 | convolution fusion | flops 13713408 | bytes 1623040 | tf_op jit(solution)/shard_map/dot_general | solution.py:52
  83.7 0.7 fusion.2
  84.4 2.1 %collective-permute-start.4 = (bf16[1024,512]{0,1:T(8,128)(2,1)S(1)}, bf16[1024,512]{0,1:T(8,128)(2,1)S(1)}, u32[]{:S(2)}, u32[]{:S(2)}) collective-permute-start(bf16[1024,512]{0,1:T(8,128)(2,1)S(1)} %fusion.2), channel_id=1, source_target_pairs={{0,32},{32,0},{1,33},{33,1},{2,34},{34,2},{3,35},{35,3},{4,36},{36... | collective-permute-start | bytes 3145736 | tf_op jit(solution)/shard_map/ppermute | solution.py:113
  86.5 0.9 fusion.11
  87.6 0.2 fusion.4
  87.9 1.1 collective-permute-done.4
  89.0 0.7 fusion
  89.7 0.5 copy.25
  90.3 1.2 pad_maximum_fusion
  91.5 3.7 %all-to-all-start.2 = ((bf16[16,88,512]{2,1,0:T(8,128)(2,1)}), bf16[16,88,512]{2,1,0:T(8,128)(2,1)S(1)}, u32[]{:S(2)}, u32[]{:S(2)}) async-start(bf16[16,88,512]{2,1,0:T(8,128)(2,1)} %pad_maximum_fusion), calls=%async_computation.2 | async-start | bytes 2883584 | tf_op jit(solution)/shard_map/all_to_all | solution.py:133
  95.3 24.3 %all-to-all-done.2 = bf16[16,88,512]{2,1,0:T(8,128)(2,1)S(1)} async-done(((bf16[16,88,512]{2,1,0:T(8,128)(2,1)}), bf16[16,88,512]{2,1,0:T(8,128)(2,1)S(1)}, u32[]{:S(2)}, u32[]{:S(2)}) %all-to-all-start.2) | async-done | bytes 1441824 | tf_op jit(solution)/shard_map/all_to_all | solution.py:133
  119.7 0.2 convert_reduce_fusion
  120.2 0.8 maximum_maximum_fusion
  120.9 10.2 %all-to-all-start.3 = ((bf16[16,8,512]{2,1,0:T(8,128)(2,1)}), bf16[16,8,512]{2,1,0:T(8,128)(2,1)S(1)}, u32[]{:S(2)}, u32[]{:S(2)}) async-start(bf16[16,8,512]{2,1,0:T(8,128)(2,1)} %maximum_maximum_fusion), calls=%async_computation.3 | async-start | bytes 262144 | tf_op jit(solution)/shard_map/all_to_all | solution.py:145
  131.1 2.1 %fusion.56 = f32[512,1024]{1,0:T(8,128)S(1)} fusion(bf16[512,512]{0,1:T(8,128)(2,1)} %copy-done.4, bf16[1024,512]{1,0:T(8,128)(2,1)} %bitcast.66), kind=kOutput, calls=%fused_computation.116 | convolution fusion | flops 536870912 | bytes 3670016 | tf_op jit(solution)/shard_map/dot_general | solution.py:52
  133.3 9.8 %all-to-all-done.3 = bf16[16,8,512]{2,1,0:T(8,128)(2,1)S(1)} async-done(((bf16[16,8,512]{2,1,0:T(8,128)(2,1)}), bf16[16,8,512]{2,1,0:T(8,128)(2,1)S(1)}, u32[]{:S(2)}, u32[]{:S(2)}) %all-to-all-start.3) | async-done | bytes 131104 | tf_op jit(solution)/shard_map/all_to_all | solution.py:145
  143.1 0.6 broadcast_in_dim.67
  143.8 5.1 %all-to-all-start.4 = ((bf16[8,8,512]{2,1,0:T(8,128)(2,1)}), bf16[8,8,512]{2,1,0:T(8,128)(2,1)S(1)}, u32[]{:S(2)}, u32[]{:S(2)}) async-start(bf16[8,8,512]{2,1,0:T(8,128)(2,1)} %broadcast_in_dim.67), calls=%async_computation.4 | async-start | bytes 131072 | tf_op jit(solution)/shard_map/all_to_all | solution.py:148
  148.9 3.1 %fusion.1 = bf16[1,512,1024]{2,1,0:T(8,128)(2,1)} fusion(f32[512,1024]{1,0:T(8,128)S(1)} %fusion.56, bf16[512,512]{0,1:T(8,128)(2,1)} %copy-done.3, bf16[1024,512]{1,0:T(8,128)(2,1)} %copy-done.2), kind=kOutput, calls=%fused_computation.10 | convolution fusion | flops 537919488 | bytes 4718592 | tf_op jit(solution)/shard_map/dot_general | solution.py:52
  152.1 6.6 %all-to-all-done.4 = bf16[8,8,512]{2,1,0:T(8,128)(2,1)S(1)} async-done(((bf16[8,8,512]{2,1,0:T(8,128)(2,1)}), bf16[8,8,512]{2,1,0:T(8,128)(2,1)S(1)}, u32[]{:S(2)}, u32[]{:S(2)}) %all-to-all-start.4) | async-done | bytes 65568 | tf_op jit(solution)/shard_map/all_to_all | solution.py:148
  158.8 5.3 %collective-permute-start.6 = (bf16[48,512]{1,0:T(8,128)(2,1)S(1)}, bf16[48,512]{1,0:T(8,128)(2,1)S(1)}, u32[]{:S(2)}, u32[]{:S(2)}) collective-permute-start(bf16[48,512]{1,0:T(8,128)(2,1)S(1)} %constant_dynamic-update-slice_fusion), channel_id=1, source_target_pairs={{0,32},{32,0},{1,33},{33,1},{2,34},{34,2},{3,35},{35,3},{4,36},{36... | collective-permute-start | bytes 147464 | tf_op jit(solution)/shard_map/ppermute | solution.py:152
  164.1 0.5 slice_bitcast_fusion.3
  164.6 0.6 slice.152
  165.9 0.6 slice_bitcast_fusion
  166.5 0.7 slice.168
  (60 shorter events, 1.0 us)
Async XLA Ops:
  0.6 41.0 %copy-start = (bf16[1,512,1024]{2,1,0:T(8,128)(2,1)S(1)}, bf16[1,512,1024]{2,1,0:T(8,128)(2,1)}, u32[]{:S(2)}) copy-start(bf16[1,512,1024]{2,1,0:T(8,128)(2,1)} %param.6) | copy-start | bytes 3145732
  1.5 13.2 %collective-permute-start = (bf16[32,512]{1,0:T(8,128)(2,1)S(1)}, bf16[32,512]{1,0:T(8,128)(2,1)S(1)}, u32[]{:S(2)}, u32[]{:S(2)}) collective-permute-start(bf16[32,512]{1,0:T(8,128)(2,1)S(1)} %slice_select_fusion), channel_id=1, source_target_pairs={{0,449},{1,448},{64,385},{65,384},{128,321},{129,320},{192,257},{1... | collective-permute-start | bytes 98312 | tf_op jit(solution)/shard_map/ppermute | solution.py:74
  34.9 8.6 %copy-start.1 = (bf16[16,64,512]{2,1,0:T(8,128)(2,1)}, bf16[16,64,512]{2,1,0:T(8,128)(2,1)S(1)}, u32[]{:S(2)}) copy-start(bf16[16,64,512]{2,1,0:T(8,128)(2,1)S(1)} %all_to_all.25) | copy-start | bytes 3145732
  34.9 8.6 %copy-start.6 = (bf16[1024,16]{0,1:T(8,128)(2,1)S(1)}, bf16[1024,16]{0,1:T(8,128)(2,1)}, u32[]{:S(2)}) copy-start(bf16[1024,16]{0,1:T(8,128)(2,1)} %param.8) | copy-start | bytes 98308
  34.9 9.0 %collective-permute-start.1 = (bf16[1024,512]{1,0:T(8,128)(2,1)S(1)}, bf16[1024,512]{1,0:T(8,128)(2,1)S(1)}, u32[]{:S(2)}, u32[]{:S(2)}) collective-permute-start(bf16[1024,512]{1,0:T(8,128)(2,1)S(1)} %bitcast.64), channel_id=1, source_target_pairs={{0,32},{32,0},{1,33},{33,1},{2,34},{34,2},{3,35},{35,3},{4,36},{36... | collective-permute-start | bytes 3145736 | tf_op jit(solution)/shard_map/ppermute | solution.py:80
  43.6 2.1 %copy-start.8 = (f32[16]{0:T(128)S(1)}, f32[16]{0:T(128)}, u32[]{:S(2)}) copy-start(f32[16]{0:T(128)} %param.9) | copy-start | bytes 196
  43.7 13.5 %copy-start.7 = (f32[512]{0:T(512)S(1)}, f32[512]{0:T(512)}, u32[]{:S(2)}) copy-start(f32[512]{0:T(512)} %param.11) | copy-start | bytes 6148
  43.7 13.5 %copy-start.5 = (f32[16,512]{1,0:T(8,128)S(1)}, f32[16,512]{1,0:T(8,128)}, u32[]{:S(2)}) copy-start(f32[16,512]{1,0:T(8,128)} %param.10) | copy-start | bytes 98308
  43.9 1.8 %copy-start.2 = (bf16[1024,512]{1,0:T(8,128)(2,1)}, bf16[1024,512]{1,0:T(8,128)(2,1)S(1)}, u32[]{:S(2)}) copy-start(bf16[1024,512]{1,0:T(8,128)(2,1)S(1)} %collective-permute-done.1) | copy-start | bytes 3145732
  45.9 3.1 %collective-permute-start.2 = (f32[16,256]{1,0:T(8,128)S(1)}, f32[16,256]{1,0:T(8,128)S(1)}, u32[]{:S(2)}, u32[]{:S(2)}) collective-permute-start(f32[16,256]{1,0:T(8,128)S(1)} %get-tuple-element.17), channel_id=1, source_target_pairs={{0,32},{32,0},{1,33},{33,1},{2,34},{34,2},{3,35},{35,3},{4,36},{36... | collective-permute-start | bytes 49160 | tf_op jit(solution)/shard_map/ppermute | solution.py:91
  49.8 21.6 %all-to-all-start.1 = ((f32[8,32,256]{2,1,0:T(8,128)}), f32[8,32,256]{2,1,0:T(8,128)S(1)}, u32[]{:S(2)}, u32[]{:S(2)}) async-start(f32[8,32,256]{2,1,0:T(8,128)} %broadcast_in_dim.26), calls=%async_computation.1 | async-start | bytes 524288 | tf_op jit(solution)/shard_map/all_to_all | solution.py:93
  73.0 6.1 %collective-permute-start.3 = (bf16[16,256]{1,0:T(8,128)(2,1)S(1)}, bf16[16,256]{1,0:T(8,128)(2,1)S(1)}, u32[]{:S(2)}, u32[]{:S(2)}) collective-permute-start(bf16[16,256]{1,0:T(8,128)(2,1)S(1)} %get-tuple-element.19), channel_id=1, source_target_pairs={{0,32},{32,0},{1,33},{33,1},{2,34},{34,2},{3,35},{35,3},{4,36},{36... | collective-permute-start | bytes 24584 | tf_op jit(solution)/shard_map/ppermute | solution.py:101
  79.3 8.1 %collective-permute-start.5 = (bf16[24,512]{1,0:T(8,128)(2,1)S(1)}, bf16[24,512]{1,0:T(8,128)(2,1)S(1)}, u32[]{:S(2)}, u32[]{:S(2)}) collective-permute-start(bf16[24,512]{1,0:T(8,128)(2,1)S(1)} %fusion.30), channel_id=1, source_target_pairs={{0,32},{32,0},{1,33},{33,1},{2,34},{34,2},{3,35},{35,3},{4,36},{36... | collective-permute-start | bytes 73736 | tf_op jit(solution)/shard_map/ppermute | solution.py:117
  83.7 3.7 %copy-start.3 = (bf16[512,512]{0,1:T(8,128)(2,1)}, bf16[512,512]{0,1:T(8,128)(2,1)S(1)}, u32[]{:S(2)}) copy-start(bf16[512,512]{0,1:T(8,128)(2,1)S(1)} %fusion.18) | copy-start | bytes 1572868
  83.7 2.8 %copy-start.9 = (f32[512,512]{0,1:T(8,128)S(1)}, f32[512,512]{0,1:T(8,128)}, u32[]{:S(2)}) copy-start(f32[512,512]{0,1:T(8,128)} %get-tuple-element.27) | copy-start | bytes 3145732
  84.4 4.6 %collective-permute-start.4 = (bf16[1024,512]{0,1:T(8,128)(2,1)S(1)}, bf16[1024,512]{0,1:T(8,128)(2,1)S(1)}, u32[]{:S(2)}, u32[]{:S(2)}) collective-permute-start(bf16[1024,512]{0,1:T(8,128)(2,1)S(1)} %fusion.2), channel_id=1, source_target_pairs={{0,32},{32,0},{1,33},{33,1},{2,34},{34,2},{3,35},{35,3},{4,36},{36... | collective-permute-start | bytes 3145736 | tf_op jit(solution)/shard_map/ppermute | solution.py:113
  87.4 1.6 copy-start.4
  91.5 28.1 %all-to-all-start.2 = ((bf16[16,88,512]{2,1,0:T(8,128)(2,1)}), bf16[16,88,512]{2,1,0:T(8,128)(2,1)S(1)}, u32[]{:S(2)}, u32[]{:S(2)}) async-start(bf16[16,88,512]{2,1,0:T(8,128)(2,1)} %pad_maximum_fusion), calls=%async_computation.2 | async-start | bytes 2883584 | tf_op jit(solution)/shard_map/all_to_all | solution.py:133
  120.9 22.1 %all-to-all-start.3 = ((bf16[16,8,512]{2,1,0:T(8,128)(2,1)}), bf16[16,8,512]{2,1,0:T(8,128)(2,1)S(1)}, u32[]{:S(2)}, u32[]{:S(2)}) async-start(bf16[16,8,512]{2,1,0:T(8,128)(2,1)} %maximum_maximum_fusion), calls=%async_computation.3 | async-start | bytes 262144 | tf_op jit(solution)/shard_map/all_to_all | solution.py:145
  143.8 14.9 %all-to-all-start.4 = ((bf16[8,8,512]{2,1,0:T(8,128)(2,1)}), bf16[8,8,512]{2,1,0:T(8,128)(2,1)S(1)}, u32[]{:S(2)}, u32[]{:S(2)}) async-start(bf16[8,8,512]{2,1,0:T(8,128)(2,1)} %broadcast_in_dim.67), calls=%async_computation.4 | async-start | bytes 131072 | tf_op jit(solution)/shard_map/all_to_all | solution.py:148
  158.8 7.1 %collective-permute-start.6 = (bf16[48,512]{1,0:T(8,128)(2,1)S(1)}, bf16[48,512]{1,0:T(8,128)(2,1)S(1)}, u32[]{:S(2)}, u32[]{:S(2)}) collective-permute-start(bf16[48,512]{1,0:T(8,128)(2,1)S(1)} %constant_dynamic-update-slice_fusion), channel_id=1, source_target_pairs={{0,32},{32,0},{1,33},{33,1},{2,34},{34,2},{3,35},{35,3},{4,36},{36... | collective-permute-start | bytes 147464 | tf_op jit(solution)/shard_map/ppermute | solution.py:152

commit v2 on v1

v2 whole, which is shorter than its diff:
```python
import jax
import jax.numpy as jnp
from jax import lax
from jax.sharding import Mesh
from jax.sharding import PartitionSpec as P

M = 16
smoothing = 0.1
FAR, NEAR, CORES, Y, X, H = 2, 4, 2, 4, 4, 2
Z = FAR * NEAR
RING = ("far", "near")
ENS, SPACE, PLANE = ("far", "near", "c"), ("y", "x", "h"), ("y", "x")
f32, bf16 = jnp.float32, jnp.bfloat16
SWAP = ((0, 1), (1, 0))
ACROSS = tuple((far * H + h, (1 - far) * H + 1 - h) for far in range(FAR) for h in range(H))


def split3(values):
    first = lax.reduce_precision(values, 8, 7)
    second = lax.reduce_precision(values - first, 8, 7)
    third = values - first - second
    return jnp.concatenate([first, second, third]).astype(bf16)


def scalar_rows(values, width):
    terms = split3(values)
    row = jnp.pad(terms, (0, width - terms.shape[0]))
    return jnp.pad(row[None, :], ((0, 7), (0, 0)))


def scalars_of(row, count):
    return row[:count] + row[count : 2 * count] + row[2 * count : 3 * count]


def member_sums(chosen, members):
    differ = chosen[None] - members
    smooth = jnp.sqrt(differ * differ + smoothing * smoothing)
    return jnp.sum(differ / smooth, axis=0), jnp.sum(smooth, axis=0)


def all_to_all(x, axes):
    return lax.all_to_all(x, axes, 0, 0, tiled=True)


def copies(x, count):
    return jnp.broadcast_to(x[None], (count,) + x.shape)


def dot(a, b, ca, cb):
    return lax.dot_general(a, b, (((ca,), (cb,)), ((), ())), preferred_element_type=f32)


def body(latents, w_mix, w_out, bias, truth, area):
    core = lax.axis_index("c")
    first = core == 0
    half_ring = lax.axis_index("h")
    points, width = latents.shape[1], latents.shape[2]
    fields = w_out.shape[1]
    rows = w_mix.shape[0]
    half = width // 2
    lat = latents[0]

    def pick(a, b):
        return jnp.where(first, a, b)

    def ordered(own, other, axis):
        return pick(
            jnp.concatenate([own, other], axis), jnp.concatenate([other, own], axis)
        )

    mine = pick(w_mix[:, :half], w_mix[:, half:])
    far = lax.ppermute(mine, ("far", "h"), ACROSS)
    near = jnp.where(
        half_ring == 0, jnp.concatenate([mine, far], 0), jnp.concatenate([far, mine], 0)
    )
    sent = jnp.broadcast_to(near[None], (Y * X, H * rows, half))
    w_own = lax.all_to_all(sent, PLANE, 0, 0, tiled=True).reshape(width, half)
    w_oth = lax.ppermute(w_own, "c", SWAP)
    out_own = pick(w_out[:half], w_out[half:])
    out_oth = pick(w_out[half:], w_out[:half])

    pre_own = dot(lat, w_own, 1, 0)
    hid_own = jax.nn.gelu(pre_own).astype(bf16)
    pre_oth = dot(lat, w_oth, 1, 0)
    hid_oth = jax.nn.gelu(pre_oth).astype(bf16)
    forecast = dot(out_own, hid_own, 0, 1) + dot(out_oth, hid_oth, 0, 1) + bias[:, None]

    sent = jnp.broadcast_to(forecast[None], (Z, fields, points))
    members = lax.all_to_all(sent, RING, 0, 0, tiled=True)
    others = lax.ppermute(members, "c", SWAP)
    slope, smooth = member_sums(forecast, members)
    slope_oth, smooth_oth = member_sums(forecast, others)
    slope, smooth = slope + slope_oth, smooth + smooth_oth
    count_all = float(M)
    pairs_norm = count_all * (count_all - 1.0)
    to_truth = forecast - truth
    absolute = jnp.sqrt(to_truth * to_truth + smoothing * smoothing)
    g = (area * (to_truth / absolute / count_all - slope / pairs_norm)).astype(bf16)
    partial = jnp.sum(
        area * (absolute / count_all - (smooth - smoothing) / (2.0 * pairs_norm))
    )
    sums = jnp.concatenate([jnp.sum(g.astype(f32), axis=1), partial.reshape(1)])

    def backward(pre, out):
        unused_value, pullback = jax.vjp(jax.nn.gelu, pre)
        return pullback(dot(g, out, 0, 1))[0].astype(bf16)

    gp_oth = backward(pre_oth, out_oth)
    mix_oth = dot(lat, gp_oth, 0, 0)
    mix_in = lax.ppermute(mix_oth.astype(bf16), "c", SWAP)
    head_oth = jnp.concatenate(
        [dot(g, hid_oth, 1, 0).astype(bf16), scalar_rows(sums, half)], 0
    )
    head_in = lax.ppermute(head_oth, "c", SWAP).astype(f32)
    gp_own = backward(pre_own, out_own)
    mix = dot(lat, gp_own, 0, 0) + mix_in.astype(f32)
    head = dot(g, hid_own, 1, 0) + head_in[:fields]
    sums = sums + scalars_of(head_in[fields], fields + 1)
    grad_rows = dot(gp_own, w_own, 1, 1) + dot(gp_oth, w_oth, 1, 1)
    grad_latents = grad_rows.astype(bf16)[None]

    extra = jnp.concatenate([head.astype(bf16), scalar_rows(sums, half)], 0)
    sent = jnp.concatenate(
        [
            mix.astype(bf16).reshape(Y * X, H * rows, half),
            jnp.broadcast_to(extra[None], (Y * X,) + extra.shape),
        ],
        1,
    )
    got = jnp.sum(lax.all_to_all(sent, PLANE, 0, 0, tiled=True).astype(f32), axis=0)

    part, hpart = rows // NEAR, fields // NEAR
    sums = scalars_of(got[H * rows + fields], fields + 1)
    mix = got[: H * rows].astype(bf16).reshape(H, NEAR, part, half)
    head = got[H * rows : H * rows + fields].astype(bf16).reshape(NEAR, hpart, half)
    tail = copies(scalar_rows(sums, half)[: 8 - hpart], NEAR)
    sent = jnp.concatenate([mix[0], mix[1], head, tail], 1)
    got = jnp.sum(all_to_all(sent, "near").astype(f32), axis=0)
    sums = scalars_of(got[H * part + hpart], fields + 1)
    mix = got[: H * part].astype(bf16).reshape(H, part, half)
    head = got[H * part : H * part + hpart].astype(bf16)
    tail = jnp.concatenate([head, scalar_rows(sums, half)[: 8 - hpart]], 0)
    sent = jnp.concatenate([mix, copies(tail, H)], 1)
    sent = jnp.broadcast_to(sent[:, None], (H, FAR, part + 8, half))
    got = jnp.sum(
        all_to_all(sent.reshape(H * FAR, part + 8, half), ("h", "far")).astype(f32), axis=0
    )
    sums = scalars_of(got[part + hpart], fields + 1)

    got = all_to_all(copies(got.astype(bf16), NEAR * CORES), ("near", "c")).astype(f32)
    got = got.reshape(NEAR, CORES, part + 8, half)
    grad_mix = jnp.concatenate([got[:, 0, :part], got[:, 1, :part]], 2).reshape(rows, width)
    head = got[:, :, part : part + hpart]
    grad_out = jnp.concatenate([head[:, 0], head[:, 1]], 2).reshape(fields, width).T
    loss = sums[fields] / (points * Y * X * H)
    return grad_latents, grad_mix, grad_out, sums[:fields], loss


def solution(mesh):
    shape = (FAR, NEAR, CORES, Y, X, H)
    fine = Mesh(mesh.devices.reshape(shape), ("far", "near", "c", "y", "x", "h"))
    in_specs = (P(ENS, SPACE, None), P(SPACE, None), P(), P(), P(None, SPACE), P(SPACE))
    out_specs = (P(ENS, SPACE, None), P(SPACE, None), P(), P(), P())
    return jax.shard_map(
        body, mesh=fine, in_specs=in_specs, out_specs=out_specs, check_vma=False
    )
```

time: 169 us -> 155 us (0.917)
  blocking collectives: 20 us -> 73.4 us
  waiting for transfers between devices: 59.1 us -> 15.4 us
  starting transfers between devices: 62.2 us -> 42.7 us
  matrix products: 14.1 us -> 11.1 us
    all_to_all x0 -> x3, blocking collectives: none -> 51.4 us  [the longest x1 23.4 us: body(): lax.all_to_all(sent, PLANE, 0, 0, tiled=True).astype(f32)]
    all_to_all x4 -> x2, waiting for transfers between devices: 54.9 us -> 10.6 us  [all_to_all(): return lax.all_to_all(x, axes, 0, 0, tiled=True)]
    all_to_all x4 -> x2, starting transfers between devices: 26.4 us -> 14.8 us  [all_to_all(): return lax.all_to_all(x, axes, 0, 0, tiled=True)]
    ppermute x4 -> x2, starting transfers between devices: 24.8 us -> 18.5 us  [the longest x1 13.3 us: body(): far = lax.ppermute(mine, ('far', 'h'), ACROSS)]
    dot_general x12, matrix products: 14.1 us -> 11.1 us  [dot(): lax.dot_general(a, b, (((ca,), (cb,)), ((), ())), preferred_element_type=...]
    all_to_all x1, blocking collectives: 20 us -> 22 us  [body(): w_own = lax.all_to_all(sent, PLANE, 0, 0, tiled=True).reshape(width, half)]
    ppermute x1, starting transfers between devices: 6.72 us -> 5 us  [body(): w_oth = lax.ppermute(w_own, 'c', SWAP)]
  transfers between devices with their start and end apart: 11 -> 7, of which waited for: 9 -> 6; matrix products, arithmetic and copies ran while one was open for 8% -> 6% of each run, Pallas kernels for 0% -> 0%
where the time goes in v2:
time: 155 us; the launch traced here: 154 us
  blocking collectives  73.4 us (47%)
  starting transfers between devices  42.7 us (28%)
  waiting for transfers between devices  15.4 us (10%)
  matrix products  11.1 us (7%)
  other arithmetic  4.94 us (3%)
  local copies, waits for them, and re-layouts  3.34 us (2%)
  between operations  2.82 us (2%)
    all_to_all x1, blocking collectives, body(): lax.all_to_all(sent, PLANE, 0, 0, tiled=True).astype(f32)  23.4 us
    all_to_all x1, blocking collectives, body(): w_own = lax.all_to_all(sent, PLANE, 0, 0, tiled=True).reshape(width, half)  22 us
    all_to_all x1, blocking collectives, body(): members = lax.all_to_all(sent, RING, 0, 0, tiled=True)  20.9 us
    all_to_all x2, starting transfers between devices, all_to_all(): return lax.all_to_all(x, axes, 0, 0, tiled=True)  14.8 us
    ppermute x1, starting transfers between devices, body(): far = lax.ppermute(mine, ('far', 'h'), ACROSS)  13.3 us
    dot_general x12, matrix products, dot(): lax.dot_general(a, b, (((ca,), (cb,)), ((), ())), preferred_element_type=...  11.1 us
    all_to_all x2, waiting for transfers between devices, all_to_all(): return lax.all_to_all(x, axes, 0, 0, tiled=True)  10.6 us
    all_to_all x1, blocking collectives, all_to_all(): return lax.all_to_all(x, axes, 0, 0, tiled=True)  7.09 us
  transfers between devices with their start and end apart: 7, of which 6 were waited for; matrix products, arithmetic and copies ran while one was open for 6% of the time, Pallas kernels for 0%

profile of v2, /device:TPU:1, one launch (start us, length us, event | category | flops | bytes accessed | tf_op | source)
XLA Modules:
  0.0 153.7 jit_solution(4930086193558808865)
XLA Ops:
  0.7 0.9 slice_select_fusion
  1.5 13.3 %collective-permute-start = (bf16[32,512]{1,0:T(8,128)(2,1)S(1)}, bf16[32,512]{1,0:T(8,128)(2,1)S(1)}, u32[]{:S(2)}, u32[]{:S(2)}) collective-permute-start(bf16[32,512]{1,0:T(8,128)(2,1)S(1)} %slice_select_fusion), channel_id=1, source_target_pairs={{0,257},{1,256},{256,1},{257,0},{2,259},{3,258},{258,3},{259,2},{4... | collective-permute-start | bytes 98312 | tf_op jit(solution)/shard_map/ppermute | solution.py:72
  14.8 1.4 collective-permute-done
  16.3 0.1 broadcast_in_dim.22
  16.4 22.0 %all_to_all.30 = bf16[16,64,512]{2,1,0:T(8,128)(2,1)S(1)} all-to-all(bf16[16,64,512]{2,1,0:T(8,128)(2,1)S(1)} %broadcast_in_dim.22), channel_id=1, replica_groups=mesh['far'=2,'near'=4,'c'=2,'y'=4,'x'=4,'h'=2] {'y','x'}, dimensions={0} | all-to-all | bytes 2097152 | tf_op jit(solution)/shard_map/all_to_all | solution.py:77
  38.4 5.0 %collective-permute-start.1 = (bf16[1024,512]{1,0:T(8,128)(2,1)S(1)}, bf16[1024,512]{1,0:T(8,128)(2,1)S(1)}, u32[]{:S(2)}, u32[]{:S(2)}) collective-permute-start(bf16[1024,512]{1,0:T(8,128)(2,1)S(1)} %bitcast.73), channel_id=1, source_target_pairs={{0,32},{32,0},{1,33},{33,1},{2,34},{34,2},{3,35},{35,3},{4,36},{36... | collective-permute-start | bytes 3145736 | tf_op jit(solution)/shard_map/ppermute | solution.py:78
  43.4 0.9 multiply_convert_fusion.1
  44.4 0.2 fusion.33
  44.5 1.1 collective-permute-done.1
  45.6 0.9 multiply_convert_fusion
  46.6 0.1 fusion.3
  46.9 20.9 %all_to_all.31 = f32[8,16,512]{2,1,0:T(8,128)S(1)} all-to-all(f32[8,16,512]{2,1,0:T(8,128)S(1)} %sub.62), channel_id=1, replica_groups=mesh['far'=2,'near'=4,'c'=2,'y'=4,'x'=4,'h'=2] {'far','near'}, dimensions={0} | all-to-all | bytes 524288 | tf_op jit(solution)/shard_map/all_to_all | solution.py:89
  67.7 5.3 %collective-permute-start.2 = (f32[8,16,512]{2,1,0:T(8,128)S(1)}, f32[8,16,512]{2,1,0:T(8,128)S(1)}, u32[]{:S(2)}, u32[]{:S(2)}) collective-permute-start(f32[8,16,512]{2,1,0:T(8,128)S(1)} %all_to_all.31), channel_id=1, source_target_pairs={{0,32},{32,0},{1,33},{33,1},{2,34},{34,2},{3,35},{35,3},{4,36},{36... | collective-permute-start | bytes 786440 | tf_op jit(solution)/shard_map/ppermute | solution.py:90
  73.0 1.1 collective-permute-done.2
  74.2 0.3 fusion.22
  74.4 0.6 convert_reduce_fusion.3
  75.1 0.2 convolution_convert_fusion.1
  75.3 0.9 fusion.17
  76.2 0.7 reduce-precision_convert_fusion.7
  77.0 0.1 fusion.47
  77.1 2.3 %collective-permute-start.4 = (bf16[24,512]{1,0:T(8,128)(2,1)S(1)}, bf16[24,512]{1,0:T(8,128)(2,1)S(1)}, u32[]{:S(2)}, u32[]{:S(2)}) collective-permute-start(bf16[24,512]{1,0:T(8,128)(2,1)S(1)} %fusion.31), channel_id=1, source_target_pairs={{0,32},{32,0},{1,33},{33,1},{2,34},{34,2},{3,35},{35,3},{4,36},{36... | collective-permute-start | bytes 73736 | tf_op jit(solution)/shard_map/ppermute | solution.py:114
  79.3 0.7 fusion.2
  80.1 2.0 %collective-permute-start.3 = (bf16[1024,512]{0,1:T(8,128)(2,1)S(1)}, bf16[1024,512]{0,1:T(8,128)(2,1)S(1)}, u32[]{:S(2)}, u32[]{:S(2)}) collective-permute-start(bf16[1024,512]{0,1:T(8,128)(2,1)S(1)} %fusion.2), channel_id=1, source_target_pairs={{0,32},{32,0},{1,33},{33,1},{2,34},{34,2},{3,35},{35,3},{4,36},{36... | collective-permute-start | bytes 3145736 | tf_op jit(solution)/shard_map/ppermute | solution.py:110
  82.1 0.9 fusion.10
  83.0 0.1 reduce-precision_convert_fusion.5
  83.1 0.1 fusion.49
  83.2 0.2 fusion.30
  83.5 1.1 collective-permute-done.3
  84.6 0.7 fusion
  85.3 0.5 copy.25
  85.9 0.1 pad_maximum_fusion
  86.1 23.4 %all_to_all.32 = bf16[16,88,512]{2,1,0:T(8,128)(2,1)S(1)} all-to-all(bf16[16,88,512]{2,1,0:T(8,128)(2,1)S(1)} %pad_maximum_fusion), channel_id=1, replica_groups=mesh['far'=2,'near'=4,'c'=2,'y'=4,'x'=4,'h'=2] {'y','x'}, dimensions={0} | all-to-all | bytes 2883584 | tf_op jit(solution)/shard_map/all_to_all | solution.py:130
  109.5 0.2 convert_reduce_fusion
  109.9 0.1 fusion.51
  110.0 7.1 %all_to_all.33 = bf16[4,24,512]{2,1,0:T(8,128)(2,1)S(1)} all-to-all(bf16[4,24,512]{2,1,0:T(8,128)(2,1)S(1)} %pad_maximum_fusion.2), channel_id=1, replica_groups=mesh['far'=2,'near'=4,'c'=2,'y'=4,'x'=4,'h'=2] {'near'}, dimensions={0} | all-to-all | bytes 196608 | tf_op jit(solution)/shard_map/all_to_all | solution.py:42
  117.2 0.1 fusion.53
  117.4 0.6 broadcast_in_dim.31
  118.0 7.4 %all-to-all-start.4 = ((bf16[4,16,512]{2,1,0:T(8,128)(2,1)}), bf16[4,16,512]{2,1,0:T(8,128)(2,1)S(1)}, u32[]{:S(2)}, u32[]{:S(2)}) async-start(bf16[4,16,512]{2,1,0:T(8,128)(2,1)} %bitcast.15), calls=%async_computation.4 | async-start | bytes 131072 | tf_op jit(solution)/shard_map/all_to_all | solution.py:42
  125.4 2.1 %fusion.66 = f32[512,1024]{1,0:T(8,128)S(1)} fusion(bf16[512,512]{0,1:T(8,128)(2,1)} %copy-done.4, bf16[1024,512]{1,0:T(8,128)(2,1)} %bitcast.75), kind=kOutput, calls=%fused_computation.131 | convolution fusion | flops 536870912 | bytes 3670016 | tf_op jit(solution)/shard_map/dot_general | solution.py:50
  127.5 9.7 %all-to-all-done.4 = bf16[4,16,512]{2,1,0:T(8,128)(2,1)S(1)} async-done(((bf16[4,16,512]{2,1,0:T(8,128)(2,1)}), bf16[4,16,512]{2,1,0:T(8,128)(2,1)S(1)}, u32[]{:S(2)}, u32[]{:S(2)}) %all-to-all-start.4) | async-done | bytes 65568 | tf_op jit(solution)/shard_map/all_to_all | solution.py:42
  137.3 0.7 broadcast_in_dim.32
  137.9 7.4 %all-to-all-start.5 = ((bf16[8,16,512]{2,1,0:T(8,128)(2,1)}), bf16[8,16,512]{2,1,0:T(8,128)(2,1)S(1)}, u32[]{:S(2)}, u32[]{:S(2)}) async-start(bf16[8,16,512]{2,1,0:T(8,128)(2,1)} %broadcast_in_dim.32), calls=%async_computation.5 | async-start | bytes 262144 | tf_op jit(solution)/shard_map/all_to_all | solution.py:42
  145.4 3.1 %fusion.1 = bf16[1,512,1024]{2,1,0:T(8,128)(2,1)} fusion(f32[512,1024]{1,0:T(8,128)S(1)} %fusion.66, bf16[512,512]{0,1:T(8,128)(2,1)} %copy-done.3, bf16[1024,512]{1,0:T(8,128)(2,1)} %copy-done.2), kind=kOutput, calls=%fused_computation.10 | convolution fusion | flops 537919488 | bytes 4718592 | tf_op jit(solution)/shard_map/dot_general | solution.py:50
  148.5 0.6 slice.166
  149.8 0.5 slice_bitcast_fusion.5
  150.3 0.9 all-to-all-done.5
  151.3 0.6 maximum_bitcast_fusion
  151.9 0.7 pad_maximum_fusion.1
  (58 shorter events, 0.7 us)
Async XLA Ops:
  0.6 42.8 %copy-start = (bf16[1,512,1024]{2,1,0:T(8,128)(2,1)S(1)}, bf16[1,512,1024]{2,1,0:T(8,128)(2,1)}, u32[]{:S(2)}) copy-start(bf16[1,512,1024]{2,1,0:T(8,128)(2,1)} %param.6) | copy-start | bytes 3145732
  1.5 14.7 %collective-permute-start = (bf16[32,512]{1,0:T(8,128)(2,1)S(1)}, bf16[32,512]{1,0:T(8,128)(2,1)S(1)}, u32[]{:S(2)}, u32[]{:S(2)}) collective-permute-start(bf16[32,512]{1,0:T(8,128)(2,1)S(1)} %slice_select_fusion), channel_id=1, source_target_pairs={{0,257},{1,256},{256,1},{257,0},{2,259},{3,258},{258,3},{259,2},{4... | collective-permute-start | bytes 98312 | tf_op jit(solution)/shard_map/ppermute | solution.py:72
  38.4 6.0 %copy-start.1 = (bf16[16,64,512]{2,1,0:T(8,128)(2,1)}, bf16[16,64,512]{2,1,0:T(8,128)(2,1)S(1)}, u32[]{:S(2)}) copy-start(bf16[16,64,512]{2,1,0:T(8,128)(2,1)S(1)} %all_to_all.30) | copy-start | bytes 3145732
  38.4 6.0 %copy-start.6 = (bf16[1024,16]{0,1:T(8,128)(2,1)S(1)}, bf16[1024,16]{0,1:T(8,128)(2,1)}, u32[]{:S(2)}) copy-start(bf16[1024,16]{0,1:T(8,128)(2,1)} %param.8) | copy-start | bytes 98308
  38.4 7.3 %collective-permute-start.1 = (bf16[1024,512]{1,0:T(8,128)(2,1)S(1)}, bf16[1024,512]{1,0:T(8,128)(2,1)S(1)}, u32[]{:S(2)}, u32[]{:S(2)}) collective-permute-start(bf16[1024,512]{1,0:T(8,128)(2,1)S(1)} %bitcast.73), channel_id=1, source_target_pairs={{0,32},{32,0},{1,33},{33,1},{2,34},{34,2},{3,35},{35,3},{4,36},{36... | collective-permute-start | bytes 3145736 | tf_op jit(solution)/shard_map/ppermute | solution.py:78
  44.5 2.1 %copy-start.8 = (f32[16]{0:T(128)S(1)}, f32[16]{0:T(128)}, u32[]{:S(2)}) copy-start(f32[16]{0:T(128)} %param.9) | copy-start | bytes 196
  45.6 1.0 copy-start.2
  46.6 27.8 %copy-start.5 = (f32[16,512]{1,0:T(8,128)S(1)}, f32[16,512]{1,0:T(8,128)}, u32[]{:S(2)}) copy-start(f32[16,512]{1,0:T(8,128)} %param.10) | copy-start | bytes 98308
  46.6 27.8 %copy-start.7 = (f32[512]{0:T(512)S(1)}, f32[512]{0:T(512)}, u32[]{:S(2)}) copy-start(f32[512]{0:T(512)} %param.11) | copy-start | bytes 6148
  67.7 6.4 %collective-permute-start.2 = (f32[8,16,512]{2,1,0:T(8,128)S(1)}, f32[8,16,512]{2,1,0:T(8,128)S(1)}, u32[]{:S(2)}, u32[]{:S(2)}) collective-permute-start(f32[8,16,512]{2,1,0:T(8,128)S(1)} %all_to_all.31), channel_id=1, source_target_pairs={{0,32},{32,0},{1,33},{33,1},{2,34},{34,2},{3,35},{35,3},{4,36},{36... | collective-permute-start | bytes 786440 | tf_op jit(solution)/shard_map/ppermute | solution.py:90
  76.2 6.8 %copy-start.3 = (bf16[512,512]{0,1:T(8,128)(2,1)}, bf16[512,512]{0,1:T(8,128)(2,1)S(1)}, u32[]{:S(2)}) copy-start(bf16[512,512]{0,1:T(8,128)(2,1)S(1)} %fusion.17) | copy-start | bytes 1572868
  77.1 6.0 %collective-permute-start.4 = (bf16[24,512]{1,0:T(8,128)(2,1)S(1)}, bf16[24,512]{1,0:T(8,128)(2,1)S(1)}, u32[]{:S(2)}, u32[]{:S(2)}) collective-permute-start(bf16[24,512]{1,0:T(8,128)(2,1)S(1)} %fusion.31), channel_id=1, source_target_pairs={{0,32},{32,0},{1,33},{33,1},{2,34},{34,2},{3,35},{35,3},{4,36},{36... | collective-permute-start | bytes 73736 | tf_op jit(solution)/shard_map/ppermute | solution.py:114
  80.1 4.6 %collective-permute-start.3 = (bf16[1024,512]{0,1:T(8,128)(2,1)S(1)}, bf16[1024,512]{0,1:T(8,128)(2,1)S(1)}, u32[]{:S(2)}, u32[]{:S(2)}) collective-permute-start(bf16[1024,512]{0,1:T(8,128)(2,1)S(1)} %fusion.2), channel_id=1, source_target_pairs={{0,32},{32,0},{1,33},{33,1},{2,34},{34,2},{3,35},{35,3},{4,36},{36... | collective-permute-start | bytes 3145736 | tf_op jit(solution)/shard_map/ppermute | solution.py:110
  83.0 1.6 %copy-start.4 = (bf16[512,512]{0,1:T(8,128)(2,1)}, bf16[512,512]{0,1:T(8,128)(2,1)S(1)}, u32[]{:S(2)}) copy-start(bf16[512,512]{0,1:T(8,128)(2,1)S(1)} %fusion.10) | copy-start | bytes 1572868
  118.0 19.3 %all-to-all-start.4 = ((bf16[4,16,512]{2,1,0:T(8,128)(2,1)}), bf16[4,16,512]{2,1,0:T(8,128)(2,1)S(1)}, u32[]{:S(2)}, u32[]{:S(2)}) async-start(bf16[4,16,512]{2,1,0:T(8,128)(2,1)} %bitcast.15), calls=%async_computation.4 | async-start | bytes 131072 | tf_op jit(solution)/shard_map/all_to_all | solution.py:42
  137.9 13.2 %all-to-all-start.5 = ((bf16[8,16,512]{2,1,0:T(8,128)(2,1)}), bf16[8,16,512]{2,1,0:T(8,128)(2,1)S(1)}, u32[]{:S(2)}, u32[]{:S(2)}) async-start(bf16[8,16,512]{2,1,0:T(8,128)(2,1)} %broadcast_in_dim.32), calls=%async_computation.5 | async-start | bytes 262144 | tf_op jit(solution)/shard_map/all_to_all | solution.py:42

commit v3 on v2

v3 whole, which is shorter than its diff:
```python
import jax
import jax.numpy as jnp
from jax import lax
from jax.sharding import Mesh
from jax.sharding import PartitionSpec as P

M = 16
smoothing = 0.1
FAR, NEAR, CORES, Y, X, H = 2, 4, 2, 4, 4, 2
Z = FAR * NEAR
RING = ("far", "near")
ENS, SPACE, PLANE = ("far", "near", "c"), ("y", "x", "h"), ("y", "x")
f32, bf16 = jnp.float32, jnp.bfloat16
SWAP = ((0, 1), (1, 0))
ACROSS = tuple((far * H + h, (1 - far) * H + 1 - h) for far in range(FAR) for h in range(H))


def scalar_rows(values, width, count):
    first = lax.reduce_precision(values, 8, 7)
    second = lax.reduce_precision(values - first, 8, 7)
    third = values - first - second
    terms = jnp.concatenate([first, second, third]).astype(bf16)
    return jnp.pad(terms[None], ((0, count - 1), (0, width - terms.shape[0])))


def scalars_of(row, count):
    return row[:count] + row[count : 2 * count] + row[2 * count : 3 * count]


def member_sums(chosen, members):
    differ = chosen[None] - members
    smooth = jnp.sqrt(differ * differ + smoothing * smoothing)
    return jnp.sum(differ / smooth, axis=0), jnp.sum(smooth, axis=0)


def pairwise(chosen, members, others, observed, weights):
    slope, smooth = member_sums(chosen, members)
    slope_oth, smooth_oth = member_sums(chosen, others)
    slope, smooth = slope + slope_oth, smooth + smooth_oth
    count_all = float(M)
    pairs_norm = count_all * (count_all - 1.0)
    to_truth = chosen - observed
    absolute = jnp.sqrt(to_truth * to_truth + smoothing * smoothing)
    gradient = weights * (to_truth / absolute / count_all - slope / pairs_norm)
    partial = jnp.sum(
        weights * (absolute / count_all - (smooth - smoothing) / (2.0 * pairs_norm))
    )
    return gradient.astype(bf16), partial


def all_to_all(x, axes):
    return lax.all_to_all(x, axes, 0, 0, tiled=True)


def copies(x, count):
    return jnp.broadcast_to(x[None], (count,) + x.shape)


def dot(a, b, ca, cb):
    return lax.dot_general(a, b, (((ca,), (cb,)), ((), ())), preferred_element_type=f32)


def body(latents, w_mix, w_out, bias, truth, area):
    first = lax.axis_index("c") == 0
    low = lax.axis_index("h") == 0
    points, width = latents.shape[1], latents.shape[2]
    fields = w_out.shape[1]
    rows = w_mix.shape[0]
    half = width // 2

    def pick(a, b):
        return jnp.where(first, a, b)

    mine = pick(w_mix[:, :half], w_mix[:, half:])
    far = lax.ppermute(mine, ("far", "h"), ACROSS)
    near = jnp.where(low, jnp.concatenate([mine, far], 0), jnp.concatenate([far, mine], 0))
    w_own = all_to_all(copies(near, Y * X), PLANE).reshape(width, half)
    out_own = pick(w_out[:half], w_out[half:])

    lat_own = latents[0]
    lat_oth = lax.ppermute(lat_own, "c", SWAP)
    pre_own = dot(lat_own, w_own, 1, 0)
    hid_own = jax.nn.gelu(pre_own).astype(bf16)
    pre_oth = dot(lat_oth, w_own, 1, 0)
    hid_oth = jax.nn.gelu(pre_oth).astype(bf16)
    fc_own, fc_oth = dot(out_own, hid_own, 0, 1), dot(out_own, hid_oth, 0, 1)

    rest = lax.ppermute(jnp.stack([fc_oth, fc_own]), "c", SWAP)
    fc_own = fc_own + rest[0] + bias[:, None]
    fc_oth = fc_oth + rest[1] + bias[:, None]
    members = all_to_all(copies(fc_own, Z), RING)
    others = lax.ppermute(members, "c", SWAP)
    g_own, partial = pairwise(fc_own, members, others, truth, area)
    g_oth, unused_partial = pairwise(fc_oth, members, others, truth, area)
    sums = jnp.concatenate([jnp.sum(g_own.astype(f32), axis=1), partial.reshape(1)])

    def backward(pre, g):
        unused_value, pullback = jax.vjp(jax.nn.gelu, pre)
        return pullback(dot(g, out_own, 0, 1))[0].astype(bf16)

    gp_own, gp_oth = backward(pre_own, g_own), backward(pre_oth, g_oth)
    mix = (dot(lat_own, gp_own, 0, 0) + dot(lat_oth, gp_oth, 0, 0)).astype(bf16)
    head = dot(g_own, hid_own, 1, 0) + dot(g_oth, hid_oth, 1, 0)

    extra = jnp.concatenate([head.astype(bf16), scalar_rows(sums, half, 8)], 0)
    sent = jnp.concatenate([mix.reshape(Y * X, H * rows, half), copies(extra, Y * X)], 1)
    got = jnp.sum(all_to_all(sent, PLANE).astype(f32), axis=0)

    piece, hpiece = rows // NEAR, fields // NEAR
    sums = scalars_of(got[H * rows + fields], fields + 1)
    mix = got[: H * rows].astype(bf16).reshape(H, NEAR, piece, half)
    head = got[H * rows : H * rows + fields].astype(bf16).reshape(NEAR, hpiece, half)
    tail = copies(scalar_rows(sums, half, 8 - hpiece), NEAR)
    sent = jnp.concatenate([mix[0], mix[1], head, tail], 1)
    got = jnp.sum(all_to_all(sent, "near").astype(f32), axis=0)
    sums = scalars_of(got[H * piece + hpiece], fields + 1)
    mix = got[: H * piece].astype(bf16).reshape(H, piece, half)
    head = got[H * piece : H * piece + hpiece].astype(bf16)
    tail = jnp.concatenate([head, scalar_rows(sums, half, 8 - hpiece)], 0)
    sent = jnp.concatenate([mix, copies(tail, H)], 1)
    sent = jnp.broadcast_to(sent[:, None], (H, FAR, piece + 8, half))
    sent = sent.reshape(H * FAR, piece + 8, half)
    got = jnp.sum(all_to_all(sent, ("h", "far")).astype(f32), axis=0)

    sums = scalars_of(got[piece + hpiece], fields + 1)
    sent = jnp.concatenate(
        [got[: piece + hpiece].astype(bf16), scalar_rows(sums, half, 8 - hpiece)], 0
    )
    got = all_to_all(copies(sent, NEAR * CORES), ("near", "c")).astype(f32)
    got = got.reshape(NEAR, CORES, piece + 8, half)
    grad_mix = jnp.concatenate([got[:, 0, :piece], got[:, 1, :piece]], 2).reshape(rows, width)
    head = got[:, :, piece : piece + hpiece]
    grad_out = jnp.concatenate([head[:, 0], head[:, 1]], 2).reshape(fields, width).T
    sums = scalars_of(got[0, 0, piece + hpiece] + got[0, 1, piece + hpiece], fields + 1)
    loss = sums[fields] / (points * Y * X * H)

    grad_rows = lax.ppermute(dot(gp_oth, w_own, 1, 1).astype(bf16), "c", SWAP)
    grad_latents = (dot(gp_own, w_own, 1, 1) + grad_rows.astype(f32)).astype(bf16)[None]
    return grad_latents, grad_mix, grad_out, sums[:fields], loss


def solution(mesh):
    shape = (FAR, NEAR, CORES, Y, X, H)
    fine = Mesh(mesh.devices.reshape(shape), ("far", "near", "c", "y", "x", "h"))
    in_specs = (P(ENS, SPACE, None), P(SPACE, None), P(), P(), P(None, SPACE), P(SPACE))
    out_specs = (P(ENS, SPACE, None), P(SPACE, None), P(), P(), P())
    return jax.shard_map(
        body, mesh=fine, in_specs=in_specs, out_specs=out_specs, check_vma=False
    )
```

time: 155 us -> 152 us (0.981)
  blocking collectives: 73.4 us -> 51.6 us
  starting transfers between devices: 42.7 us -> 54.9 us
  waiting for transfers between devices: 15.4 us -> 23.2 us
  matrix products: 11.1 us -> 9.35 us
    all_to_all x3 -> x0, blocking collectives: 66.3 us -> none  [the longest x1 23.4 us: body(): lax.all_to_all(sent, PLANE, 0, 0, tiled=True).astype(f32)]
    all_to_all x1 -> x3, blocking collectives: 7.09 us -> 51.6 us  [all_to_all(): return lax.all_to_all(x, axes, 0, 0, tiled=True)]
    all_to_all x2 -> x3, waiting for transfers between devices: 10.6 us -> 19.7 us  [all_to_all(): return lax.all_to_all(x, axes, 0, 0, tiled=True)]
    all_to_all x2 -> x3, starting transfers between devices: 14.8 us -> 21.5 us  [all_to_all(): return lax.all_to_all(x, axes, 0, 0, tiled=True)]
    ppermute x3, starting transfers between devices: 9.32 us -> 14.9 us  [the longest x1 5.41 us: body(): rest = lax.ppermute(jnp.stack([fc_oth, fc_own]), 'c', SWAP)]
    dot_general x12, matrix products: 11.1 us -> 9.35 us  [dot(): lax.dot_general(a, b, (((ca,), (cb,)), ((), ())), preferred_element_type=...]
  transfers between devices with their start and end apart: 7 -> 8, of which waited for: 6 -> 6; matrix products, arithmetic and copies ran while one was open for 6% -> 4% of each run, Pallas kernels for 0% -> 0%
where the time goes in v3:
time: 152 us; the launch traced here: 151 us
  starting transfers between devices  54.9 us (36%)
  blocking collectives  51.6 us (34%)
  waiting for transfers between devices  23.2 us (15%)
  matrix products  9.35 us (6%)
  other arithmetic  5.36 us (4%)
  local copies, waits for them, and re-layouts  4.24 us (3%)
  between operations  2.81 us (2%)
    all_to_all x3, blocking collectives, all_to_all(): return lax.all_to_all(x, axes, 0, 0, tiled=True)  51.6 us
    all_to_all x3, starting transfers between devices, all_to_all(): return lax.all_to_all(x, axes, 0, 0, tiled=True)  21.5 us
    all_to_all x3, waiting for transfers between devices, all_to_all(): return lax.all_to_all(x, axes, 0, 0, tiled=True)  19.7 us
    ppermute x1, starting transfers between devices, body(): far = lax.ppermute(mine, ('far', 'h'), ACROSS)  13.3 us
    dot_general x12, matrix products, dot(): lax.dot_general(a, b, (((ca,), (cb,)), ((), ())), preferred_element_type=...  9.35 us
    ppermute x1, starting transfers between devices, body(): rest = lax.ppermute(jnp.stack([fc_oth, fc_own]), 'c', SWAP)  5.41 us
    ppermute x1, starting transfers between devices, body(): others = lax.ppermute(members, 'c', SWAP)  5.25 us
    ppermute x1, starting transfers between devices, body(): grad_rows = lax.ppermute(dot(gp_oth, w_own, 1, 1).astype(bf16), 'c', SWAP)  5.14 us
  transfers between devices with their start and end apart: 8, of which 6 were waited for; matrix products, arithmetic and copies ran while one was open for 4% of the time, Pallas kernels for 0%

profile of v3, /device:TPU:1, one launch (start us, length us, event | category | flops | bytes accessed | tf_op | source)
XLA Modules:
  0.0 151.3 jit_solution(9601658741181366073)
XLA Ops:
  0.7 0.9 slice_select_fusion
  1.5 13.3 %collective-permute-start = (bf16[32,512]{1,0:T(8,128)(2,1)S(1)}, bf16[32,512]{1,0:T(8,128)(2,1)S(1)}, u32[]{:S(2)}, u32[]{:S(2)}) collective-permute-start(bf16[32,512]{1,0:T(8,128)(2,1)S(1)} %slice_select_fusion), channel_id=1, source_target_pairs={{0,257},{1,256},{256,1},{257,0},{2,259},{3,258},{258,3},{259,2},{4... | collective-permute-start | bytes 98312 | tf_op jit(solution)/shard_map/ppermute | solution.py:75
  14.8 1.4 collective-permute-done
  16.3 1.1 broadcast_in_dim.14
  17.3 6.8 %all-to-all-start = ((bf16[16,64,512]{2,1,0:T(8,128)(2,1)}), bf16[16,64,512]{2,1,0:T(8,128)(2,1)S(1)}, u32[]{:S(2)}, u32[]{:S(2)}) async-start(bf16[16,64,512]{2,1,0:T(8,128)(2,1)} %broadcast_in_dim.14), calls=%async_computation | async-start | bytes 2097152 | tf_op jit(solution)/shard_map/all_to_all | solution.py:52
  24.1 4.3 %collective-permute-start.1 = (bf16[512,1024]{1,0:T(8,128)(2,1)S(1)}, bf16[512,1024]{1,0:T(8,128)(2,1)S(1)}, u32[]{:S(2)}, u32[]{:S(2)}) collective-permute-start(bf16[512,1024]{1,0:T(8,128)(2,1)S(1)} %bitcast.79), channel_id=1, source_target_pairs={{0,32},{32,0},{1,33},{33,1},{2,34},{34,2},{3,35},{35,3},{4,36},{36... | collective-permute-start | bytes 3145736 | tf_op jit(solution)/shard_map/ppermute | solution.py:81
  28.5 10.6 %all-to-all-done = bf16[16,64,512]{2,1,0:T(8,128)(2,1)S(1)} async-done(((bf16[16,64,512]{2,1,0:T(8,128)(2,1)}), bf16[16,64,512]{2,1,0:T(8,128)(2,1)S(1)}, u32[]{:S(2)}, u32[]{:S(2)}) %all-to-all-start) | async-done | bytes 1048608 | tf_op jit(solution)/shard_map/all_to_all | solution.py:52
  39.1 0.9 multiply_convert_fusion.1
  40.0 0.2 fusion.72
  40.2 0.9 multiply_convert_fusion
  41.2 0.2 fusion.73
  41.4 5.4 %collective-permute-start.2 = (f32[2,16,512]{2,1,0:T(8,128)S(1)}, f32[2,16,512]{2,1,0:T(8,128)S(1)}, u32[]{:S(2)}, u32[]{:S(2)}) collective-permute-start(f32[2,16,512]{2,1,0:T(8,128)S(1)} %pad_maximum_fusion.3), channel_id=1, source_target_pairs={{0,32},{32,0},{1,33},{33,1},{2,34},{34,2},{3,35},{35,3},{4,36},{36... | collective-permute-start | bytes 196616 | tf_op jit(solution)/shard_map/ppermute | solution.py:88
  46.8 0.9 collective-permute-done.2
  47.8 20.9 %all_to_all.30 = f32[8,16,512]{2,1,0:T(8,128)S(1)} all-to-all(f32[8,16,512]{2,1,0:T(8,128)S(1)} %sub.109), channel_id=1, replica_groups=mesh['far'=2,'near'=4,'c'=2,'y'=4,'x'=4,'h'=2] {'far','near'}, dimensions={0} | all-to-all | bytes 524288 | tf_op jit(solution)/shard_map/all_to_all | solution.py:52
  68.8 5.3 %collective-permute-start.3 = (f32[8,16,512]{2,1,0:T(8,128)S(1)}, f32[8,16,512]{2,1,0:T(8,128)S(1)}, u32[]{:S(2)}, u32[]{:S(2)}) collective-permute-start(f32[8,16,512]{2,1,0:T(8,128)S(1)} %all_to_all.30), channel_id=1, source_target_pairs={{0,32},{32,0},{1,33},{33,1},{2,34},{34,2},{3,35},{35,3},{4,36},{36... | collective-permute-start | bytes 786440 | tf_op jit(solution)/shard_map/ppermute | solution.py:92
  74.0 1.1 collective-permute-done.3
  75.2 0.4 fusion.19
  75.5 0.6 convert_reduce_fusion.3
  76.2 0.2 fusion.74
  76.4 0.9 fusion.8
  77.3 0.9 fusion.15
  78.2 0.2 fusion.1
  78.5 1.0 fusion.61
  79.4 0.7 fusion.68
  80.2 0.7 fusion
  80.9 0.5 copy.25
  81.5 0.1 fusion.35
  81.6 0.1 pad_maximum_fusion
  81.7 23.5 %all_to_all.31 = bf16[16,88,512]{2,1,0:T(8,128)(2,1)S(1)} all-to-all(bf16[16,88,512]{2,1,0:T(8,128)(2,1)S(1)} %pad_maximum_fusion), channel_id=1, replica_groups=mesh['far'=2,'near'=4,'c'=2,'y'=4,'x'=4,'h'=2] {'y','x'}, dimensions={0} | all-to-all | bytes 2883584 | tf_op jit(solution)/shard_map/all_to_all | solution.py:52
  105.2 0.2 convert_reduce_fusion
  105.4 0.1 reduce-precision_convert_fusion.5
  105.6 0.1 fusion.48
  105.7 7.1 %all_to_all.32 = bf16[4,24,512]{2,1,0:T(8,128)(2,1)S(1)} all-to-all(bf16[4,24,512]{2,1,0:T(8,128)(2,1)S(1)} %pad_maximum_fusion.2), channel_id=1, replica_groups=mesh['far'=2,'near'=4,'c'=2,'y'=4,'x'=4,'h'=2] {'near'}, dimensions={0} | all-to-all | bytes 196608 | tf_op jit(solution)/shard_map/all_to_all | solution.py:52
  112.9 0.1 fusion.53
  113.0 0.6 broadcast_in_dim.19
  113.7 7.2 %all-to-all-start.4 = ((bf16[4,16,512]{2,1,0:T(8,128)(2,1)}), bf16[4,16,512]{2,1,0:T(8,128)(2,1)S(1)}, u32[]{:S(2)}, u32[]{:S(2)}) async-start(bf16[4,16,512]{2,1,0:T(8,128)(2,1)} %bitcast.18), calls=%async_computation.4 | async-start | bytes 131072 | tf_op jit(solution)/shard_map/all_to_all | solution.py:52
  120.9 1.7 %convolution_convert_fusion = bf16[512,1024]{1,0:T(8,128)(2,1)} fusion(bf16[512,512]{0,1:T(8,128)(2,1)S(1)} %copy-done.6, bf16[1024,512]{1,0:T(8,128)(2,1)S(1)} %bitcast.82), kind=kOutput, calls=%fused_computation.7 | convolution fusion | flops 537395200 | bytes 2621440 | tf_op jit(solution)/shard_map/dot_general | solution.py:60
  122.6 5.1 %collective-permute-start.4 = (bf16[512,1024]{1,0:T(8,128)(2,1)}, bf16[512,1024]{1,0:T(8,128)(2,1)S(1)}, u32[]{:S(2)}, u32[]{:S(2)}) collective-permute-start(bf16[512,1024]{1,0:T(8,128)(2,1)} %convolution_convert_fusion), channel_id=1, source_target_pairs={{0,32},{32,0},{1,33},{33,1},{2,34},{34,2},{3,35},{35,3},{4,36},{36... | collective-permute-start | bytes 3145736 | tf_op jit(solution)/shard_map/ppermute | solution.py:137
  127.8 5.0 %all-to-all-done.4 = bf16[4,16,512]{2,1,0:T(8,128)(2,1)S(1)} async-done(((bf16[4,16,512]{2,1,0:T(8,128)(2,1)}), bf16[4,16,512]{2,1,0:T(8,128)(2,1)S(1)}, u32[]{:S(2)}, u32[]{:S(2)}) %all-to-all-start.4) | async-done | bytes 65568 | tf_op jit(solution)/shard_map/all_to_all | solution.py:52
  132.9 0.1 fusion.58
  133.0 0.7 broadcast_in_dim.20
  133.6 7.5 %all-to-all-start.5 = ((bf16[8,16,512]{2,1,0:T(8,128)(2,1)}), bf16[8,16,512]{2,1,0:T(8,128)(2,1)S(1)}, u32[]{:S(2)}, u32[]{:S(2)}) async-start(bf16[8,16,512]{2,1,0:T(8,128)(2,1)} %broadcast_in_dim.20), calls=%async_computation.5 | async-start | bytes 262144 | tf_op jit(solution)/shard_map/all_to_all | solution.py:52
  141.1 1.7 %fusion.16 = bf16[1,512,1024]{2,1,0:T(8,128)(2,1)} fusion(bf16[512,1024]{1,0:T(8,128)(2,1)S(1)} %collective-permute-done.4, bf16[512,512]{0,1:T(8,128)(2,1)S(1)} %copy-done.4, bf16[1024,512]{1,0:T(8,128)(2,1)S(1)} %bitcast.83), kind=kOutput, calls=%fused_computation.28 | convolution fusion | flops 538443776 | bytes 3670016 | tf_op jit(solution)/shard_map/dot_general | solution.py:60
  142.9 4.1 %all-to-all-done.5 = bf16[8,16,512]{2,1,0:T(8,128)(2,1)S(1)} async-done(((bf16[8,16,512]{2,1,0:T(8,128)(2,1)}), bf16[8,16,512]{2,1,0:T(8,128)(2,1)S(1)}, u32[]{:S(2)}, u32[]{:S(2)}) %all-to-all-start.5) | async-done | bytes 131104 | tf_op jit(solution)/shard_map/all_to_all | solution.py:52
  147.1 0.6 slice.169
  147.7 0.5 slice_bitcast_fusion.7
  148.3 0.6 maximum_bitcast_fusion
  149.5 0.7 pad_maximum_fusion.1
  (60 shorter events, 0.7 us)
Async XLA Ops:
  0.6 23.5 %copy-start = (bf16[1,512,1024]{2,1,0:T(8,128)(2,1)S(1)}, bf16[1,512,1024]{2,1,0:T(8,128)(2,1)}, u32[]{:S(2)}) copy-start(bf16[1,512,1024]{2,1,0:T(8,128)(2,1)} %param.6) | copy-start | bytes 3145732
  0.6 27.8 %copy-start.8 = (bf16[1024,16]{0,1:T(8,128)(2,1)S(1)}, bf16[1024,16]{0,1:T(8,128)(2,1)}, u32[]{:S(2)}) copy-start(bf16[1024,16]{0,1:T(8,128)(2,1)} %param.8) | copy-start | bytes 98308
  1.5 14.7 %collective-permute-start = (bf16[32,512]{1,0:T(8,128)(2,1)S(1)}, bf16[32,512]{1,0:T(8,128)(2,1)S(1)}, u32[]{:S(2)}, u32[]{:S(2)}) collective-permute-start(bf16[32,512]{1,0:T(8,128)(2,1)S(1)} %slice_select_fusion), channel_id=1, source_target_pairs={{0,257},{1,256},{256,1},{257,0},{2,259},{3,258},{258,3},{259,2},{4... | collective-permute-start | bytes 98312 | tf_op jit(solution)/shard_map/ppermute | solution.py:75
  17.3 21.8 %all-to-all-start = ((bf16[16,64,512]{2,1,0:T(8,128)(2,1)}), bf16[16,64,512]{2,1,0:T(8,128)(2,1)S(1)}, u32[]{:S(2)}, u32[]{:S(2)}) async-start(bf16[16,64,512]{2,1,0:T(8,128)(2,1)} %broadcast_in_dim.14), calls=%async_computation | async-start | bytes 2097152 | tf_op jit(solution)/shard_map/all_to_all | solution.py:52
  24.1 16.1 %collective-permute-start.1 = (bf16[512,1024]{1,0:T(8,128)(2,1)S(1)}, bf16[512,1024]{1,0:T(8,128)(2,1)S(1)}, u32[]{:S(2)}, u32[]{:S(2)}) collective-permute-start(bf16[512,1024]{1,0:T(8,128)(2,1)S(1)} %bitcast.79), channel_id=1, source_target_pairs={{0,32},{32,0},{1,33},{33,1},{2,34},{34,2},{3,35},{35,3},{4,36},{36... | collective-permute-start | bytes 3145736 | tf_op jit(solution)/shard_map/ppermute | solution.py:81
  40.2 7.5 %copy-start.10 = (f32[16]{0:T(128)S(1)}, f32[16]{0:T(128)}, u32[]{:S(2)}) copy-start(f32[16]{0:T(128)} %param.9) | copy-start | bytes 196
  40.2 1.0 copy-start.1
  41.2 34.3 %copy-start.7 = (f32[16,512]{1,0:T(8,128)S(1)}, f32[16,512]{1,0:T(8,128)}, u32[]{:S(2)}) copy-start(f32[16,512]{1,0:T(8,128)} %param.10) | copy-start | bytes 98308
  41.2 34.3 %copy-start.9 = (f32[512]{0:T(512)S(1)}, f32[512]{0:T(512)}, u32[]{:S(2)}) copy-start(f32[512]{0:T(512)} %param.11) | copy-start | bytes 6148
  41.4 6.3 %collective-permute-start.2 = (f32[2,16,512]{2,1,0:T(8,128)S(1)}, f32[2,16,512]{2,1,0:T(8,128)S(1)}, u32[]{:S(2)}, u32[]{:S(2)}) collective-permute-start(f32[2,16,512]{2,1,0:T(8,128)S(1)} %pad_maximum_fusion.3), channel_id=1, source_target_pairs={{0,32},{32,0},{1,33},{33,1},{2,34},{34,2},{3,35},{35,3},{4,36},{36... | collective-permute-start | bytes 196616 | tf_op jit(solution)/shard_map/ppermute | solution.py:88
  68.8 6.4 %collective-permute-start.3 = (f32[8,16,512]{2,1,0:T(8,128)S(1)}, f32[8,16,512]{2,1,0:T(8,128)S(1)}, u32[]{:S(2)}, u32[]{:S(2)}) collective-permute-start(f32[8,16,512]{2,1,0:T(8,128)S(1)} %all_to_all.30), channel_id=1, source_target_pairs={{0,32},{32,0},{1,33},{33,1},{2,34},{34,2},{3,35},{35,3},{4,36},{36... | collective-permute-start | bytes 786440 | tf_op jit(solution)/shard_map/ppermute | solution.py:92
  77.3 2.1 %copy-start.3 = (bf16[512,512]{0,1:T(8,128)(2,1)}, bf16[512,512]{0,1:T(8,128)(2,1)S(1)}, u32[]{:S(2)}) copy-start(bf16[512,512]{0,1:T(8,128)(2,1)S(1)} %fusion.8) | copy-start | bytes 1572868
  78.2 2.0 %copy-start.5 = (bf16[512,512]{0,1:T(8,128)(2,1)}, bf16[512,512]{0,1:T(8,128)(2,1)S(1)}, u32[]{:S(2)}) copy-start(bf16[512,512]{0,1:T(8,128)(2,1)S(1)} %fusion.15) | copy-start | bytes 1572868
  78.2 2.0 %copy-start.2 = (bf16[512,1024]{1,0:T(8,128)(2,1)S(1)}, bf16[512,1024]{1,0:T(8,128)(2,1)}, u32[]{:S(2)}) copy-start(bf16[512,1024]{1,0:T(8,128)(2,1)} %copy-done.1) | copy-start | bytes 3145732
  105.2 15.7 %copy-start.6 = (bf16[512,512]{0,1:T(8,128)(2,1)S(1)}, bf16[512,512]{0,1:T(8,128)(2,1)}, u32[]{:S(2)}) copy-start(bf16[512,512]{0,1:T(8,128)(2,1)} %copy-done.5) | copy-start | bytes 1572868
  112.8 28.3 %copy-start.4 = (bf16[512,512]{0,1:T(8,128)(2,1)S(1)}, bf16[512,512]{0,1:T(8,128)(2,1)}, u32[]{:S(2)}) copy-start(bf16[512,512]{0,1:T(8,128)(2,1)} %copy-done.3) | copy-start | bytes 1572868
  113.7 19.1 %all-to-all-start.4 = ((bf16[4,16,512]{2,1,0:T(8,128)(2,1)}), bf16[4,16,512]{2,1,0:T(8,128)(2,1)S(1)}, u32[]{:S(2)}, u32[]{:S(2)}) async-start(bf16[4,16,512]{2,1,0:T(8,128)(2,1)} %bitcast.18), calls=%async_computation.4 | async-start | bytes 131072 | tf_op jit(solution)/shard_map/all_to_all | solution.py:52
  122.6 18.5 %collective-permute-start.4 = (bf16[512,1024]{1,0:T(8,128)(2,1)}, bf16[512,1024]{1,0:T(8,128)(2,1)S(1)}, u32[]{:S(2)}, u32[]{:S(2)}) collective-permute-start(bf16[512,1024]{1,0:T(8,128)(2,1)} %convolution_convert_fusion), channel_id=1, source_target_pairs={{0,32},{32,0},{1,33},{33,1},{2,34},{34,2},{3,35},{35,3},{4,36},{36... | collective-permute-start | bytes 3145736 | tf_op jit(solution)/shard_map/ppermute | solution.py:137
  133.6 13.3 %all-to-all-start.5 = ((bf16[8,16,512]{2,1,0:T(8,128)(2,1)}), bf16[8,16,512]{2,1,0:T(8,128)(2,1)S(1)}, u32[]{:S(2)}, u32[]{:S(2)}) async-start(bf16[8,16,512]{2,1,0:T(8,128)(2,1)} %broadcast_in_dim.20), calls=%async_computation.5 | async-start | bytes 262144 | tf_op jit(solution)/shard_map/all_to_all | solution.py:52

commit v4 on v3

v4 whole, which is shorter than its diff:
```python
import functools

import jax
import jax.numpy as jnp
from jax import lax
from jax.experimental import pallas as pl
from jax.experimental.pallas import tpu as pltpu
from jax.sharding import Mesh
from jax.sharding import PartitionSpec as P

M = 16
smoothing = 0.1
FAR, NEAR, CORES, Y, X, H = 2, 4, 2, 4, 4, 2
Z = FAR * NEAR
RING = ("far", "near")
ENS, SPACE, PLANE = ("far", "near", "c"), ("y", "x", "h"), ("y", "x")
f32, bf16 = jnp.float32, jnp.bfloat16
SWAP = ((0, 1), (1, 0))
ACROSS = tuple((far * H + h, (1 - far) * H + 1 - h) for far in range(FAR) for h in range(H))


LANES = 128


def split_row(values, width):
    first = values.astype(bf16).astype(f32)
    second = (values - first).astype(bf16).astype(f32)
    third = values - first - second
    return jnp.concatenate(
        [first, second, third, jnp.zeros((1, width - 3 * LANES), f32)], 1
    )


def joined_row(row):
    return row[:, :LANES] + row[:, LANES : 2 * LANES] + row[:, 2 * LANES : 3 * LANES]


def total(ref):
    result = ref[0].astype(f32)
    for k in range(1, ref.shape[0]):
        result = result + ref[k].astype(f32)
    return result


def call(kernel, shapes, operands, scratch=(), flops=0, through=False):
    vmem = pl.BlockSpec(memory_space=pltpu.VMEM)
    many = isinstance(shapes, list)
    size = sum(o.size * o.dtype.itemsize for o in operands)
    in_specs = [vmem] * len(operands)
    out_specs = [vmem] * len(shapes) if many else vmem
    aliases = {}
    if through:
        in_specs[-1] = out_specs[-1] = pl.BlockSpec(memory_space=pl.ANY)
        aliases = {len(operands) - 1: len(shapes) - 1}
    return pl.pallas_call(
        kernel,
        out_shape=shapes,
        in_specs=in_specs,
        out_specs=out_specs,
        input_output_aliases=aliases,
        scratch_shapes=list(scratch),
        compiler_params=pltpu.CompilerParams(vmem_limit_bytes=40 << 20),
        cost_estimate=pl.CostEstimate(flops=flops, bytes_accessed=size, transcendentals=0),
    )(*operands)


def gelu_slope(x):
    scale = 0.7978845608028654
    square = x * x
    t = jnp.tanh(scale * x * (1.0 + 0.044715 * square))
    return 0.5 * (1.0 + t) + (0.5 * scale) * x * (1.0 - t * t) * (1.0 + 0.134145 * square)


def backward_kernel(
    g_own, g_oth, terms, out, pre_own, pre_oth, hid_own, hid_oth, lat_own, lat_oth,
    gp_own, gp_oth, sent,
):
    peers, rows = sent.shape[0], lat_own.shape[1] // sent.shape[0]
    fields, half = out.shape
    for g, pre, gp in ((g_own, pre_own, gp_own), (g_oth, pre_oth, gp_oth)):
        for k in range(0, pre.shape[0], 128):
            hidden = dot(g[:, k : k + 128], out[...], 0, 0)
            gp[k : k + 128] = (hidden * gelu_slope(pre[k : k + 128])).astype(bf16)
    step = 4
    for k in range(0, peers, step):
        columns = slice(k * rows, (k + step) * rows)
        mix = dot(lat_own[:, columns], gp_own[...], 0, 0)
        mix = mix + dot(lat_oth[:, columns], gp_oth[...], 0, 0)
        sent[k : k + step, :rows] = mix.astype(bf16).reshape(step, rows, half)

    head = dot(g_own[...], hid_own[...], 1, 0) + dot(g_oth[...], hid_oth[...], 1, 0)
    sums = jnp.sum(g_own[...].astype(f32), axis=1, keepdims=True)
    lane = lax.broadcasted_iota(jnp.int32, (fields, LANES), 1)
    field = lax.broadcasted_iota(jnp.int32, (fields, LANES), 0)
    values = jnp.sum(jnp.where(lane == field, sums, 0.0), axis=0, keepdims=True)
    loss = jnp.sum(jnp.sum(terms[...], axis=1, keepdims=True), axis=0, keepdims=True)
    values = jnp.where(lane[:1] == fields, loss, values)
    tail = jnp.where(
        lax.broadcasted_iota(jnp.int32, (16, half), 0) == 0, split_row(values, half), 0.0
    )
    for k in range(peers):
        sent[k, rows : rows + fields] = head.astype(bf16)
        sent[k, rows + fields :] = tail.astype(bf16)


def pack(block, mix, head, values):
    start = 0
    for part in (*mix, head, split_row(values, block.shape[1])):
        block[start : start + part.shape[0]] = part
        start += part.shape[0]
    block[start:] = jnp.zeros((block.shape[0] - start, block.shape[1]), f32)
    return block[...].astype(bf16)


def neighbour_kernel(got, unused_in, sent, unused_out, block):
    rows, fields = got.shape[1] - 32, 16
    piece, hpiece = rows // H // NEAR, fields // NEAR
    whole = total(got)
    values = joined_row(whole[rows + fields : rows + fields + 1])
    for n in range(NEAR):
        mix = [
            whole[h * NEAR * piece + n * piece : h * NEAR * piece + (n + 1) * piece]
            for h in range(H)
        ]
        head = whole[rows + n * hpiece : rows + (n + 1) * hpiece]
        sent[n] = pack(block, mix, head, values)


def across_kernel(piece, hpiece, got, sent, block):
    whole = total(got)
    start = H * piece + hpiece
    values = joined_row(whole[start : start + 1])
    for h in range(H):
        mix = whole[h * piece : (h + 1) * piece]
        packed = pack(block, [mix], whole[H * piece : start], values)
        for far in range(FAR):
            sent[h * FAR + far] = packed


def gather_kernel(piece, hpiece, got, sent, block):
    whole = total(got)
    start = piece + hpiece
    values = joined_row(whole[start : start + 1])
    packed = pack(block, [whole[:piece]], whole[piece:start], values)
    for k in range(NEAR * CORES):
        sent[k] = packed


def assemble_kernel(count, got, mix, head, bias, loss):
    half = got.shape[2]
    piece, hpiece = mix.shape[0] // NEAR, head.shape[0] // NEAR
    for n in range(NEAR):
        for c in range(CORES):
            block = got[n * CORES + c].astype(f32)
            columns = slice(c * half, (c + 1) * half)
            mix[n * piece : (n + 1) * piece, columns] = block[:piece]
            head[n * hpiece : (n + 1) * hpiece, columns] = block[piece : piece + hpiece]
            if n == 0:
                row = joined_row(block[piece + hpiece : piece + hpiece + 1])
                values = row if c == 0 else values + row
    fields = head.shape[0]
    bias[...] = values[:, :fields]
    loss[...] = values[:, fields : fields + 1] / count


def member_sums(chosen, members):
    differ = chosen[None] - members
    smooth = jnp.sqrt(differ * differ + smoothing * smoothing)
    return jnp.sum(differ / smooth, axis=0), jnp.sum(smooth, axis=0)


def pairwise(chosen, members, others, observed, weights):
    slope, smooth = member_sums(chosen, members)
    slope_oth, smooth_oth = member_sums(chosen, others)
    slope, smooth = slope + slope_oth, smooth + smooth_oth
    count_all = float(M)
    pairs_norm = count_all * (count_all - 1.0)
    to_truth = chosen - observed
    absolute = jnp.sqrt(to_truth * to_truth + smoothing * smoothing)
    gradient = weights * (to_truth / absolute / count_all - slope / pairs_norm)
    terms = weights * (absolute / count_all - (smooth - smoothing) / (2.0 * pairs_norm))
    return gradient.astype(bf16), terms


def all_to_all(x, axes):
    return lax.all_to_all(x, axes, 0, 0, tiled=True)


def copies(x, count):
    return jnp.broadcast_to(x[None], (count,) + x.shape)


def dot(a, b, ca, cb):
    return lax.dot_general(a, b, (((ca,), (cb,)), ((), ())), preferred_element_type=f32)


def body(latents, w_mix, w_out, bias, truth, area):
    first = lax.axis_index("c") == 0
    low = lax.axis_index("h") == 0
    points, width = latents.shape[1], latents.shape[2]
    fields = w_out.shape[1]
    rows = w_mix.shape[0]
    half = width // 2

    def pick(a, b):
        return jnp.where(first, a, b)

    mine = pick(w_mix[:, :half], w_mix[:, half:])
    far = lax.ppermute(mine, ("far", "h"), ACROSS)
    near = jnp.where(low, jnp.concatenate([mine, far], 0), jnp.concatenate([far, mine], 0))
    w_own = all_to_all(copies(near, Y * X), PLANE).reshape(width, half)
    out_own = pick(w_out[:half], w_out[half:])

    lat_own = latents[0]
    lat_oth = lax.ppermute(lat_own, "c", SWAP)
    pre_own = dot(lat_own, w_own, 1, 0)
    hid_own = jax.nn.gelu(pre_own).astype(bf16)
    pre_oth = dot(lat_oth, w_own, 1, 0)
    hid_oth = jax.nn.gelu(pre_oth).astype(bf16)
    fc_own, fc_oth = dot(out_own, hid_own, 0, 1), dot(out_own, hid_oth, 0, 1)

    rest = lax.ppermute(jnp.stack([fc_oth, fc_own]), "c", SWAP)
    fc_own = fc_own + rest[0] + bias[:, None]
    fc_oth = fc_oth + rest[1] + bias[:, None]
    members = all_to_all(copies(fc_own, Z), RING)
    others = lax.ppermute(members, "c", SWAP)
    g_own, terms = pairwise(fc_own, members, others, truth, area)
    g_oth, unused_terms = pairwise(fc_oth, members, others, truth, area)

    like = jax.ShapeDtypeStruct
    gp_own, gp_oth, sent = call(
        backward_kernel,
        [
            like((points, half), bf16),
            like((points, half), bf16),
            like((Y * X, H * rows + 32, half), bf16),
        ],
        [g_own, g_oth, terms, out_own.T, pre_own, pre_oth, hid_own, hid_oth, lat_own, lat_oth],
        flops=4 * points * half * width,
    )
    got = all_to_all(sent, PLANE)

    piece, hpiece = rows // NEAR, fields // NEAR
    block = pltpu.VMEM((H * piece + 16, half), f32)
    sent, gp_oth = call(
        neighbour_kernel,
        [like((NEAR, H * piece + 16, half), bf16), like((points, half), bf16)],
        [got, gp_oth],
        [block],
        through=True,
    )
    got = all_to_all(sent, "near")
    block = pltpu.VMEM((16, half), f32)
    kernel = functools.partial(across_kernel, piece, hpiece)
    got = all_to_all(call(kernel, like((H * FAR, 16, half), bf16), [got], [block]), ("h", "far"))

    kernel = functools.partial(gather_kernel, piece, hpiece)
    sent = call(kernel, like((NEAR * CORES, 16, half), bf16), [got], [block])
    got = all_to_all(sent, ("near", "c"))
    grad_mix, grad_out, grad_bias, loss = call(
        functools.partial(assemble_kernel, points * Y * X * H),
        [
            like((rows, width), f32),
            like((fields, width), f32),
            like((1, fields), f32),
            like((1, 1), f32),
        ],
        [got],
    )

    grad_rows = lax.ppermute(dot(gp_oth, w_own, 1, 1).astype(bf16), "c", SWAP)
    grad_latents = (dot(gp_own, w_own, 1, 1) + grad_rows.astype(f32)).astype(bf16)[None]
    return grad_latents, grad_mix, grad_out.T, grad_bias[0], loss[0, 0]


def solution(mesh):
    shape = (FAR, NEAR, CORES, Y, X, H)
    fine = Mesh(mesh.devices.reshape(shape), ("far", "near", "c", "y", "x", "h"))
    in_specs = (P(ENS, SPACE, None), P(SPACE, None), P(), P(), P(None, SPACE), P(SPACE))
    out_specs = (P(ENS, SPACE, None), P(SPACE, None), P(), P(), P())
    return jax.shard_map(
        body, mesh=fine, in_specs=in_specs, out_specs=out_specs, check_vma=False
    )
```

time: 152 us -> 147 us (0.967)
  blocking collectives: 51.6 us -> 77.3 us
  starting transfers between devices: 54.9 us -> 42 us
  waiting for transfers between devices: 23.2 us -> 14.1 us
  Pallas kernels: 0 us -> 4.31 us
  other arithmetic: 5.36 us -> 1.31 us
  matrix products: 9.35 us -> 5.7 us
  local copies, waits for them, and re-layouts: 4.24 us -> 1.14 us
  between operations: 2.81 us -> 0.84 us
    all_to_all x3 -> x4, blocking collectives: 51.6 us -> 77.3 us  [all_to_all(): return lax.all_to_all(x, axes, 0, 0, tiled=True)]
    all_to_all x3 -> x2, starting transfers between devices: 21.5 us -> 10.1 us  [all_to_all(): return lax.all_to_all(x, axes, 0, 0, tiled=True)]
    all_to_all x3 -> x2, waiting for transfers between devices: 19.7 us -> 10.7 us  [all_to_all(): return lax.all_to_all(x, axes, 0, 0, tiled=True)]
    pallas_call x0 -> x5, Pallas kernels: none -> 4.31 us  [call(): pl.pallas_call(kernel, out_shape=shapes, in_specs=in_specs, out_specs=out...]
    dot_general x12 -> x6, matrix products: 9.35 us -> 5.7 us  [dot(): lax.dot_general(a, b, (((ca,), (cb,)), ((), ())), preferred_element_type=...]
    concatenate x13 -> x0, other arithmetic: 2.15 us -> none  [the longest x6 1.3 us: scalar_rows(): terms = jnp.concatenate([first, second, third]).astype(bf16)]
  transfers between devices with their start and end apart: 8 -> 7, of which waited for: 6 -> 4; matrix products, arithmetic and copies ran while one was open for 4% -> 2% of each run, Pallas kernels for 0% -> 1%
where the time goes in v4:
time: 147 us
  blocking collectives  77.3 us (53%)
  starting transfers between devices  42 us (29%)
  waiting for transfers between devices  14.1 us (10%)
  matrix products  5.7 us (4%)
  Pallas kernels  4.31 us (3%)
    all_to_all x4, blocking collectives, all_to_all(): return lax.all_to_all(x, axes, 0, 0, tiled=True)  77.3 us
    ppermute x1, starting transfers between devices, body(): far = lax.ppermute(mine, ('far', 'h'), ACROSS)  13.3 us
    all_to_all x2, waiting for transfers between devices, all_to_all(): return lax.all_to_all(x, axes, 0, 0, tiled=True)  10.7 us
    all_to_all x2, starting transfers between devices, all_to_all(): return lax.all_to_all(x, axes, 0, 0, tiled=True)  10.1 us
    dot_general x6, matrix products, dot(): lax.dot_general(a, b, (((ca,), (cb,)), ((), ())), preferred_element_type=...  5.7 us
    ppermute x1, starting transfers between devices, body(): rest = lax.ppermute(jnp.stack([fc_oth, fc_own]), 'c', SWAP)  5.41 us
    ppermute x1, starting transfers between devices, body(): others = lax.ppermute(members, 'c', SWAP)  5.25 us
    ppermute x1, starting transfers between devices, body(): lat_oth = lax.ppermute(lat_own, 'c', SWAP)  4.33 us
  transfers between devices with their start and end apart: 7, of which 4 were waited for; matrix products, arithmetic and copies ran while one was open for 2% of the time, Pallas kernels for 1%

profile of v4, /device:TPU:1, one launch (start us, length us, event | category | flops | bytes accessed | tf_op | source)
XLA Modules:
  0.0 146.7 jit_solution(4204369657603705235)
XLA Ops:
  0.6 0.8 slice_select_fusion
  1.4 13.3 %collective-permute-start = (bf16[32,512]{1,0:T(8,128)(2,1)S(1)}, bf16[32,512]{1,0:T(8,128)(2,1)S(1)}, u32[]{:S(2)}, u32[]{:S(2)}) collective-permute-start(bf16[32,512]{1,0:T(8,128)(2,1)S(1)} %slice_select_fusion), channel_id=1, source_target_pairs={{0,257},{1,256},{256,1},{257,0},{2,259},{3,258},{258,3},{259,2},{4... | collective-permute-start | bytes 98312 | tf_op jit(solution)/shard_map/ppermute | solution.py:209
  14.7 1.4 collective-permute-done
  16.2 0.0 copy-start
  16.2 1.1 broadcast_in_dim.4
  17.2 6.8 %all-to-all-start = ((bf16[16,64,512]{2,1,0:T(8,128)(2,1)}), bf16[16,64,512]{2,1,0:T(8,128)(2,1)S(1)}, u32[]{:S(2)}, u32[]{:S(2)}) async-start(bf16[16,64,512]{2,1,0:T(8,128)(2,1)} %broadcast_in_dim.4), calls=%async_computation | async-start | bytes 2097152 | tf_op jit(solution)/shard_map/all_to_all | solution.py:186
  24.0 0.0 copy-done
  24.0 4.3 %collective-permute-start.1 = (bf16[512,1024]{1,0:T(8,128)(2,1)S(1)}, bf16[512,1024]{1,0:T(8,128)(2,1)S(1)}, u32[]{:S(2)}, u32[]{:S(2)}) collective-permute-start(bf16[512,1024]{1,0:T(8,128)(2,1)S(1)} %bitcast.42), channel_id=1, source_target_pairs={{0,32},{32,0},{1,33},{33,1},{2,34},{34,2},{3,35},{35,3},{4,36},{36... | collective-permute-start | bytes 3145736 | tf_op jit(solution)/shard_map/ppermute | solution.py:215
  28.4 10.7 %all-to-all-done = bf16[16,64,512]{2,1,0:T(8,128)(2,1)S(1)} async-done(((bf16[16,64,512]{2,1,0:T(8,128)(2,1)}), bf16[16,64,512]{2,1,0:T(8,128)(2,1)S(1)}, u32[]{:S(2)}, u32[]{:S(2)}) %all-to-all-start) | async-done | bytes 1048608 | tf_op jit(solution)/shard_map/all_to_all | solution.py:186
  39.0 0.0 copy-start.1
  39.0 0.0 copy-start.3
  39.0 0.9 fusion.8
  39.9 0.0 copy-done.3
  39.9 0.2 fusion.28
  40.2 0.0 copy-start.6
  40.2 0.0 collective-permute-done.1.lat_oth
  40.2 0.0 copy-done.1
  40.2 0.9 fusion.16
  41.1 0.0 copy-start.4
  41.1 0.0 copy-start.5
  41.1 0.2 fusion.29
  41.4 5.4 %collective-permute-start.2 = (f32[2,16,512]{2,1,0:T(8,128)S(1)}, f32[2,16,512]{2,1,0:T(8,128)S(1)}, u32[]{:S(2)}, u32[]{:S(2)}) collective-permute-start(f32[2,16,512]{2,1,0:T(8,128)S(1)} %pad_maximum_fusion), channel_id=1, source_target_pairs={{0,32},{32,0},{1,33},{33,1},{2,34},{34,2},{3,35},{35,3},{4,36},{36... | collective-permute-start | bytes 196616 | tf_op jit(solution)/shard_map/ppermute | solution.py:222
  46.8 0.9 collective-permute-done.2
  47.7 0.0 copy-done.6
  47.7 0.1 fusion.24
  47.8 20.9 %all_to_all.30 = f32[8,16,512]{2,1,0:T(8,128)S(1)} all-to-all(f32[8,16,512]{2,1,0:T(8,128)S(1)} %sub.48), channel_id=1, replica_groups=mesh['far'=2,'near'=4,'c'=2,'y'=4,'x'=4,'h'=2] {'far','near'}, dimensions={0} | all-to-all | bytes 524288 | tf_op jit(solution)/shard_map/all_to_all | solution.py:186
  68.7 5.3 %collective-permute-start.3 = (f32[8,16,512]{2,1,0:T(8,128)S(1)}, f32[8,16,512]{2,1,0:T(8,128)S(1)}, u32[]{:S(2)}, u32[]{:S(2)}) collective-permute-start(f32[8,16,512]{2,1,0:T(8,128)S(1)} %all_to_all.30), channel_id=1, source_target_pairs={{0,32},{32,0},{1,33},{33,1},{2,34},{34,2},{3,35},{35,3},{4,36},{36... | collective-permute-start | bytes 786440 | tf_op jit(solution)/shard_map/ppermute | solution.py:226
  74.0 1.1 collective-permute-done.3
  75.1 0.4 fusion.19
  75.5 0.0 copy-done.4
  75.5 0.0 copy-done.5
  75.5 0.1 subtract_multiply_fusion
  75.6 2.6 %shard_map.101 = (bf16[512,512]{1,0:T(8,128)(2,1)S(1)}, bf16[512,512]{1,0:T(8,128)(2,1)S(1)}, bf16[16,96,512]{2,1,0:T(8,128)(2,1)S(1)}) custom-call(bf16[16,512]{1,0:T(8,128)(2,1)S(1)} %get-tuple-element.33.g_own, bf16[16,512]{1,0:T(8,128)(2,1)S(1)} %get-tuple-element.36.g_oth, f32[16,512]{1,0:T(8,128)S(1)} %get-tuple-element.32.terms, ...), custom_call_target="tpu_custom_call" | custom-call | flops 1073741824 | bytes 5324800 | tf_op jit(solution)/shard_map/pallas_call | solution.py:55
  78.2 24.7 %all_to_all.31.got = bf16[16,96,512]{2,1,0:T(8,128)(2,1)S(1)} all-to-all(bf16[16,96,512]{2,1,0:T(8,128)(2,1)S(1)} %get-tuple-element.15), channel_id=1, replica_groups=mesh['far'=2,'near'=4,'c'=2,'y'=4,'x'=4,'h'=2] {'y','x'}, dimensions={0} | all-to-all | bytes 3145728 | tf_op jit(solution)/shard_map/all_to_all | solution.py:186
  102.9 0.0 copy-start.2
  102.9 0.9 shard_map.102
  103.8 3.3 %all-to-all-start.3 = ((bf16[4,32,512]{2,1,0:T(8,128)(2,1)}), bf16[4,32,512]{2,1,0:T(8,128)(2,1)S(1)}, u32[]{:S(2)}, u32[]{:S(2)}) async-start(bf16[4,32,512]{2,1,0:T(8,128)(2,1)} %get-tuple-element.18), calls=%async_computation.3 | async-start | bytes 262144 | tf_op jit(solution)/shard_map/all_to_all | solution.py:186
  107.1 0.0 copy-done.2
  107.1 1.7 %convolution_convert_fusion = bf16[512,1024]{1,0:T(8,128)(2,1)} fusion(bf16[512,512]{1,0:T(8,128)(2,1)S(1)} %get-tuple-element.17, bf16[1024,512]{1,0:T(8,128)(2,1)S(1)} %bitcast.46), kind=kOutput, calls=%fused_computation.3 | convolution fusion | flops 537395200 | bytes 2621440 | tf_op jit(solution)/shard_map/dot_general | solution.py:194
  108.9 3.7 %collective-permute-start.4 = (bf16[512,1024]{1,0:T(8,128)(2,1)}, bf16[512,1024]{1,0:T(8,128)(2,1)S(1)}, u32[]{:S(2)}, u32[]{:S(2)}) collective-permute-start(bf16[512,1024]{1,0:T(8,128)(2,1)} %convolution_convert_fusion), channel_id=1, source_target_pairs={{0,32},{32,0},{1,33},{33,1},{2,34},{34,2},{3,35},{35,3},{4,36},{36... | collective-permute-start | bytes 3145736 | tf_op jit(solution)/shard_map/ppermute | solution.py:271
  112.5 0.0 all-to-all-done.3.got
  112.6 18.7 %all_to_all.32.got = bf16[4,16,512]{2,1,0:T(8,128)(2,1)S(1)} all-to-all(bf16[4,16,512]{2,1,0:T(8,128)(2,1)S(1)} %shard_map.103), channel_id=1, replica_groups=mesh['far'=2,'near'=4,'c'=2,'y'=4,'x'=4,'h'=2] {'h','far'}, dimensions={0} | all-to-all | bytes 131072 | tf_op jit(solution)/shard_map/all_to_all | solution.py:186
  131.3 12.9 %all_to_all.33.got = bf16[8,16,512]{2,1,0:T(8,128)(2,1)S(1)} all-to-all(bf16[8,16,512]{2,1,0:T(8,128)(2,1)S(1)} %shard_map.104), channel_id=1, replica_groups=mesh['far'=2,'near'=4,'c'=2,'y'=4,'x'=4,'h'=2] {'near','c'}, dimensions={0} | all-to-all | bytes 262144 | tf_op jit(solution)/shard_map/all_to_all | solution.py:186
  144.2 0.7 shard_map.105
  144.9 0.0 collective-permute-done.4
  144.9 1.7 %fusion = bf16[1,512,1024]{2,1,0:T(8,128)(2,1)} fusion(bf16[512,1024]{1,0:T(8,128)(2,1)S(1)} %collective-permute-done.4, bf16[512,512]{1,0:T(8,128)(2,1)S(1)} %get-tuple-element.14, bf16[1024,512]{1,0:T(8,128)(2,1)S(1)} %bitcast.47), kind=kOutput, calls=%fused_computation.4 | convolution fusion | flops 538443776 | bytes 3670016 | tf_op jit(solution)/shard_map/dot_general | solution.py:194
  (6 shorter events, 0.1 us)
Async XLA Ops:
  1.4 14.7 %collective-permute-start = (bf16[32,512]{1,0:T(8,128)(2,1)S(1)}, bf16[32,512]{1,0:T(8,128)(2,1)S(1)}, u32[]{:S(2)}, u32[]{:S(2)}) collective-permute-start(bf16[32,512]{1,0:T(8,128)(2,1)S(1)} %slice_select_fusion), channel_id=1, source_target_pairs={{0,257},{1,256},{256,1},{257,0},{2,259},{3,258},{258,3},{259,2},{4... | collective-permute-start | bytes 98312 | tf_op jit(solution)/shard_map/ppermute | solution.py:209
  16.2 7.8 %copy-start = (bf16[1,512,1024]{2,1,0:T(8,128)(2,1)S(1)}, bf16[1,512,1024]{2,1,0:T(8,128)(2,1)}, u32[]{:S(2)}) copy-start(bf16[1,512,1024]{2,1,0:T(8,128)(2,1)} %param.6) | copy-start | bytes 3145732
  17.2 21.8 %all-to-all-start = ((bf16[16,64,512]{2,1,0:T(8,128)(2,1)}), bf16[16,64,512]{2,1,0:T(8,128)(2,1)S(1)}, u32[]{:S(2)}, u32[]{:S(2)}) async-start(bf16[16,64,512]{2,1,0:T(8,128)(2,1)} %broadcast_in_dim.4), calls=%async_computation | async-start | bytes 2097152 | tf_op jit(solution)/shard_map/all_to_all | solution.py:186
  24.0 16.2 %collective-permute-start.1 = (bf16[512,1024]{1,0:T(8,128)(2,1)S(1)}, bf16[512,1024]{1,0:T(8,128)(2,1)S(1)}, u32[]{:S(2)}, u32[]{:S(2)}) collective-permute-start(bf16[512,1024]{1,0:T(8,128)(2,1)S(1)} %bitcast.42), channel_id=1, source_target_pairs={{0,32},{32,0},{1,33},{33,1},{2,34},{34,2},{3,35},{35,3},{4,36},{36... | collective-permute-start | bytes 3145736 | tf_op jit(solution)/shard_map/ppermute | solution.py:215
  39.0 1.2 copy-start.1
  39.0 0.9 copy-start.3
  40.2 7.5 %copy-start.6 = (f32[16]{0:T(128)S(1)}, f32[16]{0:T(128)}, u32[]{:S(2)}) copy-start(f32[16]{0:T(128)} %param.9) | copy-start | bytes 196
  41.1 34.4 %copy-start.4 = (f32[16,512]{1,0:T(8,128)S(1)}, f32[16,512]{1,0:T(8,128)}, u32[]{:S(2)}) copy-start(f32[16,512]{1,0:T(8,128)} %param.10) | copy-start | bytes 98308
  41.1 34.4 %copy-start.5 = (f32[512]{0:T(512)S(1)}, f32[512]{0:T(512)}, u32[]{:S(2)}) copy-start(f32[512]{0:T(512)} %param.11) | copy-start | bytes 6148
  41.4 6.3 %collective-permute-start.2 = (f32[2,16,512]{2,1,0:T(8,128)S(1)}, f32[2,16,512]{2,1,0:T(8,128)S(1)}, u32[]{:S(2)}, u32[]{:S(2)}) collective-permute-start(f32[2,16,512]{2,1,0:T(8,128)S(1)} %pad_maximum_fusion), channel_id=1, source_target_pairs={{0,32},{32,0},{1,33},{33,1},{2,34},{34,2},{3,35},{35,3},{4,36},{36... | collective-permute-start | bytes 196616 | tf_op jit(solution)/shard_map/ppermute | solution.py:222
  68.7 6.4 %collective-permute-start.3 = (f32[8,16,512]{2,1,0:T(8,128)S(1)}, f32[8,16,512]{2,1,0:T(8,128)S(1)}, u32[]{:S(2)}, u32[]{:S(2)}) collective-permute-start(f32[8,16,512]{2,1,0:T(8,128)S(1)} %all_to_all.30), channel_id=1, source_target_pairs={{0,32},{32,0},{1,33},{33,1},{2,34},{34,2},{3,35},{35,3},{4,36},{36... | collective-permute-start | bytes 786440 | tf_op jit(solution)/shard_map/ppermute | solution.py:226
  102.9 4.2 %copy-start.2 = (bf16[16,64,512]{2,1,0:T(8,128)(2,1)S(1)}, bf16[16,64,512]{2,1,0:T(8,128)(2,1)}, u32[]{:S(2)}) copy-start(bf16[16,64,512]{2,1,0:T(8,128)(2,1)} %copy-done.1) | copy-start | bytes 3145732
  103.8 8.7 %all-to-all-start.3 = ((bf16[4,32,512]{2,1,0:T(8,128)(2,1)}), bf16[4,32,512]{2,1,0:T(8,128)(2,1)S(1)}, u32[]{:S(2)}, u32[]{:S(2)}) async-start(bf16[4,32,512]{2,1,0:T(8,128)(2,1)} %get-tuple-element.18), calls=%async_computation.3 | async-start | bytes 262144 | tf_op jit(solution)/shard_map/all_to_all | solution.py:186
  108.9 36.1 %collective-permute-start.4 = (bf16[512,1024]{1,0:T(8,128)(2,1)}, bf16[512,1024]{1,0:T(8,128)(2,1)S(1)}, u32[]{:S(2)}, u32[]{:S(2)}) collective-permute-start(bf16[512,1024]{1,0:T(8,128)(2,1)} %convolution_convert_fusion), channel_id=1, source_target_pairs={{0,32},{32,0},{1,33},{33,1},{2,34},{34,2},{3,35},{35,3},{4,36},{36... | collective-permute-start | bytes 3145736 | tf_op jit(solution)/shard_map/ppermute | solution.py:271

commit v5 on v4

--- a/solution.py
+++ b/solution.py
@@ -71,6 +71,12 @@
     return 0.5 * (1.0 + t) + (0.5 * scale) * x * (1.0 - t * t) * (1.0 + 0.134145 * square)
 
 
+def forecast_kernel(out, hid_own, hid_oth, part):
+    fields = out.shape[0]
+    part[:fields] = dot(out[...], hid_own[...], 1, 1)
+    part[fields:] = dot(out[...], hid_oth[...], 1, 1)
+
+
 def backward_kernel(
     g_own, g_oth, terms, out, pre_own, pre_oth, hid_own, hid_oth, lat_own, lat_oth,
     gp_own, gp_oth, sent,
@@ -103,6 +109,14 @@
         sent[k, rows + fields :] = tail.astype(bf16)
 
 
+def partial_kernel(gp, weight, rows):
+    rows[...] = dot(gp[...], weight[...], 1, 1).astype(bf16)
+
+
+def latents_kernel(gp, weight, other, rows):
+    rows[...] = (dot(gp[...], weight[...], 1, 1) + other[...].astype(f32)).astype(bf16)
+
+
 def pack(block, mix, head, values):
     start = 0
     for part in (*mix, head, split_row(values, block.shape[1])):
@@ -209,7 +223,7 @@
     far = lax.ppermute(mine, ("far", "h"), ACROSS)
     near = jnp.where(low, jnp.concatenate([mine, far], 0), jnp.concatenate([far, mine], 0))
     w_own = all_to_all(copies(near, Y * X), PLANE).reshape(width, half)
-    out_own = pick(w_out[:half], w_out[half:])
+    out_own = pick(w_out.T[:, :half], w_out.T[:, half:])
 
     lat_own = latents[0]
     lat_oth = lax.ppermute(lat_own, "c", SWAP)
@@ -217,17 +231,24 @@
     hid_own = jax.nn.gelu(pre_own).astype(bf16)
     pre_oth = dot(lat_oth, w_own, 1, 0)
     hid_oth = jax.nn.gelu(pre_oth).astype(bf16)
-    fc_own, fc_oth = dot(out_own, hid_own, 0, 1), dot(out_own, hid_oth, 0, 1)
-
-    rest = lax.ppermute(jnp.stack([fc_oth, fc_own]), "c", SWAP)
-    fc_own = fc_own + rest[0] + bias[:, None]
-    fc_oth = fc_oth + rest[1] + bias[:, None]
+
+    like = jax.ShapeDtypeStruct
+    part = call(
+        forecast_kernel,
+        like((2 * fields, points), f32),
+        [out_own, hid_own, hid_oth],
+        flops=4 * fields * points * half,
+    )
+    both = lax.all_gather(part, "c", axis=0)
+    rest = pick(both[1], both[0])
+    fc_own = part[:fields] + rest[fields:] + bias[:, None]
+    fc_oth = part[fields:] + rest[:fields] + bias[:, None]
     members = all_to_all(copies(fc_own, Z), RING)
-    others = lax.ppermute(members, "c", SWAP)
+    both = lax.all_gather(members, "c", axis=0)
+    others = pick(both[1], both[0])
     g_own, terms = pairwise(fc_own, members, others, truth, area)
     g_oth, unused_terms = pairwise(fc_oth, members, others, truth, area)
 
-    like = jax.ShapeDtypeStruct
     gp_own, gp_oth, sent = call(
         backward_kernel,
         [
@@ -235,7 +256,7 @@
             like((points, half), bf16),
             like((Y * X, H * rows + 32, half), bf16),
         ],
-        [g_own, g_oth, terms, out_own.T, pre_own, pre_oth, hid_own, hid_oth, lat_own, lat_oth],
+        [g_own, g_oth, terms, out_own, pre_own, pre_oth, hid_own, hid_oth, lat_own, lat_oth],
         flops=4 * points * half * width,
     )
     got = all_to_all(sent, PLANE)
@@ -268,8 +289,10 @@
         [got],
     )
 
-    grad_rows = lax.ppermute(dot(gp_oth, w_own, 1, 1).astype(bf16), "c", SWAP)
-    grad_latents = (dot(gp_own, w_own, 1, 1) + grad_rows.astype(f32)).astype(bf16)[None]
+    rows_like, work = like((points, width), bf16), 16 * points * half * width
+    grad_rows = call(partial_kernel, rows_like, [gp_oth, w_own], flops=work)
+    grad_rows = lax.ppermute(grad_rows, "c", SWAP)
+    grad_latents = call(latents_kernel, rows_like, [gp_own, w_own, grad_rows], flops=work)[None]
     return grad_latents, grad_mix, grad_out.T, grad_bias[0], loss[0, 0]
 
 

time: 147 us -> 146 us (level)
  starting transfers between devices: 42 us -> 34.6 us
  blocking collectives: 77.3 us -> 81.9 us
  matrix products: 5.7 us -> 1.81 us
  Pallas kernels: 4.31 us -> 7.13 us
  local copies, waits for them, and re-layouts: 1.14 us -> 2.95 us
    ppermute x3 -> x1, starting transfers between devices: 14.3 us -> 3.71 us  [body(): grad_rows = lax.ppermute(grad_rows, 'c', SWAP)]
    all_gather x0 -> x2, blocking collectives: none -> 10.2 us  [the longest x1 5.15 us: body(): both = lax.all_gather(members, 'c', axis=0)]
    all_to_all x4, blocking collectives: 77.3 us -> 71.7 us  [all_to_all(): return lax.all_to_all(x, axes, 0, 0, tiled=True)]
    dot_general x6 -> x2, matrix products: 5.7 us -> 1.81 us  [dot(): lax.dot_general(a, b, (((ca,), (cb,)), ((), ())), preferred_element_type=...]
    all_to_all x2, starting transfers between devices: 10.1 us -> 13.3 us  [all_to_all(): return lax.all_to_all(x, axes, 0, 0, tiled=True)]
    all_to_all x2, waiting for transfers between devices: 10.7 us -> 13.7 us  [all_to_all(): return lax.all_to_all(x, axes, 0, 0, tiled=True)]
    pallas_call x5 -> x8, Pallas kernels: 4.31 us -> 7.13 us  [call(): pl.pallas_call(kernel, out_shape=shapes, in_specs=in_specs, out_specs=out...]
    ppermute x3 -> x1, waiting for transfers between devices: 2.01 us -> 0.01 us  [body(): grad_rows = lax.ppermute(grad_rows, 'c', SWAP)]
  transfers between devices with their start and end apart: 7 -> 5, of which waited for: 4 -> 3; matrix products, arithmetic and copies ran while one was open for 2% -> 1% of each run, Pallas kernels for 1% -> 2%
where the time goes in v5:
time: 146 us
  blocking collectives  81.9 us (56%)
  starting transfers between devices  34.6 us (24%)
  waiting for transfers between devices  15.1 us (10%)
  Pallas kernels  7.13 us (5%)
  local copies, waits for them, and re-layouts  2.95 us (2%)
  matrix products  1.81 us (1%)
    all_to_all x4, blocking collectives, all_to_all(): return lax.all_to_all(x, axes, 0, 0, tiled=True)  71.7 us
    all_to_all x2, waiting for transfers between devices, all_to_all(): return lax.all_to_all(x, axes, 0, 0, tiled=True)  13.7 us
    all_to_all x2, starting transfers between devices, all_to_all(): return lax.all_to_all(x, axes, 0, 0, tiled=True)  13.3 us
    ppermute x1, starting transfers between devices, body(): far = lax.ppermute(mine, ('far', 'h'), ACROSS)  13.3 us
    pallas_call x8, Pallas kernels, call(): pl.pallas_call(kernel, out_shape=shapes, in_specs=in_specs, out_specs=out...  7.13 us
    all_gather x1, blocking collectives, body(): both = lax.all_gather(members, 'c', axis=0)  5.15 us
    all_gather x1, blocking collectives, body(): both = lax.all_gather(part, 'c', axis=0)  5.05 us
    ppermute x1, starting transfers between devices, body(): lat_oth = lax.ppermute(lat_own, 'c', SWAP)  4.33 us
  transfers between devices with their start and end apart: 5, of which 3 were waited for; matrix products, arithmetic and copies ran while one was open for 1% of the time, Pallas kernels for 2%

profile of v5, /device:TPU:1, one launch (start us, length us, event | category | flops | bytes accessed | tf_op | source)
XLA Modules:
  0.0 145.7 jit_solution(1528243380648849413)
XLA Ops:
  0.6 0.8 slice_select_fusion.2
  1.4 13.3 %collective-permute-start = (bf16[32,512]{1,0:T(8,128)(2,1)S(1)}, bf16[32,512]{1,0:T(8,128)(2,1)S(1)}, u32[]{:S(2)}, u32[]{:S(2)}) collective-permute-start(bf16[32,512]{1,0:T(8,128)(2,1)S(1)} %slice_select_fusion.2), channel_id=1, source_target_pairs={{0,257},{1,256},{256,1},{257,0},{2,259},{3,258},{258,3},{259,2},{4... | collective-permute-start | bytes 98312 | tf_op jit(solution)/shard_map/ppermute | solution.py:223
  14.7 1.4 collective-permute-done
  16.2 0.0 copy-start
  16.2 0.0 copy-start.3
  16.2 1.1 broadcast_in_dim.4
  17.3 6.8 %all-to-all-start = ((bf16[16,64,512]{2,1,0:T(8,128)(2,1)}), bf16[16,64,512]{2,1,0:T(8,128)(2,1)S(1)}, u32[]{:S(2)}, u32[]{:S(2)}) async-start(bf16[16,64,512]{2,1,0:T(8,128)(2,1)} %broadcast_in_dim.4), calls=%async_computation | async-start | bytes 2097152 | tf_op jit(solution)/shard_map/all_to_all | solution.py:200
  24.0 0.0 copy-done
  24.0 4.3 %collective-permute-start.1 = (bf16[512,1024]{1,0:T(8,128)(2,1)S(1)}, bf16[512,1024]{1,0:T(8,128)(2,1)S(1)}, u32[]{:S(2)}, u32[]{:S(2)}) collective-permute-start(bf16[512,1024]{1,0:T(8,128)(2,1)S(1)} %bitcast.36), channel_id=1, source_target_pairs={{0,32},{32,0},{1,33},{33,1},{2,34},{34,2},{3,35},{35,3},{4,36},{36... | collective-permute-start | bytes 3145736 | tf_op jit(solution)/shard_map/ppermute | solution.py:229
  28.4 0.0 copy-done.3
  28.4 10.6 %all-to-all-done = bf16[16,64,512]{2,1,0:T(8,128)(2,1)S(1)} async-done(((bf16[16,64,512]{2,1,0:T(8,128)(2,1)}), bf16[16,64,512]{2,1,0:T(8,128)(2,1)S(1)}, u32[]{:S(2)}, u32[]{:S(2)}) %all-to-all-start) | async-done | bytes 1048608 | tf_op jit(solution)/shard_map/all_to_all | solution.py:200
  39.0 0.9 fusion.7
  39.9 0.0 copy-start.6
  39.9 0.0 collective-permute-done.1.lat_oth
  40.0 0.9 fusion.15
  40.9 0.4 shard_map.101
  41.2 5.0 %all-gather = f32[64,512]{1,0:T(8,128)S(1)} all-gather(f32[32,512]{1,0:T(8,128)S(1)} %shard_map.101), channel_id=2, replica_groups=mesh['far'=2,'near'=4,'c'=2,'y'=4,'x'=4,'h'=2] {'c'}, dimensions={0}, use_global_device_ids=true | all-gather | bytes 196608 | tf_op jit(solution)/shard_map/all_gather | solution.py:242
  46.3 0.0 copy-start.4
  46.3 0.0 copy-start.5
  46.3 0.0 copy-done.6
  46.3 0.1 fusion.24
  46.4 20.9 %all_to_all.30 = f32[8,16,512]{2,1,0:T(8,128)S(1)} all-to-all(f32[8,16,512]{2,1,0:T(8,128)S(1)} %sub.48), channel_id=1, replica_groups=mesh['far'=2,'near'=4,'c'=2,'y'=4,'x'=4,'h'=2] {'far','near'}, dimensions={0} | all-to-all | bytes 524288 | tf_op jit(solution)/shard_map/all_to_all | solution.py:200
  67.4 5.2 %all-gather.1 = f32[16,16,512]{2,1,0:T(8,128)S(1)} all-gather(f32[8,16,512]{2,1,0:T(8,128)S(1)} %all_to_all.30), channel_id=3, replica_groups=mesh['far'=2,'near'=4,'c'=2,'y'=4,'x'=4,'h'=2] {'c'}, dimensions={0}, use_global_device_ids=true | all-gather | bytes 786432 | tf_op jit(solution)/shard_map/all_gather | solution.py:247
  72.5 0.4 fusion.18
  72.9 0.0 copy-done.4
  72.9 0.0 copy-done.5
  72.9 0.1 subtract_multiply_fusion
  73.0 2.6 %shard_map.102 = (bf16[512,512]{1,0:T(8,128)(2,1)S(1)}, bf16[512,512]{1,0:T(8,128)(2,1)S(1)}, bf16[16,96,512]{2,1,0:T(8,128)(2,1)S(1)}) custom-call(bf16[16,512]{1,0:T(8,128)(2,1)S(1)} %get-tuple-element.35.g_own, bf16[16,512]{1,0:T(8,128)(2,1)S(1)} %get-tuple-element.36.g_oth, f32[16,512]{1,0:T(8,128)S(1)} %get-tuple-element.34.terms, ...), custom_call_target="tpu_custom_call" | custom-call | flops 1073741824 | bytes 5324800 | tf_op jit(solution)/shard_map/pallas_call | solution.py:55
  75.6 0.0 copy-start.1
  75.6 0.8 copy-done.1
  76.4 24.6 %all_to_all.31.got = bf16[16,96,512]{2,1,0:T(8,128)(2,1)S(1)} all-to-all(bf16[16,96,512]{2,1,0:T(8,128)(2,1)S(1)} %get-tuple-element.15), channel_id=1, replica_groups=mesh['far'=2,'near'=4,'c'=2,'y'=4,'x'=4,'h'=2] {'y','x'}, dimensions={0} | all-to-all | bytes 3145728 | tf_op jit(solution)/shard_map/all_to_all | solution.py:200
  101.0 0.2 shard_map.103
  101.3 0.7 shard_map.104
  102.0 3.7 %collective-permute-start.2 = (bf16[512,1024]{1,0:T(8,128)(2,1)S(1)}, bf16[512,1024]{1,0:T(8,128)(2,1)S(1)}, u32[]{:S(2)}, u32[]{:S(2)}) collective-permute-start(bf16[512,1024]{1,0:T(8,128)(2,1)S(1)} %shard_map.104), channel_id=1, source_target_pairs={{0,32},{32,0},{1,33},{33,1},{2,34},{34,2},{3,35},{35,3},{4,36},{36... | collective-permute-start | bytes 3145736 | tf_op jit(solution)/shard_map/ppermute | solution.py:294
  105.7 7.3 %all_to_all.32.got = bf16[4,32,512]{2,1,0:T(8,128)(2,1)S(1)} all-to-all(bf16[4,32,512]{2,1,0:T(8,128)(2,1)S(1)} %get-tuple-element.18), channel_id=1, replica_groups=mesh['far'=2,'near'=4,'c'=2,'y'=4,'x'=4,'h'=2] {'near'}, dimensions={0} | all-to-all | bytes 262144 | tf_op jit(solution)/shard_map/all_to_all | solution.py:200
  113.1 18.9 %all_to_all.33.got = bf16[4,16,512]{2,1,0:T(8,128)(2,1)S(1)} all-to-all(bf16[4,16,512]{2,1,0:T(8,128)(2,1)S(1)} %shard_map.106), channel_id=1, replica_groups=mesh['far'=2,'near'=4,'c'=2,'y'=4,'x'=4,'h'=2] {'h','far'}, dimensions={0} | all-to-all | bytes 131072 | tf_op jit(solution)/shard_map/all_to_all | solution.py:200
  131.9 0.7 shard_map.107
  132.6 6.6 %all-to-all-start.5 = ((bf16[8,16,512]{2,1,0:T(8,128)(2,1)}), bf16[8,16,512]{2,1,0:T(8,128)(2,1)S(1)}, u32[]{:S(2)}, u32[]{:S(2)}) async-start(bf16[8,16,512]{2,1,0:T(8,128)(2,1)} %shard_map.107), calls=%async_computation.5 | async-start | bytes 262144 | tf_op jit(solution)/shard_map/all_to_all | solution.py:200
  139.2 0.0 collective-permute-done.2.other
  139.2 0.0 copy-start.2
  139.2 1.0 copy-done.2
  140.2 1.7 %shard_map.105 = bf16[512,1024]{1,0:T(8,128)(2,1)} custom-call(bf16[512,512]{1,0:T(8,128)(2,1)S(1)} %copy-done.2, bf16[1024,512]{1,0:T(8,128)(2,1)S(1)} %bitcast.35, bf16[512,1024]{1,0:T(8,128)(2,1)S(1)} %collective-permute-done.2.other), custom_call_target="tpu_custom_call" | custom-call | flops 4294967296 | bytes 2621440 | tf_op jit(solution)/shard_map/pallas_call | solution.py:55
  141.9 3.1 %all-to-all-done.5.got = bf16[8,16,512]{2,1,0:T(8,128)(2,1)S(1)} async-done(((bf16[8,16,512]{2,1,0:T(8,128)(2,1)}), bf16[8,16,512]{2,1,0:T(8,128)(2,1)S(1)}, u32[]{:S(2)}, u32[]{:S(2)}) %all-to-all-start.5) | async-done | bytes 131104 | tf_op jit(solution)/shard_map/all_to_all | solution.py:200
  145.0 0.7 shard_map.108
  (5 shorter events, 0.1 us)
Async XLA Ops:
  1.4 14.7 %collective-permute-start = (bf16[32,512]{1,0:T(8,128)(2,1)S(1)}, bf16[32,512]{1,0:T(8,128)(2,1)S(1)}, u32[]{:S(2)}, u32[]{:S(2)}) collective-permute-start(bf16[32,512]{1,0:T(8,128)(2,1)S(1)} %slice_select_fusion.2), channel_id=1, source_target_pairs={{0,257},{1,256},{256,1},{257,0},{2,259},{3,258},{258,3},{259,2},{4... | collective-permute-start | bytes 98312 | tf_op jit(solution)/shard_map/ppermute | solution.py:223
  16.2 7.9 %copy-start = (bf16[1,512,1024]{2,1,0:T(8,128)(2,1)S(1)}, bf16[1,512,1024]{2,1,0:T(8,128)(2,1)}, u32[]{:S(2)}) copy-start(bf16[1,512,1024]{2,1,0:T(8,128)(2,1)} %param.6) | copy-start | bytes 3145732
  16.2 12.2 %copy-start.3 = (bf16[1024,16]{0,1:T(8,128)(2,1)S(1)}, bf16[1024,16]{0,1:T(8,128)(2,1)}, u32[]{:S(2)}) copy-start(bf16[1024,16]{0,1:T(8,128)(2,1)} %param.8) | copy-start | bytes 98308
  17.3 21.8 %all-to-all-start = ((bf16[16,64,512]{2,1,0:T(8,128)(2,1)}), bf16[16,64,512]{2,1,0:T(8,128)(2,1)S(1)}, u32[]{:S(2)}, u32[]{:S(2)}) async-start(bf16[16,64,512]{2,1,0:T(8,128)(2,1)} %broadcast_in_dim.4), calls=%async_computation | async-start | bytes 2097152 | tf_op jit(solution)/shard_map/all_to_all | solution.py:200
  24.0 15.9 %collective-permute-start.1 = (bf16[512,1024]{1,0:T(8,128)(2,1)S(1)}, bf16[512,1024]{1,0:T(8,128)(2,1)S(1)}, u32[]{:S(2)}, u32[]{:S(2)}) collective-permute-start(bf16[512,1024]{1,0:T(8,128)(2,1)S(1)} %bitcast.36), channel_id=1, source_target_pairs={{0,32},{32,0},{1,33},{33,1},{2,34},{34,2},{3,35},{35,3},{4,36},{36... | collective-permute-start | bytes 3145736 | tf_op jit(solution)/shard_map/ppermute | solution.py:229
  39.9 6.4 %copy-start.6 = (f32[16]{0:T(128)S(1)}, f32[16]{0:T(128)}, u32[]{:S(2)}) copy-start(f32[16]{0:T(128)} %param.9) | copy-start | bytes 196
  46.3 26.6 %copy-start.4 = (f32[16,512]{1,0:T(8,128)S(1)}, f32[16,512]{1,0:T(8,128)}, u32[]{:S(2)}) copy-start(f32[16,512]{1,0:T(8,128)} %param.10) | copy-start | bytes 98308
  46.3 26.6 %copy-start.5 = (f32[512]{0:T(512)S(1)}, f32[512]{0:T(512)}, u32[]{:S(2)}) copy-start(f32[512]{0:T(512)} %param.11) | copy-start | bytes 6148
  75.6 0.8 copy-start.1
  102.0 37.2 %collective-permute-start.2 = (bf16[512,1024]{1,0:T(8,128)(2,1)S(1)}, bf16[512,1024]{1,0:T(8,128)(2,1)S(1)}, u32[]{:S(2)}, u32[]{:S(2)}) collective-permute-start(bf16[512,1024]{1,0:T(8,128)(2,1)S(1)} %shard_map.104), channel_id=1, source_target_pairs={{0,32},{32,0},{1,33},{33,1},{2,34},{34,2},{3,35},{35,3},{4,36},{36... | collective-permute-start | bytes 3145736 | tf_op jit(solution)/shard_map/ppermute | solution.py:294
  132.6 12.4 %all-to-all-start.5 = ((bf16[8,16,512]{2,1,0:T(8,128)(2,1)}), bf16[8,16,512]{2,1,0:T(8,128)(2,1)S(1)}, u32[]{:S(2)}, u32[]{:S(2)}) async-start(bf16[8,16,512]{2,1,0:T(8,128)(2,1)} %shard_map.107), calls=%async_computation.5 | async-start | bytes 262144 | tf_op jit(solution)/shard_map/all_to_all | solution.py:200
  139.2 1.0 copy-start.2

commit v6 on v5

--- a/solution.py
+++ b/solution.py
@@ -42,16 +42,16 @@
     return result
 
 
-def call(kernel, shapes, operands, scratch=(), flops=0, through=False):
+def call(kernel, shapes, operands, scratch=(), flops=0, through=0):
     vmem = pl.BlockSpec(memory_space=pltpu.VMEM)
     many = isinstance(shapes, list)
     size = sum(o.size * o.dtype.itemsize for o in operands)
     in_specs = [vmem] * len(operands)
     out_specs = [vmem] * len(shapes) if many else vmem
     aliases = {}
-    if through:
-        in_specs[-1] = out_specs[-1] = pl.BlockSpec(memory_space=pl.ANY)
-        aliases = {len(operands) - 1: len(shapes) - 1}
+    for k in range(1, through + 1):
+        in_specs[-k] = out_specs[-k] = pl.BlockSpec(memory_space=pl.ANY)
+        aliases[len(operands) - k] = len(shapes) - k
     return pl.pallas_call(
         kernel,
         out_shape=shapes,
@@ -126,7 +126,7 @@
     return block[...].astype(bf16)
 
 
-def neighbour_kernel(got, unused_in, sent, unused_out, block):
+def neighbour_kernel(got, unused_a, unused_b, sent, unused_c, unused_d, block):
     rows, fields = got.shape[1] - 32, 16
     piece, hpiece = rows // H // NEAR, fields // NEAR
     whole = total(got)
@@ -263,12 +263,13 @@
 
     piece, hpiece = rows // NEAR, fields // NEAR
     block = pltpu.VMEM((H * piece + 16, half), f32)
-    sent, gp_oth = call(
+    gp_like = like((points, half), bf16)
+    sent, gp_own, gp_oth = call(
         neighbour_kernel,
-        [like((NEAR, H * piece + 16, half), bf16), like((points, half), bf16)],
-        [got, gp_oth],
+        [like((NEAR, H * piece + 16, half), bf16), gp_like, gp_like],
+        [got, gp_own, gp_oth],
         [block],
-        through=True,
+        through=2,
     )
     got = all_to_all(sent, "near")
     block = pltpu.VMEM((16, half), f32)

time: 146 us -> 146 us (level)
  no operation moved by 1% of the time
where the time goes in v6:
time: 146 us; the launch traced here: 145 us
  blocking collectives  81.9 us (56%)
  starting transfers between devices  34.6 us (24%)
  waiting for transfers between devices  15.1 us (10%)
  Pallas kernels  7.13 us (5%)
  local copies, waits for them, and re-layouts  2.2 us (2%)
  matrix products  1.81 us (1%)
    all_to_all x4, blocking collectives, all_to_all(): return lax.all_to_all(x, axes, 0, 0, tiled=True)  71.7 us
    all_to_all x2, waiting for transfers between devices, all_to_all(): return lax.all_to_all(x, axes, 0, 0, tiled=True)  13.7 us
    all_to_all x2, starting transfers between devices, all_to_all(): return lax.all_to_all(x, axes, 0, 0, tiled=True)  13.3 us
    ppermute x1, starting transfers between devices, body(): far = lax.ppermute(mine, ('far', 'h'), ACROSS)  13.3 us
    pallas_call x8, Pallas kernels, call(): pl.pallas_call(kernel, out_shape=shapes, in_specs=in_specs, out_specs=out...  7.13 us
    all_gather x1, blocking collectives, body(): both = lax.all_gather(members, 'c', axis=0)  5.15 us
    all_gather x1, blocking collectives, body(): both = lax.all_gather(part, 'c', axis=0)  5.05 us
    ppermute x1, starting transfers between devices, body(): lat_oth = lax.ppermute(lat_own, 'c', SWAP)  4.33 us
  transfers between devices with their start and end apart: 5, of which 3 were waited for; matrix products, arithmetic and copies ran while one was open for 1% of the time, Pallas kernels for 2%

profile of v6, /device:TPU:1, one launch (start us, length us, event | category | flops | bytes accessed | tf_op | source)
XLA Modules:
  0.0 145.0 jit_solution(12014814438099696209)
XLA Ops:
  0.6 0.8 slice_select_fusion.2
  1.4 13.3 %collective-permute-start = (bf16[32,512]{1,0:T(8,128)(2,1)S(1)}, bf16[32,512]{1,0:T(8,128)(2,1)S(1)}, u32[]{:S(2)}, u32[]{:S(2)}) collective-permute-start(bf16[32,512]{1,0:T(8,128)(2,1)S(1)} %slice_select_fusion.2), channel_id=1, source_target_pairs={{0,257},{1,256},{256,1},{257,0},{2,259},{3,258},{258,3},{259,2},{4... | collective-permute-start | bytes 98312 | tf_op jit(solution)/shard_map/ppermute | solution.py:223
  14.7 1.4 collective-permute-done
  16.2 0.0 copy-start
  16.2 0.0 copy-start.3
  16.2 1.1 broadcast_in_dim.4
  17.3 6.8 %all-to-all-start = ((bf16[16,64,512]{2,1,0:T(8,128)(2,1)}), bf16[16,64,512]{2,1,0:T(8,128)(2,1)S(1)}, u32[]{:S(2)}, u32[]{:S(2)}) async-start(bf16[16,64,512]{2,1,0:T(8,128)(2,1)} %broadcast_in_dim.4), calls=%async_computation | async-start | bytes 2097152 | tf_op jit(solution)/shard_map/all_to_all | solution.py:200
  24.0 0.0 copy-done
  24.0 4.3 %collective-permute-start.1 = (bf16[512,1024]{1,0:T(8,128)(2,1)S(1)}, bf16[512,1024]{1,0:T(8,128)(2,1)S(1)}, u32[]{:S(2)}, u32[]{:S(2)}) collective-permute-start(bf16[512,1024]{1,0:T(8,128)(2,1)S(1)} %bitcast.36), channel_id=1, source_target_pairs={{0,32},{32,0},{1,33},{33,1},{2,34},{34,2},{3,35},{35,3},{4,36},{36... | collective-permute-start | bytes 3145736 | tf_op jit(solution)/shard_map/ppermute | solution.py:229
  28.4 0.0 copy-done.3
  28.4 10.6 %all-to-all-done = bf16[16,64,512]{2,1,0:T(8,128)(2,1)S(1)} async-done(((bf16[16,64,512]{2,1,0:T(8,128)(2,1)}), bf16[16,64,512]{2,1,0:T(8,128)(2,1)S(1)}, u32[]{:S(2)}, u32[]{:S(2)}) %all-to-all-start) | async-done | bytes 1048608 | tf_op jit(solution)/shard_map/all_to_all | solution.py:200
  39.0 0.9 fusion.7
  39.9 0.0 copy-start.6
  39.9 0.0 collective-permute-done.1.lat_oth
  40.0 0.9 fusion.15
  40.9 0.4 shard_map.101
  41.2 5.0 %all-gather = f32[64,512]{1,0:T(8,128)S(1)} all-gather(f32[32,512]{1,0:T(8,128)S(1)} %shard_map.101), channel_id=2, replica_groups=mesh['far'=2,'near'=4,'c'=2,'y'=4,'x'=4,'h'=2] {'c'}, dimensions={0}, use_global_device_ids=true | all-gather | bytes 196608 | tf_op jit(solution)/shard_map/all_gather | solution.py:242
  46.3 0.0 copy-start.4
  46.3 0.0 copy-start.5
  46.3 0.0 copy-done.6
  46.3 0.1 fusion.24
  46.4 20.9 %all_to_all.30 = f32[8,16,512]{2,1,0:T(8,128)S(1)} all-to-all(f32[8,16,512]{2,1,0:T(8,128)S(1)} %sub.48), channel_id=1, replica_groups=mesh['far'=2,'near'=4,'c'=2,'y'=4,'x'=4,'h'=2] {'far','near'}, dimensions={0} | all-to-all | bytes 524288 | tf_op jit(solution)/shard_map/all_to_all | solution.py:200
  67.4 5.2 %all-gather.1 = f32[16,16,512]{2,1,0:T(8,128)S(1)} all-gather(f32[8,16,512]{2,1,0:T(8,128)S(1)} %all_to_all.30), channel_id=3, replica_groups=mesh['far'=2,'near'=4,'c'=2,'y'=4,'x'=4,'h'=2] {'c'}, dimensions={0}, use_global_device_ids=true | all-gather | bytes 786432 | tf_op jit(solution)/shard_map/all_gather | solution.py:247
  72.5 0.4 fusion.18
  72.9 0.0 copy-done.4
  72.9 0.0 copy-done.5
  72.9 0.1 subtract_multiply_fusion
  73.0 2.6 %shard_map.102 = (bf16[512,512]{1,0:T(8,128)(2,1)S(1)}, bf16[512,512]{1,0:T(8,128)(2,1)S(1)}, bf16[16,96,512]{2,1,0:T(8,128)(2,1)S(1)}) custom-call(bf16[16,512]{1,0:T(8,128)(2,1)S(1)} %get-tuple-element.37.g_own, bf16[16,512]{1,0:T(8,128)(2,1)S(1)} %get-tuple-element.38.g_oth, f32[16,512]{1,0:T(8,128)S(1)} %get-tuple-element.36.terms, ...), custom_call_target="tpu_custom_call" | custom-call | flops 1073741824 | bytes 5324800 | tf_op jit(solution)/shard_map/pallas_call | solution.py:55
  75.6 24.6 %all_to_all.31.got = bf16[16,96,512]{2,1,0:T(8,128)(2,1)S(1)} all-to-all(bf16[16,96,512]{2,1,0:T(8,128)(2,1)S(1)} %get-tuple-element.15), channel_id=1, replica_groups=mesh['far'=2,'near'=4,'c'=2,'y'=4,'x'=4,'h'=2] {'y','x'}, dimensions={0} | all-to-all | bytes 3145728 | tf_op jit(solution)/shard_map/all_to_all | solution.py:200
  100.2 0.2 shard_map.103
  100.5 0.0 copy-start.1
  100.5 0.7 shard_map.104
  101.2 0.0 copy-done.1
  101.3 3.7 %collective-permute-start.2 = (bf16[512,1024]{1,0:T(8,128)(2,1)S(1)}, bf16[512,1024]{1,0:T(8,128)(2,1)S(1)}, u32[]{:S(2)}, u32[]{:S(2)}) collective-permute-start(bf16[512,1024]{1,0:T(8,128)(2,1)S(1)} %shard_map.104), channel_id=1, source_target_pairs={{0,32},{32,0},{1,33},{33,1},{2,34},{34,2},{3,35},{35,3},{4,36},{36... | collective-permute-start | bytes 3145736 | tf_op jit(solution)/shard_map/ppermute | solution.py:295
  105.0 7.3 %all_to_all.32.got = bf16[4,32,512]{2,1,0:T(8,128)(2,1)S(1)} all-to-all(bf16[4,32,512]{2,1,0:T(8,128)(2,1)S(1)} %get-tuple-element.20), channel_id=1, replica_groups=mesh['far'=2,'near'=4,'c'=2,'y'=4,'x'=4,'h'=2] {'near'}, dimensions={0} | all-to-all | bytes 262144 | tf_op jit(solution)/shard_map/all_to_all | solution.py:200
  112.3 18.9 %all_to_all.33.got = bf16[4,16,512]{2,1,0:T(8,128)(2,1)S(1)} all-to-all(bf16[4,16,512]{2,1,0:T(8,128)(2,1)S(1)} %shard_map.106), channel_id=1, replica_groups=mesh['far'=2,'near'=4,'c'=2,'y'=4,'x'=4,'h'=2] {'h','far'}, dimensions={0} | all-to-all | bytes 131072 | tf_op jit(solution)/shard_map/all_to_all | solution.py:200
  131.2 0.7 shard_map.107
  131.9 6.6 %all-to-all-start.5 = ((bf16[8,16,512]{2,1,0:T(8,128)(2,1)}), bf16[8,16,512]{2,1,0:T(8,128)(2,1)S(1)}, u32[]{:S(2)}, u32[]{:S(2)}) async-start(bf16[8,16,512]{2,1,0:T(8,128)(2,1)} %shard_map.107), calls=%async_computation.5 | async-start | bytes 262144 | tf_op jit(solution)/shard_map/all_to_all | solution.py:200
  138.4 0.0 collective-permute-done.2.other
  138.4 0.0 copy-start.2
  138.4 1.0 copy-done.2
  139.5 1.7 %shard_map.105 = bf16[512,1024]{1,0:T(8,128)(2,1)} custom-call(bf16[512,512]{1,0:T(8,128)(2,1)S(1)} %copy-done.2, bf16[1024,512]{1,0:T(8,128)(2,1)S(1)} %bitcast.35, bf16[512,1024]{1,0:T(8,128)(2,1)S(1)} %collective-permute-done.2.other), custom_call_target="tpu_custom_call" | custom-call | flops 4294967296 | bytes 2621440 | tf_op jit(solution)/shard_map/pallas_call | solution.py:55
  141.2 3.1 %all-to-all-done.5.got = bf16[8,16,512]{2,1,0:T(8,128)(2,1)S(1)} async-done(((bf16[8,16,512]{2,1,0:T(8,128)(2,1)}), bf16[8,16,512]{2,1,0:T(8,128)(2,1)S(1)}, u32[]{:S(2)}, u32[]{:S(2)}) %all-to-all-start.5) | async-done | bytes 131104 | tf_op jit(solution)/shard_map/all_to_all | solution.py:200
  144.3 0.7 shard_map.108
  (5 shorter events, 0.1 us)
Async XLA Ops:
  1.4 14.7 %collective-permute-start = (bf16[32,512]{1,0:T(8,128)(2,1)S(1)}, bf16[32,512]{1,0:T(8,128)(2,1)S(1)}, u32[]{:S(2)}, u32[]{:S(2)}) collective-permute-start(bf16[32,512]{1,0:T(8,128)(2,1)S(1)} %slice_select_fusion.2), channel_id=1, source_target_pairs={{0,257},{1,256},{256,1},{257,0},{2,259},{3,258},{258,3},{259,2},{4... | collective-permute-start | bytes 98312 | tf_op jit(solution)/shard_map/ppermute | solution.py:223
  16.2 7.9 %copy-start = (bf16[1,512,1024]{2,1,0:T(8,128)(2,1)S(1)}, bf16[1,512,1024]{2,1,0:T(8,128)(2,1)}, u32[]{:S(2)}) copy-start(bf16[1,512,1024]{2,1,0:T(8,128)(2,1)} %param.6) | copy-start | bytes 3145732
  16.2 12.2 %copy-start.3 = (bf16[1024,16]{0,1:T(8,128)(2,1)S(1)}, bf16[1024,16]{0,1:T(8,128)(2,1)}, u32[]{:S(2)}) copy-start(bf16[1024,16]{0,1:T(8,128)(2,1)} %param.8) | copy-start | bytes 98308
  17.3 21.8 %all-to-all-start = ((bf16[16,64,512]{2,1,0:T(8,128)(2,1)}), bf16[16,64,512]{2,1,0:T(8,128)(2,1)S(1)}, u32[]{:S(2)}, u32[]{:S(2)}) async-start(bf16[16,64,512]{2,1,0:T(8,128)(2,1)} %broadcast_in_dim.4), calls=%async_computation | async-start | bytes 2097152 | tf_op jit(solution)/shard_map/all_to_all | solution.py:200
  24.0 15.9 %collective-permute-start.1 = (bf16[512,1024]{1,0:T(8,128)(2,1)S(1)}, bf16[512,1024]{1,0:T(8,128)(2,1)S(1)}, u32[]{:S(2)}, u32[]{:S(2)}) collective-permute-start(bf16[512,1024]{1,0:T(8,128)(2,1)S(1)} %bitcast.36), channel_id=1, source_target_pairs={{0,32},{32,0},{1,33},{33,1},{2,34},{34,2},{3,35},{35,3},{4,36},{36... | collective-permute-start | bytes 3145736 | tf_op jit(solution)/shard_map/ppermute | solution.py:229
  39.9 6.4 %copy-start.6 = (f32[16]{0:T(128)S(1)}, f32[16]{0:T(128)}, u32[]{:S(2)}) copy-start(f32[16]{0:T(128)} %param.9) | copy-start | bytes 196
  46.3 26.6 %copy-start.4 = (f32[16,512]{1,0:T(8,128)S(1)}, f32[16,512]{1,0:T(8,128)}, u32[]{:S(2)}) copy-start(f32[16,512]{1,0:T(8,128)} %param.10) | copy-start | bytes 98308
  46.3 26.6 %copy-start.5 = (f32[512]{0:T(512)S(1)}, f32[512]{0:T(512)}, u32[]{:S(2)}) copy-start(f32[512]{0:T(512)} %param.11) | copy-start | bytes 6148
  100.5 0.8 copy-start.1
  101.3 37.2 %collective-permute-start.2 = (bf16[512,1024]{1,0:T(8,128)(2,1)S(1)}, bf16[512,1024]{1,0:T(8,128)(2,1)S(1)}, u32[]{:S(2)}, u32[]{:S(2)}) collective-permute-start(bf16[512,1024]{1,0:T(8,128)(2,1)S(1)} %shard_map.104), channel_id=1, source_target_pairs={{0,32},{32,0},{1,33},{33,1},{2,34},{34,2},{3,35},{35,3},{4,36},{36... | collective-permute-start | bytes 3145736 | tf_op jit(solution)/shard_map/ppermute | solution.py:295
  131.9 12.4 %all-to-all-start.5 = ((bf16[8,16,512]{2,1,0:T(8,128)(2,1)}), bf16[8,16,512]{2,1,0:T(8,128)(2,1)S(1)}, u32[]{:S(2)}, u32[]{:S(2)}) async-start(bf16[8,16,512]{2,1,0:T(8,128)(2,1)} %shard_map.107), calls=%async_computation.5 | async-start | bytes 262144 | tf_op jit(solution)/shard_map/all_to_all | solution.py:200
  138.4 1.0 copy-start.2

commit v7 on v6

--- a/solution.py
+++ b/solution.py
@@ -87,13 +87,6 @@
         for k in range(0, pre.shape[0], 128):
             hidden = dot(g[:, k : k + 128], out[...], 0, 0)
             gp[k : k + 128] = (hidden * gelu_slope(pre[k : k + 128])).astype(bf16)
-    step = 4
-    for k in range(0, peers, step):
-        columns = slice(k * rows, (k + step) * rows)
-        mix = dot(lat_own[:, columns], gp_own[...], 0, 0)
-        mix = mix + dot(lat_oth[:, columns], gp_oth[...], 0, 0)
-        sent[k : k + step, :rows] = mix.astype(bf16).reshape(step, rows, half)
-
     head = dot(g_own[...], hid_own[...], 1, 0) + dot(g_oth[...], hid_oth[...], 1, 0)
     sums = jnp.sum(g_own[...].astype(f32), axis=1, keepdims=True)
     lane = lax.broadcasted_iota(jnp.int32, (fields, LANES), 1)
@@ -102,11 +95,16 @@
     loss = jnp.sum(jnp.sum(terms[...], axis=1, keepdims=True), axis=0, keepdims=True)
     values = jnp.where(lane[:1] == fields, loss, values)
     tail = jnp.where(
-        lax.broadcasted_iota(jnp.int32, (16, half), 0) == 0, split_row(values, half), 0.0
-    )
-    for k in range(peers):
-        sent[k, rows : rows + fields] = head.astype(bf16)
-        sent[k, rows + fields :] = tail.astype(bf16)
+        lax.broadcasted_iota(jnp.int32, (8, half), 0) == 0, split_row(values, half), 0.0
+    )
+    step = 4
+    for k in range(0, peers, step):
+        columns = slice(k * rows, (k + step) * rows)
+        mix = dot(lat_own[:, columns], gp_own[...], 0, 0)
+        mix = mix + dot(lat_oth[:, columns], gp_oth[...], 0, 0)
+        for j in range(step):
+            block = [mix[j * rows : (j + 1) * rows], head, tail]
+            sent[k + j] = jnp.concatenate(block, 0).astype(bf16)
 
 
 def partial_kernel(gp, weight, rows):
@@ -127,7 +125,7 @@
 
 
 def neighbour_kernel(got, unused_a, unused_b, sent, unused_c, unused_d, block):
-    rows, fields = got.shape[1] - 32, 16
+    rows, fields = got.shape[1] - 24, 16
     piece, hpiece = rows // H // NEAR, fields // NEAR
     whole = total(got)
     values = joined_row(whole[rows + fields : rows + fields + 1])
@@ -254,7 +252,7 @@
         [
             like((points, half), bf16),
             like((points, half), bf16),
-            like((Y * X, H * rows + 32, half), bf16),
+            like((Y * X, H * rows + 24, half), bf16),
         ],
         [g_own, g_oth, terms, out_own, pre_own, pre_oth, hid_own, hid_oth, lat_own, lat_oth],
         flops=4 * points * half * width,

time: 146 us -> 145 us (level)
  blocking collectives: 81.9 us -> 85.6 us
  starting transfers between devices: 34.6 us -> 31.1 us
  waiting for transfers between devices: 15.1 us -> 12.1 us
  local copies, waits for them, and re-layouts: 2.2 us -> 3.75 us
    all_to_all x4, blocking collectives: 71.7 us -> 75.4 us  [all_to_all(): return lax.all_to_all(x, axes, 0, 0, tiled=True)]
    all_to_all x2, starting transfers between devices: 13.3 us -> 10.1 us  [all_to_all(): return lax.all_to_all(x, axes, 0, 0, tiled=True)]
    all_to_all x2, waiting for transfers between devices: 13.7 us -> 10.6 us  [all_to_all(): return lax.all_to_all(x, axes, 0, 0, tiled=True)]
    unnamed x14 -> x18, local copies, waits for them, and re-layouts: 1.11 us -> 2.66 us
  transfers between devices with their start and end apart: 5 -> 5, of which waited for: 3 -> 2; matrix products, arithmetic and copies ran while one was open for 1% -> 1% of each run, Pallas kernels for 2% -> 2%
where the time goes in v7:
time: 145 us
  blocking collectives  85.6 us (59%)
  starting transfers between devices  31.1 us (21%)
  waiting for transfers between devices  12.1 us (8%)
  Pallas kernels  8.03 us (6%)
  local copies, waits for them, and re-layouts  3.75 us (3%)
  matrix products  1.81 us (1%)
    all_to_all x4, blocking collectives, all_to_all(): return lax.all_to_all(x, axes, 0, 0, tiled=True)  75.4 us
    ppermute x1, starting transfers between devices, body(): far = lax.ppermute(mine, ('far', 'h'), ACROSS)  13.3 us
    all_to_all x2, waiting for transfers between devices, all_to_all(): return lax.all_to_all(x, axes, 0, 0, tiled=True)  10.6 us
    all_to_all x2, starting transfers between devices, all_to_all(): return lax.all_to_all(x, axes, 0, 0, tiled=True)  10.1 us
    pallas_call x8, Pallas kernels, call(): pl.pallas_call(kernel, out_shape=shapes, in_specs=in_specs, out_specs=out...  8.03 us
    all_gather x1, blocking collectives, body(): both = lax.all_gather(members, 'c', axis=0)  5.15 us
    all_gather x1, blocking collectives, body(): both = lax.all_gather(part, 'c', axis=0)  5.05 us
    ppermute x1, starting transfers between devices, body(): lat_oth = lax.ppermute(lat_own, 'c', SWAP)  4.33 us
  transfers between devices with their start and end apart: 5, of which 2 were waited for; matrix products, arithmetic and copies ran while one was open for 1% of the time, Pallas kernels for 2%

profile of v7, /device:TPU:1, one launch (start us, length us, event | category | flops | bytes accessed | tf_op | source)
XLA Modules:
  0.0 144.6 jit_solution(13762785526256371576)
XLA Ops:
  0.6 0.8 slice_select_fusion.2
  1.4 13.3 %collective-permute-start = (bf16[32,512]{1,0:T(8,128)(2,1)S(1)}, bf16[32,512]{1,0:T(8,128)(2,1)S(1)}, u32[]{:S(2)}, u32[]{:S(2)}) collective-permute-start(bf16[32,512]{1,0:T(8,128)(2,1)S(1)} %slice_select_fusion.2), channel_id=1, source_target_pairs={{0,257},{1,256},{256,1},{257,0},{2,259},{3,258},{258,3},{259,2},{4... | collective-permute-start | bytes 98312 | tf_op jit(solution)/shard_map/ppermute | solution.py:221
  14.7 1.4 collective-permute-done
  16.2 0.0 copy-start
  16.2 0.0 copy-start.5
  16.2 1.1 broadcast_in_dim.4
  17.3 6.8 %all-to-all-start = ((bf16[16,64,512]{2,1,0:T(8,128)(2,1)}), bf16[16,64,512]{2,1,0:T(8,128)(2,1)S(1)}, u32[]{:S(2)}, u32[]{:S(2)}) async-start(bf16[16,64,512]{2,1,0:T(8,128)(2,1)} %broadcast_in_dim.4), calls=%async_computation | async-start | bytes 2097152 | tf_op jit(solution)/shard_map/all_to_all | solution.py:198
  24.0 0.0 copy-done
  24.0 4.3 %collective-permute-start.1 = (bf16[512,1024]{1,0:T(8,128)(2,1)S(1)}, bf16[512,1024]{1,0:T(8,128)(2,1)S(1)}, u32[]{:S(2)}, u32[]{:S(2)}) collective-permute-start(bf16[512,1024]{1,0:T(8,128)(2,1)S(1)} %bitcast.36), channel_id=1, source_target_pairs={{0,32},{32,0},{1,33},{33,1},{2,34},{34,2},{3,35},{35,3},{4,36},{36... | collective-permute-start | bytes 3145736 | tf_op jit(solution)/shard_map/ppermute | solution.py:227
  28.4 0.0 copy-done.5
  28.4 10.6 %all-to-all-done = bf16[16,64,512]{2,1,0:T(8,128)(2,1)S(1)} async-done(((bf16[16,64,512]{2,1,0:T(8,128)(2,1)}), bf16[16,64,512]{2,1,0:T(8,128)(2,1)S(1)}, u32[]{:S(2)}, u32[]{:S(2)}) %all-to-all-start) | async-done | bytes 1048608 | tf_op jit(solution)/shard_map/all_to_all | solution.py:198
  39.0 0.9 fusion.7
  39.9 0.0 collective-permute-done.1.lat_oth
  39.9 0.9 fusion.15
  40.9 0.0 copy-start.8
  40.9 0.4 shard_map.101
  41.2 5.1 %all-gather = f32[64,512]{1,0:T(8,128)S(1)} all-gather(f32[32,512]{1,0:T(8,128)S(1)} %shard_map.101), channel_id=2, replica_groups=mesh['far'=2,'near'=4,'c'=2,'y'=4,'x'=4,'h'=2] {'c'}, dimensions={0}, use_global_device_ids=true | all-gather | bytes 196608 | tf_op jit(solution)/shard_map/all_gather | solution.py:240
  46.3 0.0 copy-done.8
  46.3 0.0 copy-start.6
  46.3 0.0 copy-start.7
  46.3 0.1 fusion.24
  46.4 20.9 %all_to_all.30 = f32[8,16,512]{2,1,0:T(8,128)S(1)} all-to-all(f32[8,16,512]{2,1,0:T(8,128)S(1)} %sub.48), channel_id=1, replica_groups=mesh['far'=2,'near'=4,'c'=2,'y'=4,'x'=4,'h'=2] {'far','near'}, dimensions={0} | all-to-all | bytes 524288 | tf_op jit(solution)/shard_map/all_to_all | solution.py:198
  67.4 5.2 %all-gather.1 = f32[16,16,512]{2,1,0:T(8,128)S(1)} all-gather(f32[8,16,512]{2,1,0:T(8,128)S(1)} %all_to_all.30), channel_id=3, replica_groups=mesh['far'=2,'near'=4,'c'=2,'y'=4,'x'=4,'h'=2] {'c'}, dimensions={0}, use_global_device_ids=true | all-gather | bytes 786432 | tf_op jit(solution)/shard_map/all_gather | solution.py:245
  72.5 0.4 fusion.18
  72.9 0.0 copy-done.6
  72.9 0.0 copy-done.7
  72.9 0.1 subtract_multiply_fusion
  73.0 2.6 %shard_map.102 = (bf16[512,512]{1,0:T(8,128)(2,1)S(1)}, bf16[512,512]{1,0:T(8,128)(2,1)S(1)}, bf16[16,88,512]{2,1,0:T(8,128)(2,1)S(1)}) custom-call(bf16[16,512]{1,0:T(8,128)(2,1)S(1)} %get-tuple-element.37.g_own, bf16[16,512]{1,0:T(8,128)(2,1)S(1)} %get-tuple-element.38.g_oth, f32[16,512]{1,0:T(8,128)S(1)} %get-tuple-element.36.terms, ...), custom_call_target="tpu_custom_call" | custom-call | flops 1073741824 | bytes 5324800 | tf_op jit(solution)/shard_map/pallas_call | solution.py:55
  75.6 23.5 %all_to_all.31.got = bf16[16,88,512]{2,1,0:T(8,128)(2,1)S(1)} all-to-all(bf16[16,88,512]{2,1,0:T(8,128)(2,1)S(1)} %get-tuple-element.15), channel_id=1, replica_groups=mesh['far'=2,'near'=4,'c'=2,'y'=4,'x'=4,'h'=2] {'y','x'}, dimensions={0} | all-to-all | bytes 2883584 | tf_op jit(solution)/shard_map/all_to_all | solution.py:198
  99.1 0.9 shard_map.103
  100.0 0.0 copy-start.1
  100.0 0.8 copy-done.1
  100.8 0.0 copy-start.3
  100.8 0.8 copy-done.3
  101.5 3.3 %all-to-all-start.3 = ((bf16[4,32,512]{2,1,0:T(8,128)(2,1)}), bf16[4,32,512]{2,1,0:T(8,128)(2,1)S(1)}, u32[]{:S(2)}, u32[]{:S(2)}) async-start(bf16[4,32,512]{2,1,0:T(8,128)(2,1)} %get-tuple-element.20), calls=%async_computation.3 | async-start | bytes 262144 | tf_op jit(solution)/shard_map/all_to_all | solution.py:198
  104.9 0.0 copy-start.4
  104.9 1.0 copy-done.4
  105.9 0.0 copy-start.2
  105.9 1.7 %shard_map.104 = bf16[512,1024]{1,0:T(8,128)(2,1)} custom-call(bf16[512,512]{1,0:T(8,128)(2,1)S(1)} %copy-done.4, bf16[1024,512]{1,0:T(8,128)(2,1)S(1)} %bitcast.34), custom_call_target="tpu_custom_call" | custom-call | flops 4294967296 | bytes 1572864 | tf_op jit(solution)/shard_map/pallas_call | solution.py:55
  107.6 3.5 %collective-permute-start.2 = (bf16[512,1024]{1,0:T(8,128)(2,1)}, bf16[512,1024]{1,0:T(8,128)(2,1)S(1)}, u32[]{:S(2)}, u32[]{:S(2)}) collective-permute-start(bf16[512,1024]{1,0:T(8,128)(2,1)} %shard_map.104), channel_id=1, source_target_pairs={{0,32},{32,0},{1,33},{33,1},{2,34},{34,2},{3,35},{35,3},{4,36},{36... | collective-permute-start | bytes 3145736 | tf_op jit(solution)/shard_map/ppermute | solution.py:293
  111.1 0.0 all-to-all-done.3.got
  111.1 18.7 %all_to_all.32.got = bf16[4,16,512]{2,1,0:T(8,128)(2,1)S(1)} all-to-all(bf16[4,16,512]{2,1,0:T(8,128)(2,1)S(1)} %shard_map.106), channel_id=1, replica_groups=mesh['far'=2,'near'=4,'c'=2,'y'=4,'x'=4,'h'=2] {'h','far'}, dimensions={0} | all-to-all | bytes 131072 | tf_op jit(solution)/shard_map/all_to_all | solution.py:198
  129.9 12.3 %all_to_all.33.got = bf16[8,16,512]{2,1,0:T(8,128)(2,1)S(1)} all-to-all(bf16[8,16,512]{2,1,0:T(8,128)(2,1)S(1)} %shard_map.107), channel_id=1, replica_groups=mesh['far'=2,'near'=4,'c'=2,'y'=4,'x'=4,'h'=2] {'near','c'}, dimensions={0} | all-to-all | bytes 262144 | tf_op jit(solution)/shard_map/all_to_all | solution.py:198
  142.2 0.7 shard_map.108
  142.9 0.0 collective-permute-done.2.other
  142.9 0.0 copy-done.2
  142.9 1.7 %shard_map.105 = bf16[512,1024]{1,0:T(8,128)(2,1)} custom-call(bf16[512,512]{1,0:T(8,128)(2,1)S(1)} %copy-done.2, bf16[1024,512]{1,0:T(8,128)(2,1)S(1)} %bitcast.35, bf16[512,1024]{1,0:T(8,128)(2,1)S(1)} %collective-permute-done.2.other), custom_call_target="tpu_custom_call" | custom-call | flops 4294967296 | bytes 2621440 | tf_op jit(solution)/shard_map/pallas_call | solution.py:55
  (6 shorter events, 0.1 us)
Async XLA Ops:
  1.4 14.7 %collective-permute-start = (bf16[32,512]{1,0:T(8,128)(2,1)S(1)}, bf16[32,512]{1,0:T(8,128)(2,1)S(1)}, u32[]{:S(2)}, u32[]{:S(2)}) collective-permute-start(bf16[32,512]{1,0:T(8,128)(2,1)S(1)} %slice_select_fusion.2), channel_id=1, source_target_pairs={{0,257},{1,256},{256,1},{257,0},{2,259},{3,258},{258,3},{259,2},{4... | collective-permute-start | bytes 98312 | tf_op jit(solution)/shard_map/ppermute | solution.py:221
  16.2 7.9 %copy-start = (bf16[1,512,1024]{2,1,0:T(8,128)(2,1)S(1)}, bf16[1,512,1024]{2,1,0:T(8,128)(2,1)}, u32[]{:S(2)}) copy-start(bf16[1,512,1024]{2,1,0:T(8,128)(2,1)} %param.6) | copy-start | bytes 3145732
  16.2 12.2 %copy-start.5 = (bf16[1024,16]{0,1:T(8,128)(2,1)S(1)}, bf16[1024,16]{0,1:T(8,128)(2,1)}, u32[]{:S(2)}) copy-start(bf16[1024,16]{0,1:T(8,128)(2,1)} %param.8) | copy-start | bytes 98308
  17.3 21.8 %all-to-all-start = ((bf16[16,64,512]{2,1,0:T(8,128)(2,1)}), bf16[16,64,512]{2,1,0:T(8,128)(2,1)S(1)}, u32[]{:S(2)}, u32[]{:S(2)}) async-start(bf16[16,64,512]{2,1,0:T(8,128)(2,1)} %broadcast_in_dim.4), calls=%async_computation | async-start | bytes 2097152 | tf_op jit(solution)/shard_map/all_to_all | solution.py:198
  24.0 15.9 %collective-permute-start.1 = (bf16[512,1024]{1,0:T(8,128)(2,1)S(1)}, bf16[512,1024]{1,0:T(8,128)(2,1)S(1)}, u32[]{:S(2)}, u32[]{:S(2)}) collective-permute-start(bf16[512,1024]{1,0:T(8,128)(2,1)S(1)} %bitcast.36), channel_id=1, source_target_pairs={{0,32},{32,0},{1,33},{33,1},{2,34},{34,2},{3,35},{35,3},{4,36},{36... | collective-permute-start | bytes 3145736 | tf_op jit(solution)/shard_map/ppermute | solution.py:227
  40.9 5.5 %copy-start.8 = (f32[16]{0:T(128)S(1)}, f32[16]{0:T(128)}, u32[]{:S(2)}) copy-start(f32[16]{0:T(128)} %param.9) | copy-start | bytes 196
  46.3 26.6 %copy-start.6 = (f32[16,512]{1,0:T(8,128)S(1)}, f32[16,512]{1,0:T(8,128)}, u32[]{:S(2)}) copy-start(f32[16,512]{1,0:T(8,128)} %param.10) | copy-start | bytes 98308
  46.3 26.6 %copy-start.7 = (f32[512]{0:T(512)S(1)}, f32[512]{0:T(512)}, u32[]{:S(2)}) copy-start(f32[512]{0:T(512)} %param.11) | copy-start | bytes 6148
  100.0 0.8 copy-start.1
  100.8 0.8 copy-start.3
  101.5 9.6 %all-to-all-start.3 = ((bf16[4,32,512]{2,1,0:T(8,128)(2,1)}), bf16[4,32,512]{2,1,0:T(8,128)(2,1)S(1)}, u32[]{:S(2)}, u32[]{:S(2)}) async-start(bf16[4,32,512]{2,1,0:T(8,128)(2,1)} %get-tuple-element.20), calls=%async_computation.3 | async-start | bytes 262144 | tf_op jit(solution)/shard_map/all_to_all | solution.py:198
  104.9 1.0 copy-start.4
  105.9 36.9 %copy-start.2 = (bf16[512,512]{1,0:T(8,128)(2,1)S(1)}, bf16[512,512]{1,0:T(8,128)(2,1)}, u32[]{:S(2)}) copy-start(bf16[512,512]{1,0:T(8,128)(2,1)} %copy-done.1) | copy-start | bytes 1572868
  107.6 35.2 %collective-permute-start.2 = (bf16[512,1024]{1,0:T(8,128)(2,1)}, bf16[512,1024]{1,0:T(8,128)(2,1)S(1)}, u32[]{:S(2)}, u32[]{:S(2)}) collective-permute-start(bf16[512,1024]{1,0:T(8,128)(2,1)} %shard_map.104), channel_id=1, source_target_pairs={{0,32},{32,0},{1,33},{33,1},{2,34},{34,2},{3,35},{35,3},{4,36},{36... | collective-permute-start | bytes 3145736 | tf_op jit(solution)/shard_map/ppermute | solution.py:293

commit v8 on v7

--- a/solution.py
+++ b/solution.py
@@ -158,7 +158,7 @@
         sent[k] = packed
 
 
-def assemble_kernel(count, got, mix, head, bias, loss):
+def assemble_kernel(count, got, unused_in, mix, head, bias, loss, unused_out):
     half = got.shape[2]
     piece, hpiece = mix.shape[0] // NEAR, head.shape[0] // NEAR
     for n in range(NEAR):
@@ -277,22 +277,23 @@
     kernel = functools.partial(gather_kernel, piece, hpiece)
     sent = call(kernel, like((NEAR * CORES, 16, half), bf16), [got], [block])
     got = all_to_all(sent, ("near", "c"))
-    grad_mix, grad_out, grad_bias, loss = call(
+    rows_like, work = like((points, width), bf16), 16 * points * half * width
+    grad_rows = call(partial_kernel, rows_like, [gp_oth, w_own], flops=work)
+    grad_rows = lax.ppermute(grad_rows, "c", SWAP)
+    grad_latents = call(latents_kernel, rows_like, [gp_own, w_own, grad_rows], flops=work)
+    grad_mix, grad_out, grad_bias, loss, grad_latents = call(
         functools.partial(assemble_kernel, points * Y * X * H),
         [
             like((rows, width), f32),
             like((fields, width), f32),
             like((1, fields), f32),
             like((1, 1), f32),
+            rows_like,
         ],
-        [got],
-    )
-
-    rows_like, work = like((points, width), bf16), 16 * points * half * width
-    grad_rows = call(partial_kernel, rows_like, [gp_oth, w_own], flops=work)
-    grad_rows = lax.ppermute(grad_rows, "c", SWAP)
-    grad_latents = call(latents_kernel, rows_like, [gp_own, w_own, grad_rows], flops=work)[None]
-    return grad_latents, grad_mix, grad_out.T, grad_bias[0], loss[0, 0]
+        [got, grad_latents],
+        through=1,
+    )
+    return grad_latents[None], grad_mix, grad_out.T, grad_bias[0], loss[0, 0]
 
 
 def solution(mesh):

time: 145 us -> 144 us (level)
  blocking collectives: 85.6 us -> 80.8 us
  starting transfers between devices: 31.1 us -> 34.4 us
  waiting for transfers between devices: 12.1 us -> 15.1 us
  local copies, waits for them, and re-layouts: 3.75 us -> 2.2 us
    all_to_all x4, blocking collectives: 75.4 us -> 70.6 us  [all_to_all(): return lax.all_to_all(x, axes, 0, 0, tiled=True)]
    all_to_all x2, starting transfers between devices: 10.1 us -> 13.3 us  [all_to_all(): return lax.all_to_all(x, axes, 0, 0, tiled=True)]
    all_to_all x2, waiting for transfers between devices: 10.6 us -> 13.7 us  [all_to_all(): return lax.all_to_all(x, axes, 0, 0, tiled=True)]
    unnamed x18 -> x14, local copies, waits for them, and re-layouts: 2.66 us -> 1.11 us
  transfers between devices with their start and end apart: 5 -> 5, of which waited for: 2 -> 3; matrix products, arithmetic and copies ran while one was open for 1% -> 1% of each run, Pallas kernels for 2% -> 2%
where the time goes in v8:
time: 144 us
  blocking collectives  80.8 us (56%)
  starting transfers between devices  34.4 us (24%)
  waiting for transfers between devices  15.1 us (10%)
  Pallas kernels  7.07 us (5%)
  local copies, waits for them, and re-layouts  2.2 us (2%)
  matrix products  1.81 us (1%)
    all_to_all x4, blocking collectives, all_to_all(): return lax.all_to_all(x, axes, 0, 0, tiled=True)  70.6 us
    all_to_all x2, waiting for transfers between devices, all_to_all(): return lax.all_to_all(x, axes, 0, 0, tiled=True)  13.7 us
    all_to_all x2, starting transfers between devices, all_to_all(): return lax.all_to_all(x, axes, 0, 0, tiled=True)  13.3 us
    ppermute x1, starting transfers between devices, body(): far = lax.ppermute(mine, ('far', 'h'), ACROSS)  13.3 us
    pallas_call x8, Pallas kernels, call(): pl.pallas_call(kernel, out_shape=shapes, in_specs=in_specs, out_specs=out...  7.07 us
    all_gather x1, blocking collectives, body(): both = lax.all_gather(members, 'c', axis=0)  5.15 us
    all_gather x1, blocking collectives, body(): both = lax.all_gather(part, 'c', axis=0)  5.05 us
    ppermute x1, starting transfers between devices, body(): lat_oth = lax.ppermute(lat_own, 'c', SWAP)  4.33 us
  transfers between devices with their start and end apart: 5, of which 3 were waited for; matrix products, arithmetic and copies ran while one was open for 1% of the time, Pallas kernels for 2%

profile of v8, /device:TPU:1, one launch (start us, length us, event | category | flops | bytes accessed | tf_op | source)
XLA Modules:
  0.0 143.5 jit_solution(14872956110389898429)
XLA Ops:
  0.6 0.8 slice_select_fusion.2
  1.4 13.3 %collective-permute-start = (bf16[32,512]{1,0:T(8,128)(2,1)S(1)}, bf16[32,512]{1,0:T(8,128)(2,1)S(1)}, u32[]{:S(2)}, u32[]{:S(2)}) collective-permute-start(bf16[32,512]{1,0:T(8,128)(2,1)S(1)} %slice_select_fusion.2), channel_id=1, source_target_pairs={{0,257},{1,256},{256,1},{257,0},{2,259},{3,258},{258,3},{259,2},{4... | collective-permute-start | bytes 98312 | tf_op jit(solution)/shard_map/ppermute | solution.py:221
  14.7 1.4 collective-permute-done
  16.2 0.0 copy-start
  16.2 0.0 copy-start.3
  16.2 1.1 broadcast_in_dim.4
  17.3 6.8 %all-to-all-start = ((bf16[16,64,512]{2,1,0:T(8,128)(2,1)}), bf16[16,64,512]{2,1,0:T(8,128)(2,1)S(1)}, u32[]{:S(2)}, u32[]{:S(2)}) async-start(bf16[16,64,512]{2,1,0:T(8,128)(2,1)} %broadcast_in_dim.4), calls=%async_computation | async-start | bytes 2097152 | tf_op jit(solution)/shard_map/all_to_all | solution.py:198
  24.0 0.0 copy-done
  24.0 4.3 %collective-permute-start.1 = (bf16[512,1024]{1,0:T(8,128)(2,1)S(1)}, bf16[512,1024]{1,0:T(8,128)(2,1)S(1)}, u32[]{:S(2)}, u32[]{:S(2)}) collective-permute-start(bf16[512,1024]{1,0:T(8,128)(2,1)S(1)} %bitcast.36), channel_id=1, source_target_pairs={{0,32},{32,0},{1,33},{33,1},{2,34},{34,2},{3,35},{35,3},{4,36},{36... | collective-permute-start | bytes 3145736 | tf_op jit(solution)/shard_map/ppermute | solution.py:227
  28.4 0.0 copy-done.3
  28.4 10.6 %all-to-all-done = bf16[16,64,512]{2,1,0:T(8,128)(2,1)S(1)} async-done(((bf16[16,64,512]{2,1,0:T(8,128)(2,1)}), bf16[16,64,512]{2,1,0:T(8,128)(2,1)S(1)}, u32[]{:S(2)}, u32[]{:S(2)}) %all-to-all-start) | async-done | bytes 1048608 | tf_op jit(solution)/shard_map/all_to_all | solution.py:198
  39.0 0.9 fusion.7
  39.9 0.0 collective-permute-done.1.lat_oth
  39.9 0.9 fusion.15
  40.9 0.0 copy-start.6
  40.9 0.4 shard_map.101
  41.2 5.1 %all-gather = f32[64,512]{1,0:T(8,128)S(1)} all-gather(f32[32,512]{1,0:T(8,128)S(1)} %shard_map.101), channel_id=2, replica_groups=mesh['far'=2,'near'=4,'c'=2,'y'=4,'x'=4,'h'=2] {'c'}, dimensions={0}, use_global_device_ids=true | all-gather | bytes 196608 | tf_op jit(solution)/shard_map/all_gather | solution.py:240
  46.3 0.0 copy-done.6
  46.3 0.0 copy-start.4
  46.3 0.0 copy-start.5
  46.3 0.1 fusion.24
  46.4 20.9 %all_to_all.30 = f32[8,16,512]{2,1,0:T(8,128)S(1)} all-to-all(f32[8,16,512]{2,1,0:T(8,128)S(1)} %sub.48), channel_id=1, replica_groups=mesh['far'=2,'near'=4,'c'=2,'y'=4,'x'=4,'h'=2] {'far','near'}, dimensions={0} | all-to-all | bytes 524288 | tf_op jit(solution)/shard_map/all_to_all | solution.py:198
  67.4 5.2 %all-gather.1 = f32[16,16,512]{2,1,0:T(8,128)S(1)} all-gather(f32[8,16,512]{2,1,0:T(8,128)S(1)} %all_to_all.30), channel_id=3, replica_groups=mesh['far'=2,'near'=4,'c'=2,'y'=4,'x'=4,'h'=2] {'c'}, dimensions={0}, use_global_device_ids=true | all-gather | bytes 786432 | tf_op jit(solution)/shard_map/all_gather | solution.py:245
  72.5 0.4 fusion.18
  72.9 0.0 copy-done.4
  72.9 0.0 copy-done.5
  72.9 0.1 subtract_multiply_fusion
  73.0 2.6 %shard_map.102 = (bf16[512,512]{1,0:T(8,128)(2,1)S(1)}, bf16[512,512]{1,0:T(8,128)(2,1)S(1)}, bf16[16,88,512]{2,1,0:T(8,128)(2,1)S(1)}) custom-call(bf16[16,512]{1,0:T(8,128)(2,1)S(1)} %get-tuple-element.39.g_own, bf16[16,512]{1,0:T(8,128)(2,1)S(1)} %get-tuple-element.40.g_oth, f32[16,512]{1,0:T(8,128)S(1)} %get-tuple-element.38.terms, ...), custom_call_target="tpu_custom_call" | custom-call | flops 1073741824 | bytes 5324800 | tf_op jit(solution)/shard_map/pallas_call | solution.py:55
  75.6 23.5 %all_to_all.31.got = bf16[16,88,512]{2,1,0:T(8,128)(2,1)S(1)} all-to-all(bf16[16,88,512]{2,1,0:T(8,128)(2,1)S(1)} %get-tuple-element.16), channel_id=1, replica_groups=mesh['far'=2,'near'=4,'c'=2,'y'=4,'x'=4,'h'=2] {'y','x'}, dimensions={0} | all-to-all | bytes 2883584 | tf_op jit(solution)/shard_map/all_to_all | solution.py:198
  99.1 0.2 shard_map.103
  99.3 0.0 copy-start.1
  99.3 0.7 shard_map.106
  100.1 0.0 copy-done.1
  100.1 3.4 %collective-permute-start.2 = (bf16[512,1024]{1,0:T(8,128)(2,1)S(1)}, bf16[512,1024]{1,0:T(8,128)(2,1)S(1)}, u32[]{:S(2)}, u32[]{:S(2)}) collective-permute-start(bf16[512,1024]{1,0:T(8,128)(2,1)S(1)} %shard_map.106), channel_id=1, source_target_pairs={{0,32},{32,0},{1,33},{33,1},{2,34},{34,2},{3,35},{35,3},{4,36},{36... | collective-permute-start | bytes 3145736 | tf_op jit(solution)/shard_map/ppermute | solution.py:282
  103.6 7.3 %all_to_all.32.got = bf16[4,32,512]{2,1,0:T(8,128)(2,1)S(1)} all-to-all(bf16[4,32,512]{2,1,0:T(8,128)(2,1)S(1)} %get-tuple-element.19), channel_id=1, replica_groups=mesh['far'=2,'near'=4,'c'=2,'y'=4,'x'=4,'h'=2] {'near'}, dimensions={0} | all-to-all | bytes 262144 | tf_op jit(solution)/shard_map/all_to_all | solution.py:198
  110.9 18.9 %all_to_all.33.got = bf16[4,16,512]{2,1,0:T(8,128)(2,1)S(1)} all-to-all(bf16[4,16,512]{2,1,0:T(8,128)(2,1)S(1)} %shard_map.104), channel_id=1, replica_groups=mesh['far'=2,'near'=4,'c'=2,'y'=4,'x'=4,'h'=2] {'h','far'}, dimensions={0} | all-to-all | bytes 131072 | tf_op jit(solution)/shard_map/all_to_all | solution.py:198
  129.7 0.7 shard_map.105
  130.4 6.6 %all-to-all-start.5 = ((bf16[8,16,512]{2,1,0:T(8,128)(2,1)}), bf16[8,16,512]{2,1,0:T(8,128)(2,1)S(1)}, u32[]{:S(2)}, u32[]{:S(2)}) async-start(bf16[8,16,512]{2,1,0:T(8,128)(2,1)} %shard_map.105), calls=%async_computation.5 | async-start | bytes 262144 | tf_op jit(solution)/shard_map/all_to_all | solution.py:198
  137.0 0.0 collective-permute-done.2.other
  137.0 0.0 copy-start.2
  137.0 1.0 copy-done.2
  138.0 1.7 %shard_map.107.unused_in = bf16[512,1024]{1,0:T(8,128)(2,1)} custom-call(bf16[512,512]{1,0:T(8,128)(2,1)S(1)} %copy-done.2, bf16[1024,512]{1,0:T(8,128)(2,1)S(1)} %bitcast.35, bf16[512,1024]{1,0:T(8,128)(2,1)S(1)} %collective-permute-done.2.other), custom_call_target="tpu_custom_call" | custom-call | flops 4294967296 | bytes 2621440 | tf_op jit(solution)/shard_map/pallas_call | solution.py:55
  139.8 3.1 %all-to-all-done.5.got = bf16[8,16,512]{2,1,0:T(8,128)(2,1)S(1)} async-done(((bf16[8,16,512]{2,1,0:T(8,128)(2,1)}), bf16[8,16,512]{2,1,0:T(8,128)(2,1)S(1)}, u32[]{:S(2)}, u32[]{:S(2)}) %all-to-all-start.5) | async-done | bytes 131104 | tf_op jit(solution)/shard_map/all_to_all | solution.py:198
  142.8 0.7 shard_map.108
  (5 shorter events, 0.1 us)
Async XLA Ops:
  1.4 14.7 %collective-permute-start = (bf16[32,512]{1,0:T(8,128)(2,1)S(1)}, bf16[32,512]{1,0:T(8,128)(2,1)S(1)}, u32[]{:S(2)}, u32[]{:S(2)}) collective-permute-start(bf16[32,512]{1,0:T(8,128)(2,1)S(1)} %slice_select_fusion.2), channel_id=1, source_target_pairs={{0,257},{1,256},{256,1},{257,0},{2,259},{3,258},{258,3},{259,2},{4... | collective-permute-start | bytes 98312 | tf_op jit(solution)/shard_map/ppermute | solution.py:221
  16.2 7.9 %copy-start = (bf16[1,512,1024]{2,1,0:T(8,128)(2,1)S(1)}, bf16[1,512,1024]{2,1,0:T(8,128)(2,1)}, u32[]{:S(2)}) copy-start(bf16[1,512,1024]{2,1,0:T(8,128)(2,1)} %param.6) | copy-start | bytes 3145732
  16.2 12.2 %copy-start.3 = (bf16[1024,16]{0,1:T(8,128)(2,1)S(1)}, bf16[1024,16]{0,1:T(8,128)(2,1)}, u32[]{:S(2)}) copy-start(bf16[1024,16]{0,1:T(8,128)(2,1)} %param.8) | copy-start | bytes 98308
  17.3 21.8 %all-to-all-start = ((bf16[16,64,512]{2,1,0:T(8,128)(2,1)}), bf16[16,64,512]{2,1,0:T(8,128)(2,1)S(1)}, u32[]{:S(2)}, u32[]{:S(2)}) async-start(bf16[16,64,512]{2,1,0:T(8,128)(2,1)} %broadcast_in_dim.4), calls=%async_computation | async-start | bytes 2097152 | tf_op jit(solution)/shard_map/all_to_all | solution.py:198
  24.0 15.9 %collective-permute-start.1 = (bf16[512,1024]{1,0:T(8,128)(2,1)S(1)}, bf16[512,1024]{1,0:T(8,128)(2,1)S(1)}, u32[]{:S(2)}, u32[]{:S(2)}) collective-permute-start(bf16[512,1024]{1,0:T(8,128)(2,1)S(1)} %bitcast.36), channel_id=1, source_target_pairs={{0,32},{32,0},{1,33},{33,1},{2,34},{34,2},{3,35},{35,3},{4,36},{36... | collective-permute-start | bytes 3145736 | tf_op jit(solution)/shard_map/ppermute | solution.py:227
  40.9 5.5 %copy-start.6 = (f32[16]{0:T(128)S(1)}, f32[16]{0:T(128)}, u32[]{:S(2)}) copy-start(f32[16]{0:T(128)} %param.9) | copy-start | bytes 196
  46.3 26.6 %copy-start.4 = (f32[16,512]{1,0:T(8,128)S(1)}, f32[16,512]{1,0:T(8,128)}, u32[]{:S(2)}) copy-start(f32[16,512]{1,0:T(8,128)} %param.10) | copy-start | bytes 98308
  46.3 26.6 %copy-start.5 = (f32[512]{0:T(512)S(1)}, f32[512]{0:T(512)}, u32[]{:S(2)}) copy-start(f32[512]{0:T(512)} %param.11) | copy-start | bytes 6148
  99.3 0.8 copy-start.1
  100.1 36.9 %collective-permute-start.2 = (bf16[512,1024]{1,0:T(8,128)(2,1)S(1)}, bf16[512,1024]{1,0:T(8,128)(2,1)S(1)}, u32[]{:S(2)}, u32[]{:S(2)}) collective-permute-start(bf16[512,1024]{1,0:T(8,128)(2,1)S(1)} %shard_map.106), channel_id=1, source_target_pairs={{0,32},{32,0},{1,33},{33,1},{2,34},{34,2},{3,35},{35,3},{4,36},{36... | collective-permute-start | bytes 3145736 | tf_op jit(solution)/shard_map/ppermute | solution.py:282
  130.4 12.4 %all-to-all-start.5 = ((bf16[8,16,512]{2,1,0:T(8,128)(2,1)}), bf16[8,16,512]{2,1,0:T(8,128)(2,1)S(1)}, u32[]{:S(2)}, u32[]{:S(2)}) async-start(bf16[8,16,512]{2,1,0:T(8,128)(2,1)} %shard_map.105), calls=%async_computation.5 | async-start | bytes 262144 | tf_op jit(solution)/shard_map/all_to_all | solution.py:198
  137.0 1.0 copy-start.2

commit v9 on v8

--- a/solution.py
+++ b/solution.py
@@ -71,6 +71,11 @@
     return 0.5 * (1.0 + t) + (0.5 * scale) * x * (1.0 - t * t) * (1.0 + 0.134145 * square)
 
 
+def repeat_kernel(block, sent):
+    for k in range(sent.shape[0]):
+        sent[k] = block[...]
+
+
 def forecast_kernel(out, hid_own, hid_oth, part):
     fields = out.shape[0]
     part[:fields] = dot(out[...], hid_own[...], 1, 1)
@@ -220,7 +225,8 @@
     mine = pick(w_mix[:, :half], w_mix[:, half:])
     far = lax.ppermute(mine, ("far", "h"), ACROSS)
     near = jnp.where(low, jnp.concatenate([mine, far], 0), jnp.concatenate([far, mine], 0))
-    w_own = all_to_all(copies(near, Y * X), PLANE).reshape(width, half)
+    sent = jax.ShapeDtypeStruct((Y * X, H * rows, half), bf16)
+    w_own = all_to_all(call(repeat_kernel, sent, [near]), PLANE).reshape(width, half)
     out_own = pick(w_out.T[:, :half], w_out.T[:, half:])
 
     lat_own = latents[0]

time: 144 us -> 144 us (level)
    pallas_call x8 -> x9, Pallas kernels: 7.07 us -> 8.1 us  [call(): pl.pallas_call(kernel, out_shape=shapes, in_specs=in_specs, out_specs=out...]
where the time goes in v9:
time: 144 us; the launch traced here: 143 us
  blocking collectives  80.8 us (56%)
  starting transfers between devices  34.3 us (24%)
  waiting for transfers between devices  15.1 us (10%)
  Pallas kernels  8.1 us (6%)
  matrix products  1.8 us (1%)
    all_to_all x4, blocking collectives, all_to_all(): return lax.all_to_all(x, axes, 0, 0, tiled=True)  70.6 us
    all_to_all x2, waiting for transfers between devices, all_to_all(): return lax.all_to_all(x, axes, 0, 0, tiled=True)  13.7 us
    all_to_all x2, starting transfers between devices, all_to_all(): return lax.all_to_all(x, axes, 0, 0, tiled=True)  13.3 us
    ppermute x1, starting transfers between devices, body(): far = lax.ppermute(mine, ('far', 'h'), ACROSS)  13.3 us
    pallas_call x9, Pallas kernels, call(): pl.pallas_call(kernel, out_shape=shapes, in_specs=in_specs, out_specs=out...  8.1 us
    all_gather x1, blocking collectives, body(): both = lax.all_gather(members, 'c', axis=0)  5.15 us
    all_gather x1, blocking collectives, body(): both = lax.all_gather(part, 'c', axis=0)  5.05 us
    ppermute x1, starting transfers between devices, body(): lat_oth = lax.ppermute(lat_own, 'c', SWAP)  4.33 us
  transfers between devices with their start and end apart: 5, of which 3 were waited for; matrix products, arithmetic and copies ran while one was open for 1% of the time, Pallas kernels for 2%

profile of v9, /device:TPU:1, one launch (start us, length us, event | category | flops | bytes accessed | tf_op | source)
XLA Modules:
  0.0 143.5 jit_solution(14584157141947259867)
XLA Ops:
  0.6 0.8 slice_select_fusion.2
  1.4 13.3 %collective-permute-start = (bf16[32,512]{1,0:T(8,128)(2,1)S(1)}, bf16[32,512]{1,0:T(8,128)(2,1)S(1)}, u32[]{:S(2)}, u32[]{:S(2)}) collective-permute-start(bf16[32,512]{1,0:T(8,128)(2,1)S(1)} %slice_select_fusion.2), channel_id=1, source_target_pairs={{0,257},{1,256},{256,1},{257,0},{2,259},{3,258},{258,3},{259,2},{4... | collective-permute-start | bytes 98312 | tf_op jit(solution)/shard_map/ppermute | solution.py:226
  14.7 1.4 collective-permute-done
  16.2 0.0 copy-start
  16.2 0.0 copy-start.3
  16.2 1.0 shard_map.101
  17.2 6.8 %all-to-all-start = ((bf16[16,64,512]{2,1,0:T(8,128)(2,1)}), bf16[16,64,512]{2,1,0:T(8,128)(2,1)S(1)}, u32[]{:S(2)}, u32[]{:S(2)}) async-start(bf16[16,64,512]{2,1,0:T(8,128)(2,1)} %shard_map.101), calls=%async_computation | async-start | bytes 2097152 | tf_op jit(solution)/shard_map/all_to_all | solution.py:203
  24.0 0.0 copy-done
  24.0 4.3 %collective-permute-start.1 = (bf16[512,1024]{1,0:T(8,128)(2,1)S(1)}, bf16[512,1024]{1,0:T(8,128)(2,1)S(1)}, u32[]{:S(2)}, u32[]{:S(2)}) collective-permute-start(bf16[512,1024]{1,0:T(8,128)(2,1)S(1)} %bitcast.36), channel_id=1, source_target_pairs={{0,32},{32,0},{1,33},{33,1},{2,34},{34,2},{3,35},{35,3},{4,36},{36... | collective-permute-start | bytes 3145736 | tf_op jit(solution)/shard_map/ppermute | solution.py:233
  28.3 0.0 copy-done.3
  28.4 10.6 %all-to-all-done = bf16[16,64,512]{2,1,0:T(8,128)(2,1)S(1)} async-done(((bf16[16,64,512]{2,1,0:T(8,128)(2,1)}), bf16[16,64,512]{2,1,0:T(8,128)(2,1)S(1)}, u32[]{:S(2)}, u32[]{:S(2)}) %all-to-all-start) | async-done | bytes 1048608 | tf_op jit(solution)/shard_map/all_to_all | solution.py:203
  39.0 0.9 fusion.7
  39.9 0.0 collective-permute-done.1.lat_oth
  39.9 0.9 fusion.15
  40.8 0.0 copy-start.6
  40.8 0.4 shard_map.102
  41.2 5.1 %all-gather = f32[64,512]{1,0:T(8,128)S(1)} all-gather(f32[32,512]{1,0:T(8,128)S(1)} %shard_map.102), channel_id=2, replica_groups=mesh['far'=2,'near'=4,'c'=2,'y'=4,'x'=4,'h'=2] {'c'}, dimensions={0}, use_global_device_ids=true | all-gather | bytes 196608 | tf_op jit(solution)/shard_map/all_gather | solution.py:246
  46.3 0.0 copy-done.6
  46.3 0.0 copy-start.4
  46.3 0.0 copy-start.5
  46.3 0.1 fusion.24
  46.4 20.9 %all_to_all.30 = f32[8,16,512]{2,1,0:T(8,128)S(1)} all-to-all(f32[8,16,512]{2,1,0:T(8,128)S(1)} %sub.48), channel_id=1, replica_groups=mesh['far'=2,'near'=4,'c'=2,'y'=4,'x'=4,'h'=2] {'far','near'}, dimensions={0} | all-to-all | bytes 524288 | tf_op jit(solution)/shard_map/all_to_all | solution.py:203
  67.3 5.2 %all-gather.1 = f32[16,16,512]{2,1,0:T(8,128)S(1)} all-gather(f32[8,16,512]{2,1,0:T(8,128)S(1)} %all_to_all.30), channel_id=3, replica_groups=mesh['far'=2,'near'=4,'c'=2,'y'=4,'x'=4,'h'=2] {'c'}, dimensions={0}, use_global_device_ids=true | all-gather | bytes 786432 | tf_op jit(solution)/shard_map/all_gather | solution.py:251
  72.5 0.4 fusion.18
  72.9 0.0 copy-done.4
  72.9 0.0 copy-done.5
  72.9 0.1 subtract_multiply_fusion
  72.9 2.6 %shard_map.103 = (bf16[512,512]{1,0:T(8,128)(2,1)S(1)}, bf16[512,512]{1,0:T(8,128)(2,1)S(1)}, bf16[16,88,512]{2,1,0:T(8,128)(2,1)S(1)}) custom-call(bf16[16,512]{1,0:T(8,128)(2,1)S(1)} %get-tuple-element.39.g_own, bf16[16,512]{1,0:T(8,128)(2,1)S(1)} %get-tuple-element.40.g_oth, f32[16,512]{1,0:T(8,128)S(1)} %get-tuple-element.38.terms, ...), custom_call_target="tpu_custom_call" | custom-call | flops 1073741824 | bytes 5324800 | tf_op jit(solution)/shard_map/pallas_call | solution.py:55
  75.5 23.5 %all_to_all.31.got = bf16[16,88,512]{2,1,0:T(8,128)(2,1)S(1)} all-to-all(bf16[16,88,512]{2,1,0:T(8,128)(2,1)S(1)} %get-tuple-element.16), channel_id=1, replica_groups=mesh['far'=2,'near'=4,'c'=2,'y'=4,'x'=4,'h'=2] {'y','x'}, dimensions={0} | all-to-all | bytes 2883584 | tf_op jit(solution)/shard_map/all_to_all | solution.py:203
  99.1 0.2 shard_map.104
  99.3 0.0 copy-start.1
  99.3 0.7 shard_map.107
  100.1 0.0 copy-done.1
  100.1 3.4 %collective-permute-start.2 = (bf16[512,1024]{1,0:T(8,128)(2,1)S(1)}, bf16[512,1024]{1,0:T(8,128)(2,1)S(1)}, u32[]{:S(2)}, u32[]{:S(2)}) collective-permute-start(bf16[512,1024]{1,0:T(8,128)(2,1)S(1)} %shard_map.107), channel_id=1, source_target_pairs={{0,32},{32,0},{1,33},{33,1},{2,34},{34,2},{3,35},{35,3},{4,36},{36... | collective-permute-start | bytes 3145736 | tf_op jit(solution)/shard_map/ppermute | solution.py:288
  103.5 7.3 %all_to_all.32.got = bf16[4,32,512]{2,1,0:T(8,128)(2,1)S(1)} all-to-all(bf16[4,32,512]{2,1,0:T(8,128)(2,1)S(1)} %get-tuple-element.19), channel_id=1, replica_groups=mesh['far'=2,'near'=4,'c'=2,'y'=4,'x'=4,'h'=2] {'near'}, dimensions={0} | all-to-all | bytes 262144 | tf_op jit(solution)/shard_map/all_to_all | solution.py:203
  110.9 18.8 %all_to_all.33.got = bf16[4,16,512]{2,1,0:T(8,128)(2,1)S(1)} all-to-all(bf16[4,16,512]{2,1,0:T(8,128)(2,1)S(1)} %shard_map.105), channel_id=1, replica_groups=mesh['far'=2,'near'=4,'c'=2,'y'=4,'x'=4,'h'=2] {'h','far'}, dimensions={0} | all-to-all | bytes 131072 | tf_op jit(solution)/shard_map/all_to_all | solution.py:203
  129.7 0.7 shard_map.106
  130.4 6.6 %all-to-all-start.5 = ((bf16[8,16,512]{2,1,0:T(8,128)(2,1)}), bf16[8,16,512]{2,1,0:T(8,128)(2,1)S(1)}, u32[]{:S(2)}, u32[]{:S(2)}) async-start(bf16[8,16,512]{2,1,0:T(8,128)(2,1)} %shard_map.106), calls=%async_computation.5 | async-start | bytes 262144 | tf_op jit(solution)/shard_map/all_to_all | solution.py:203
  136.9 0.0 collective-permute-done.2.other
  136.9 0.0 copy-start.2
  137.0 1.0 copy-done.2
  138.0 1.7 %shard_map.108.unused_in = bf16[512,1024]{1,0:T(8,128)(2,1)} custom-call(bf16[512,512]{1,0:T(8,128)(2,1)S(1)} %copy-done.2, bf16[1024,512]{1,0:T(8,128)(2,1)S(1)} %bitcast.35, bf16[512,1024]{1,0:T(8,128)(2,1)S(1)} %collective-permute-done.2.other), custom_call_target="tpu_custom_call" | custom-call | flops 4294967296 | bytes 2621440 | tf_op jit(solution)/shard_map/pallas_call | solution.py:55
  139.7 3.1 %all-to-all-done.5.got = bf16[8,16,512]{2,1,0:T(8,128)(2,1)S(1)} async-done(((bf16[8,16,512]{2,1,0:T(8,128)(2,1)}), bf16[8,16,512]{2,1,0:T(8,128)(2,1)S(1)}, u32[]{:S(2)}, u32[]{:S(2)}) %all-to-all-start.5) | async-done | bytes 131104 | tf_op jit(solution)/shard_map/all_to_all | solution.py:203
  142.8 0.7 shard_map.109
  (5 shorter events, 0.1 us)
Async XLA Ops:
  1.4 14.7 %collective-permute-start = (bf16[32,512]{1,0:T(8,128)(2,1)S(1)}, bf16[32,512]{1,0:T(8,128)(2,1)S(1)}, u32[]{:S(2)}, u32[]{:S(2)}) collective-permute-start(bf16[32,512]{1,0:T(8,128)(2,1)S(1)} %slice_select_fusion.2), channel_id=1, source_target_pairs={{0,257},{1,256},{256,1},{257,0},{2,259},{3,258},{258,3},{259,2},{4... | collective-permute-start | bytes 98312 | tf_op jit(solution)/shard_map/ppermute | solution.py:226
  16.2 7.8 %copy-start = (bf16[1,512,1024]{2,1,0:T(8,128)(2,1)S(1)}, bf16[1,512,1024]{2,1,0:T(8,128)(2,1)}, u32[]{:S(2)}) copy-start(bf16[1,512,1024]{2,1,0:T(8,128)(2,1)} %param.6) | copy-start | bytes 3145732
  16.2 12.2 %copy-start.3 = (bf16[1024,16]{0,1:T(8,128)(2,1)S(1)}, bf16[1024,16]{0,1:T(8,128)(2,1)}, u32[]{:S(2)}) copy-start(bf16[1024,16]{0,1:T(8,128)(2,1)} %param.8) | copy-start | bytes 98308
  17.2 21.8 %all-to-all-start = ((bf16[16,64,512]{2,1,0:T(8,128)(2,1)}), bf16[16,64,512]{2,1,0:T(8,128)(2,1)S(1)}, u32[]{:S(2)}, u32[]{:S(2)}) async-start(bf16[16,64,512]{2,1,0:T(8,128)(2,1)} %shard_map.101), calls=%async_computation | async-start | bytes 2097152 | tf_op jit(solution)/shard_map/all_to_all | solution.py:203
  24.0 15.9 %collective-permute-start.1 = (bf16[512,1024]{1,0:T(8,128)(2,1)S(1)}, bf16[512,1024]{1,0:T(8,128)(2,1)S(1)}, u32[]{:S(2)}, u32[]{:S(2)}) collective-permute-start(bf16[512,1024]{1,0:T(8,128)(2,1)S(1)} %bitcast.36), channel_id=1, source_target_pairs={{0,32},{32,0},{1,33},{33,1},{2,34},{34,2},{3,35},{35,3},{4,36},{36... | collective-permute-start | bytes 3145736 | tf_op jit(solution)/shard_map/ppermute | solution.py:233
  40.8 5.5 %copy-start.6 = (f32[16]{0:T(128)S(1)}, f32[16]{0:T(128)}, u32[]{:S(2)}) copy-start(f32[16]{0:T(128)} %param.9) | copy-start | bytes 196
  46.3 26.6 %copy-start.4 = (f32[16,512]{1,0:T(8,128)S(1)}, f32[16,512]{1,0:T(8,128)}, u32[]{:S(2)}) copy-start(f32[16,512]{1,0:T(8,128)} %param.10) | copy-start | bytes 98308
  46.3 26.6 %copy-start.5 = (f32[512]{0:T(512)S(1)}, f32[512]{0:T(512)}, u32[]{:S(2)}) copy-start(f32[512]{0:T(512)} %param.11) | copy-start | bytes 6148
  99.3 0.8 copy-start.1
  100.1 36.8 %collective-permute-start.2 = (bf16[512,1024]{1,0:T(8,128)(2,1)S(1)}, bf16[512,1024]{1,0:T(8,128)(2,1)S(1)}, u32[]{:S(2)}, u32[]{:S(2)}) collective-permute-start(bf16[512,1024]{1,0:T(8,128)(2,1)S(1)} %shard_map.107), channel_id=1, source_target_pairs={{0,32},{32,0},{1,33},{33,1},{2,34},{34,2},{3,35},{35,3},{4,36},{36... | collective-permute-start | bytes 3145736 | tf_op jit(solution)/shard_map/ppermute | solution.py:288
  130.4 12.4 %all-to-all-start.5 = ((bf16[8,16,512]{2,1,0:T(8,128)(2,1)}), bf16[8,16,512]{2,1,0:T(8,128)(2,1)S(1)}, u32[]{:S(2)}, u32[]{:S(2)}) async-start(bf16[8,16,512]{2,1,0:T(8,128)(2,1)} %shard_map.106), calls=%async_computation.5 | async-start | bytes 262144 | tf_op jit(solution)/shard_map/all_to_all | solution.py:203
  136.9 1.0 copy-start.2
